TPU v7x, 512 devices: a whole 4x4x16 slice. The times are simulated.
512 devices in a mesh: fsdp: 64 (over x, z), basis: 8 (over y, core).
Axes of the slice: x: 4, y: 4, z: 16, core: 2. Of those that a mesh axis runs over, the one named last changes fastest.
Arguments:
- gradient: bfloat16 [8, 576, 18432], P('basis', 'fsdp'), may hold values from -6000 to 6000
- first_moment: bfloat16 [8, 576, 18432], P('basis', 'fsdp'), may hold values from -0.29882812 to 0.29882812
- second_moment: bfloat16 [8, 576, 18432], P('basis', None, 'fsdp'), may hold values from 0.0099487305 to 0.5
- statistic: float32 [8, 576, 576], P('basis', 'fsdp'), may hold values from -1 to 3, as said below
- eigenbasis: float32 [8, 576, 576], P('basis', 'fsdp'), may hold values from -1 to 2, as said below
Outputs:
- update: bfloat16 [8, 576, 18432], P('basis', 'fsdp')
- new_first: bfloat16 [8, 576, 18432], P('basis', 'fsdp')
- new_second: bfloat16 [8, 576, 18432], P('basis', None, 'fsdp')
- new_stat: float32 [8, 576, 576], P('basis', 'fsdp')
- new_basis: float32 [8, 576, 576], P('basis', 'fsdp')
Inputs may be any that keep to these rules, and one draw needn't show every extreme that they name: `statistic`: symmetric in each block, positive definite. `eigenbasis`: each block invertible.
All inputs are finite; a program needn't handle non-finite values.
Results may differ from a plain program's by a relative error of at most 0.00055.
The roundings to bfloat16 on the way count: a program that leaves them out, or rounds other values in their place, can miss the bound.
Values may be sent and summed in bfloat16 or wider, within the bound.
No kernel may reach another device: no remote copies, remote signals or barrier semaphores. Data moves between devices by JAX's collectives and lax.ppermute only.
A program may use at most 128 MiB of HBM per device.

v0:
```python
import jax
import jax.numpy as jnp
from jax import lax
from jax.sharding import PartitionSpec as P

FF = 18432


beta_first = 0.9
beta_second = 0.95
clip_rms = 0.5
tiny_eps = 1e-08


def lead_dot(left, right, precision_mode):
    return lax.dot_general(
        left,
        right,
        (((0,), (0,)), ((), ())),
        preferred_element_type=jnp.float32,
        precision=precision_mode,
    )


def local(gradient, first_moment, second_moment, statistic, eigenbasis):
    entries = gradient.shape[1] * gradient.shape[2] * lax.axis_size("fsdp") * lax.axis_size("basis")
    local_squares = jnp.sum(jnp.square(gradient.astype(jnp.float32)))
    total_squares = lax.psum(local_squares, ("fsdp", "basis"))
    clip_factor = jnp.minimum(1.0, clip_rms / jnp.sqrt(total_squares / entries + 1e-06))
    new_first = (
        beta_first * first_moment.astype(jnp.float32)
        + (1.0 - beta_first) * clip_factor * gradient.astype(jnp.float32)
    ).astype(jnp.bfloat16)
    grad_cols, moment_cols = (
        lax.all_to_all(gradient, "fsdp", split_axis=2, concat_axis=1, tiled=True),
        lax.all_to_all(first_moment, "fsdp", split_axis=2, concat_axis=1, tiled=True),
    )
    full_basis = lax.all_gather(eigenbasis, "fsdp", axis=1, tiled=True)[0]
    rounded_basis = full_basis.astype(jnp.bfloat16)
    block_cols = grad_cols[0]
    grad_rot = lead_dot(rounded_basis, block_cols, None)
    moment_rot = lead_dot(rounded_basis, moment_cols[0], None)
    scaled_rot = clip_factor * grad_rot
    rotated_first = beta_first * moment_rot + (1.0 - beta_first) * scaled_rot
    second_full = (
        beta_second * second_moment[0].astype(jnp.float32)
        + (1.0 - beta_second) * scaled_rot * scaled_rot
    )
    direction = (rotated_first / (jnp.sqrt(second_full) + tiny_eps)).astype(jnp.bfloat16)
    update_cols = jnp.dot(rounded_basis, direction, preferred_element_type=jnp.float32).astype(
        jnp.bfloat16
    )
    update = lax.all_to_all(update_cols[None], "fsdp", split_axis=1, concat_axis=2, tiled=True)
    stat_share = lax.psum_scatter(
        lax.dot_general(
            block_cols, block_cols, (((1,), (1,)), ((), ())), preferred_element_type=jnp.float32
        )
        / FF,
        "fsdp",
        scatter_dimension=0,
        tiled=True,
    )
    new_stat = (
        beta_second * statistic[0] + (1.0 - beta_second) * clip_factor * clip_factor * stat_share
    )
    refreshed = jnp.dot(new_stat, full_basis, precision=lax.Precision.HIGHEST)
    gram_matrix = lax.psum(lead_dot(refreshed, refreshed, lax.Precision.HIGHEST), "fsdp")
    factor = jnp.linalg.cholesky(gram_matrix)
    new_basis = lax.linalg.triangular_solve(
        factor, refreshed, left_side=False, lower=True, transpose_a=True
    )
    return (
        update,
        new_first,
        second_full.astype(jnp.bfloat16)[None],
        new_stat[None],
        new_basis[None],
    )


def solution(mesh):
    return jax.shard_map(
        local,
        mesh=mesh,
        in_specs=(
            P("basis", "fsdp", None),
            P("basis", "fsdp", None),
            P("basis", None, "fsdp"),
            P("basis", "fsdp", None),
            P("basis", "fsdp", None),
        ),
        out_specs=(
            P("basis", "fsdp", None),
            P("basis", "fsdp", None),
            P("basis", None, "fsdp"),
            P("basis", "fsdp", None),
            P("basis", "fsdp", None),
        ),
        check_vma=False,
    )
```

profile of v0, /device:TPU:8, one launch (start us, length us, event | category | flops | bytes accessed | tf_op | source)
XLA Modules:
  0.0 1069.2 jit_solution(13437801848072199116)
XLA Ops:
  7.9 17.4 %copy.48 = bf16[1,9,18432]{1,0,2:T(2,128)(2,1)} copy(bf16[1,9,18432]{2,1,0:T(8,128)(2,1)} %param.5) | data formatting | bytes 663552 | tf_op args[0]
  25.8 101.9 %reduce.33 = bf16[18432,9]{1,0:T(8,128)(2,1)} reduce(bf16[18432,1,9]{2,1,0:T(2,128)(2,1)} %bitcast.119, bf16[]{:T(256)} %broadcast.253), dimensions={1}, to_apply=%bitcast.86.reduce_sub_computation | reduce | bytes 663554
  127.7 7.6 reshape.88
  135.3 18.8 %all-to-all-start.1 = ((bf16[64,2,1296]{2,1,0:T(2,128)(2,1)}), bf16[64,2,1296]{2,1,0:T(2,128)(2,1)S(1)}, u32[]{:S(2)}, u32[]{:S(2)}) async-start(bf16[64,2,1296]{2,1,0:T(2,128)(2,1)} %reshape.88), calls=%async_computation.1 | async-start | bytes 720896 | tf_op jit(solution)/shard_map/all_to_all | solution.py:35
  154.1 14.5 %copy.45 = bf16[1,9,18432]{1,0,2:T(2,128)(2,1)} copy(bf16[1,9,18432]{2,1,0:T(8,128)(2,1)S(1)} %copy-done.4) | data formatting | bytes 663552 | tf_op args[1]
  168.6 101.9 %reduce.32 = bf16[18432,9]{1,0:T(8,128)(2,1)} reduce(bf16[18432,1,9]{2,1,0:T(2,128)(2,1)} %bitcast.122, bf16[]{:T(256)} %broadcast.253), dimensions={1}, to_apply=%bitcast.84.reduce_sub_computation | reduce | bytes 663554
  270.5 7.5 reshape.86
  278.1 15.2 %all-to-all-start = ((bf16[64,2,1296]{2,1,0:T(2,128)(2,1)}), bf16[64,2,1296]{2,1,0:T(2,128)(2,1)S(1)}, u32[]{:S(2)}, u32[]{:S(2)}) async-start(bf16[64,2,1296]{2,1,0:T(2,128)(2,1)} %reshape.86), calls=%async_computation | async-start | bytes 720896 | tf_op jit(solution)/shard_map/all_to_all | solution.py:36
  293.4 16.4 %reshape.89 = bf16[18432,1,9]{2,1,0:T(2,128)(2,1)} reshape(bf16[64,2,1296]{2,1,0:T(2,128)(2,1)S(1)} %all-to-all-done.1) | data formatting | bytes 663552
  309.8 17.5 %copy.49 = bf16[1,9,18432]{2,1,0:T(8,128)(2,1)S(1)} copy(bf16[1,9,18432]{1,0,2:T(2,128)(2,1)} %bitcast.120) | data formatting | bytes 663552 | tf_op jit(solution)/shard_map/all_to_all | solution.py:35
  331.3 104.6 %psum.14 = f32[]{:T(128)} all-reduce(f32[]{:T(128)} %fusion.8), channel_id=1, replica_groups=mesh['fsdp'=64,'basis'=8] {'fsdp','basis'}, use_global_device_ids=true, to_apply=%region_1.0 | all-reduce | flops 1 | bytes 8 | tf_op jit(solution)/shard_map/psum | solution.py:28
  438.5 16.4 %reshape.87 = bf16[18432,1,9]{2,1,0:T(2,128)(2,1)} reshape(bf16[64,2,1296]{2,1,0:T(2,128)(2,1)S(1)} %all-to-all-done) | data formatting | bytes 663552
  455.0 17.5 %copy.46 = bf16[1,9,18432]{2,1,0:T(8,128)(2,1)S(1)} copy(bf16[1,9,18432]{1,0,2:T(2,128)(2,1)} %bitcast.121) | data formatting | bytes 663552 | tf_op jit(solution)/shard_map/all_to_all | solution.py:36
  476.7 3.7 fusion.7
  480.4 2.5 copy.51
  482.9 3.5 reduce.34
  487.9 10.6 all-to-all-start.2
  498.5 111.1 %all-reduce.9.cloned.1.call-done = f32[576,576]{1,0:T(8,128)} async-done(((f32[576,576]{1,0:T(8,128)}), f32[576,576]{1,0:T(8,128)}) %all-reduce.9.cloned.1.call-update) | async-done | bytes 1327120
  611.8 2.5 fusion.81
  619.3 2.5 bitcast_reduce_fusion
  623.7 262.2 %all-reduce.7.cloned.1.call-done = f32[576,576]{0,1:T(8,128)} async-done(((f32[576,576]{0,1:T(8,128)}), f32[576,576]{0,1:T(8,128)}) %all-reduce.7.cloned.1.call-update) | async-done | bytes 1327120 | tf_op jit(solution)/shard_map/psum | solution.py:67
  889.2 11.7 %cholesky.134 = f32[128,128]{1,0:T(8,128)S(1)} custom-call(f32[128,128]{1,0:T(8,128)S(1)} %cholesky.346), custom_call_target="Cholesky" | custom-call | tf_op jit(solution)/shard_map/jit(cholesky)/cholesky | solution.py:68
  901.0 9.8 custom-call.38
  912.2 13.4 %cholesky.274 = f32[128,128]{1,0:T(8,128)} custom-call(f32[128,128]{1,0:T(8,128)} %cholesky.350), custom_call_target="Cholesky" | custom-call | tf_op jit(solution)/shard_map/jit(cholesky)/cholesky | solution.py:68
  927.0 11.3 %custom-call.39 = f32[1,128,128]{1,2,0:T(8,128)} custom-call(f32[1,128,128]{2,1,0:T(8,128)} %get-tuple-element.55), custom_call_target="InvertDiagBlocksLowerTriangular" | custom-call | tf_op jit(solution)/shard_map/jit(cholesky)/cholesky | solution.py:68
  940.5 12.5 %cholesky.295 = f32[128,128]{1,0:T(8,128)S(1)} custom-call(f32[128,128]{1,0:T(8,128)} %cholesky.355), custom_call_target="Cholesky" | custom-call | tf_op jit(solution)/shard_map/jit(cholesky)/cholesky | solution.py:68
  954.2 10.6 custom-call.40
  965.5 11.9 %cholesky.314 = f32[128,128]{1,0:T(8,128)S(1)} custom-call(f32[128,128]{1,0:T(8,128)S(1)} %cholesky.360), custom_call_target="Cholesky" | custom-call | tf_op jit(solution)/shard_map/jit(cholesky)/cholesky | solution.py:68
  978.0 9.8 custom-call.41
  988.3 5.8 cholesky.334
  1002.0 8.5 while.1
  1010.6 49.1 %custom-call.42 = f32[5,128,128]{1,2,0:T(8,128)S(1)} custom-call(f32[5,128,128]{2,1,0:T(8,128)S(1)} %pad_maximum_fusion), custom_call_target="InvertDiagBlocksLowerTriangular" | custom-call | tf_op jit(solution)/shard_map/triangular_solve | solution.py:69
  (108 shorter events, 48.0 us)
Async XLA Ops:
  7.2 466.7 %all-gather.2.cloned.1.call-start = ((), (), s32[]{:S(2)}) async-start(), calls=%async_computation.3 | async-start | bytes 1497600 | tf_op jit(solution)/shard_map/all_gather | solution.py:38
  127.7 26.4 %copy-start.4 = (bf16[1,9,18432]{2,1,0:T(8,128)(2,1)S(1)}, bf16[1,9,18432]{2,1,0:T(8,128)(2,1)}, u32[]{:S(2)}) copy-start(bf16[1,9,18432]{2,1,0:T(8,128)(2,1)} %param.6) | copy-start | bytes 995332
  135.3 142.8 %all-to-all-start.1 = ((bf16[64,2,1296]{2,1,0:T(2,128)(2,1)}), bf16[64,2,1296]{2,1,0:T(2,128)(2,1)S(1)}, u32[]{:S(2)}, u32[]{:S(2)}) async-start(bf16[64,2,1296]{2,1,0:T(2,128)(2,1)} %reshape.88), calls=%async_computation.1 | async-start | bytes 720896 | tf_op jit(solution)/shard_map/all_to_all | solution.py:35
  278.1 160.5 %all-to-all-start = ((bf16[64,2,1296]{2,1,0:T(2,128)(2,1)}), bf16[64,2,1296]{2,1,0:T(2,128)(2,1)S(1)}, u32[]{:S(2)}, u32[]{:S(2)}) async-start(bf16[64,2,1296]{2,1,0:T(2,128)(2,1)} %reshape.86), calls=%async_computation | async-start | bytes 720896 | tf_op jit(solution)/shard_map/all_to_all | solution.py:36
  293.3 316.3 %all-reduce.9.cloned.1.call-start = ((), (), s32[]{:S(2)}) async-start(), calls=%async_computation.5 | async-start | bytes 2949120
  328.6 1.8 copy-start.1
  473.5 3.2 copy-start.7
  475.8 0.9 copy-start.5
  482.9 126.7 %copy-start.9 = (f32[1,9,576]{2,0,1:T(1,128)S(1)}, f32[1,9,576]{2,0,1:T(1,128)}, u32[]{:S(2)}) copy-start(f32[1,9,576]{2,0,1:T(1,128)} %param.8) | copy-start | bytes 62212
  487.9 130.5 %all-to-all-start.2 = ((bf16[64,2,1296]{2,1,0:T(2,128)(2,1)}), bf16[64,2,1296]{2,1,0:T(2,128)(2,1)S(1)}, u32[]{:S(2)}, u32[]{:S(2)}) async-start(bf16[64,2,1296]{2,1,0:T(2,128)(2,1)} %reshape.90), calls=%async_computation.2 | async-start | bytes 720896 | tf_op jit(solution)/shard_map/all_to_all | solution.py:53
  498.5 387.4 %all-reduce.7.cloned.1.call-start = ((), (), s32[]{:S(2)}) async-start(), calls=%async_computation.4 | async-start | bytes 2949120 | tf_op jit(solution)/shard_map/psum | solution.py:67
  614.3 1.7 copy-start.6
  614.3 1.7 copy-start.8
  885.9 2.0 copy-start
  888.0 1.1 copy-start.2
  889.2 21.7 %copy-start.3 = (f32[576,576]{1,0:T(8,128)S(1)}, f32[576,576]{1,0:T(8,128)}, u32[]{:S(2)}) copy-start(f32[576,576]{1,0:T(8,128)} %copy-done.2) | copy-start | bytes 3981316
  1001.3 0.7 copy-start.10
Sparse Core Ops, SparseCore 0:
  11.0 144.7 all-gather.1
  330.5 279.0 all-reduce.8
  614.5 271.3 all-reduce.6
where the time goes:
time: 1080 us; the launch traced here: 1070 us
  waiting for transfers between devices  374 us (35%)
  other arithmetic  365 us (34%)
  local copies, waits for them, and re-layouts  144 us (13%)
  blocking collectives  105 us (10%)
  starting transfers between devices  44.7 us (4%)
  between operations  19.2 us (2%)
  matrix products  17.2 us (2%)
    psum x1, waiting for transfers between devices, local(): lax.psum(lead_dot(refreshed, refreshed, lax.Precision.HIGHEST), 'fsdp')  262 us
    unnamed x4, other arithmetic  207 us
    unnamed x4, waiting for transfers between devices  112 us
    psum x1, blocking collectives, local(): total_squares = lax.psum(local_squares, ('fsdp', 'basis'))  105 us
    another operation x18, other arithmetic, local(): factor = jnp.linalg.cholesky(gram_matrix)  104 us
    unnamed x34, local copies, waits for them, and re-layouts  88 us
    another operation x7, other arithmetic, local(): lax.linalg.triangular_solve(factor, refreshed, left_side=False, lower=Tru...  50 us
  transfers between devices with their start and end apart: 6, of which 2 were waited for; matrix products, arithmetic and copies ran while one was open for 33% of the time, Pallas kernels for 0%

commit v1 on v0

v1 whole, which is shorter than its diff:
```python
import functools

import jax
import jax.numpy as jnp
from jax import lax
from jax.experimental import pallas as pl
from jax.experimental.pallas import tpu as pltpu
from jax.sharding import Mesh, PartitionSpec as P

FF = 18432
BK = 576
NX, NZ, NB = 4, 16, 8
ROWS = 9
XROWS = ROWS * NZ
COLS = FF // (NX * NZ)
REST = COLS - 256
XSTEP = COLS * NZ
PIECES = NX * COLS
TILES = PIECES // 128
PACK = 96
WIDE = 640
BTILES = WIDE // 128
BPACK = 48
ENTRIES = NB * BK * FF
HIGH = lax.Precision.HIGHEST

beta_first = 0.9
beta_second = 0.95
clip_rms = 0.5
tiny_eps = 1e-08

F32 = jnp.float32
BF16 = jnp.bfloat16


def vmem(n):
    return [pl.BlockSpec(memory_space=pltpu.VMEM)] * n


def call(body, out_shape, n_in, scratch=(), flops=0, nbytes=1 << 20):
    outs = out_shape if isinstance(out_shape, (tuple, list)) else (out_shape,)
    return pl.pallas_call(
        body,
        out_shape=tuple(outs),
        in_specs=vmem(n_in),
        out_specs=tuple(vmem(len(outs))),
        scratch_shapes=list(scratch),
        compiler_params=pltpu.CompilerParams(vmem_limit_bytes=48 << 20),
        cost_estimate=pl.CostEstimate(
            flops=flops, bytes_accessed=nbytes, transcendentals=0
        ),
    )


def struct(shape, dtype):
    return jax.ShapeDtypeStruct(shape, dtype)


def pack_natural(src, buf, out_ref):
    lane = lax.broadcasted_iota(jnp.int32, (16, 128), 1)
    for z in range(NZ):
        rest = jnp.zeros((16, 128), F32)
        for xp in range(NX):
            start = XSTEP * xp + COLS * z
            base = start // 128 * 128
            off = start - base
            w = src[:, base : base + 384]
            if off:
                w = pltpu.roll(w, 384 - off, 1)
            for t in range(2):
                at = ROWS * (2 * xp + t)
                buf[at : at + ROWS, :] = w[:ROWS, 128 * t : 128 * t + 128]
            r = w[:, 256:384]
            if xp:
                r = pltpu.roll(r, REST * xp, 1)
            rest = jnp.where((lane >= REST * xp) & (lane < REST * (xp + 1)), r, rest)
        buf[8 * ROWS : 9 * ROWS, :] = rest[:ROWS]
        out_ref[z] = buf[...].astype(BF16)


def pack_gradient_body(g_ref, out_ref, sum_ref, src, buf):
    g = g_ref[0].astype(F32)
    src[:ROWS, :] = g
    buf[9 * ROWS :, :] = jnp.zeros((PACK - 9 * ROWS, 128), F32)
    pack_natural(src, buf, out_ref)
    total = jnp.sum(g * g)
    sum_ref[...] = jnp.full(sum_ref.shape, total, F32)


def pack_moment_body(m_ref, out_ref, src, buf):
    src[:ROWS, :] = m_ref[0].astype(F32)
    buf[9 * ROWS :, :] = jnp.zeros((PACK - 9 * ROWS, 128), F32)
    pack_natural(src, buf, out_ref)


def pack_basis_body(b_ref, sums_ref, out_ref, buf):
    buf[...] = jnp.zeros(buf.shape, F32)
    for t in range(4):
        buf[ROWS * t : ROWS * (t + 1), :] = b_ref[0, :, 128 * t : 128 * t + 128]
    buf[4 * ROWS : 5 * ROWS, 0:64] = b_ref[0, :, 512:576]
    total = jnp.sum(sums_ref[:, 0:1, :], axis=0)
    buf[45:46, :] = total
    for z in range(NZ):
        out_ref[z] = buf[...]


def unpack_rows(in_ref, buf, full):
    for z in range(NZ):
        buf[...] = in_ref[z].astype(F32)
        for t in range(TILES):
            full[ROWS * z : ROWS * (z + 1), 128 * t : 128 * t + 128] = buf[
                ROWS * t : ROWS * (t + 1), :
            ]


def unpack_gradient_body(in_ref, out_ref, buf, full):
    unpack_rows(in_ref, buf, full)
    g = full[...].astype(BF16)
    for xp in range(NX):
        out_ref[xp] = g


def unpack_moment_body(in_ref, out_ref, buf, full):
    unpack_rows(in_ref, buf, full)
    lane = lax.broadcasted_iota(jnp.int32, (XROWS, 128), 1)
    for xp in range(NX):
        out_ref[xp, :, 0:256] = full[:, 256 * xp : 256 * xp + 256].astype(BF16)
        r = full[:, 1024:1152]
        if xp:
            r = pltpu.roll(r, 128 - REST * xp, 1)
        out_ref[xp, :, 256:384] = jnp.where(lane < REST, r, 0.0).astype(BF16)


def covariance_body(own_ref, all_ref, out_ref, prod):
    own = own_ref[0]
    every = all_ref[...].reshape(BK, PIECES)
    prod[:, :BK] = lax.dot_general(
        own, every, (((1,), (1,)), ((), ())), preferred_element_type=F32
    )
    prod[:, BK:] = jnp.zeros((XROWS, WIDE - BK), F32)
    for z in range(NZ):
        for t in range(BTILES):
            out_ref[z, ROWS * t : ROWS * (t + 1), :] = prod[
                ROWS * z : ROWS * (z + 1), 128 * t : 128 * t + 128
            ]
        out_ref[z, 45:48, :] = jnp.zeros((3, 128), F32)


def unpack_square(in_ref, full):
    for f in range(NX * NZ):
        for t in range(BTILES):
            full[ROWS * f : ROWS * (f + 1), 128 * t : 128 * t + 128] = in_ref[
                f, ROWS * t : ROWS * (t + 1), :
            ]


def unpack_basis_body(in_ref, full_ref, round_ref, clip_ref):
    unpack_square(in_ref, full_ref)
    round_ref[...] = full_ref[:, :BK].astype(BF16)
    total = jnp.sum(in_ref[:, 45, :], axis=0, keepdims=True)[:, 0:1] / ENTRIES
    factor = jnp.minimum(1.0, clip_rms / jnp.sqrt(total + 1e-06))
    clip_ref[...] = jnp.broadcast_to(factor, clip_ref.shape)


def refresh_body(rs_ref, stat_ref, basis_ref, clip_ref, stat_out, own_out, pack_out, cov, buf):
    clip = clip_ref[0:1, 0:1]
    buf[...] = jnp.sum(rs_ref[...], axis=0)
    cov[...] = jnp.zeros(cov.shape, F32)
    for t in range(BTILES):
        cov[:ROWS, 128 * t : 128 * t + 128] = buf[ROWS * t : ROWS * (t + 1), :]
    share = cov[:, :BK] / FF
    new_stat = (1.0 - beta_second) * clip * clip * share
    new_stat = new_stat[:ROWS] + beta_second * stat_ref[0]
    stat_out[0] = new_stat
    cov[:ROWS, :BK] = new_stat
    refreshed = jnp.dot(
        cov[:, :BK], basis_ref[...], preferred_element_type=F32, precision=HIGH
    )
    own_out[...] = refreshed
    buf[...] = jnp.zeros(buf.shape, F32)
    cov[...] = refreshed
    for t in range(BTILES):
        buf[ROWS * t : ROWS * (t + 1), :] = cov[:ROWS, 128 * t : 128 * t + 128]
    for z in range(NZ):
        pack_out[z] = buf[...]


def rotate_body(x_ref, g_ref, m_ref, basis_ref, second_ref, clip_ref, up_ref, second_out):
    x = x_ref[0]
    clip = clip_ref[0:1, 0:1]
    basis = basis_ref[...]
    main = g_ref[:, :, pl.ds(pl.multiple_of(256 * x, 128), 256)].reshape(BK, 256)
    rest = g_ref[:, :, 1024:1152].reshape(BK, 128).astype(F32)
    rest = pltpu.roll(rest, lax.rem(128 - REST * x, 128), 1).astype(BF16)
    piece = jnp.concatenate([main, rest], axis=1)
    lead = (((0,), (0,)), ((), ()))
    grad_rot = lax.dot_general(piece, basis, lead, preferred_element_type=F32)[:COLS]
    moment = m_ref[...].reshape(BK, 384)
    moment_rot = lax.dot_general(moment, basis, lead, preferred_element_type=F32)[:COLS]
    scaled = clip * grad_rot
    first = beta_first * moment_rot + (1.0 - beta_first) * scaled
    second = beta_second * second_ref[0].astype(F32) + (1.0 - beta_second) * scaled * scaled
    second_out[0] = second.astype(BF16)
    direction = (first / (jnp.sqrt(second) + tiny_eps)).astype(BF16)
    update = lax.dot_general(
        basis, direction, (((1,), (1,)), ((), ())), preferred_element_type=F32
    )
    for xp in range(NX):
        part = update[XROWS * xp : XROWS * (xp + 1)].astype(BF16)
        up_ref[xp, :, 0:COLS] = part
        up_ref[xp, :, COLS:384] = jnp.zeros((XROWS, 384 - COLS), BF16)


def pack_update_body(in_ref, out_ref, full, buf):
    lane = lax.broadcasted_iota(jnp.int32, (XROWS, 128), 1)
    rest = jnp.zeros((XROWS, 128), F32)
    for xp in range(NX):
        full[:, 256 * xp : 256 * xp + 256] = in_ref[xp, :, 0:256].astype(F32)
        r = in_ref[xp, :, 256:384].astype(F32)
        if xp:
            r = pltpu.roll(r, REST * xp, 1)
        rest = jnp.where((lane >= REST * xp) & (lane < REST * (xp + 1)), r, rest)
    full[:, 1024:1152] = rest
    buf[9 * ROWS :, :] = jnp.zeros((PACK - 9 * ROWS, 128), F32)
    for z in range(NZ):
        for t in range(TILES):
            buf[ROWS * t : ROWS * (t + 1), :] = full[
                ROWS * z : ROWS * (z + 1), 128 * t : 128 * t + 128
            ]
        out_ref[z] = buf[...].astype(BF16)


def unpack_update_body(in_ref, out_ref, buf, row, nat):
    lane = lax.broadcasted_iota(jnp.int32, (16, 128), 1)
    for q in range(NZ // 4):
        for s in range(4):
            buf[...] = in_ref[4 * q + s].astype(F32)
            off = REST * s
            for xp in range(NX):
                for t in range(2):
                    at = ROWS * (2 * xp + t)
                    row[:ROWS, 128 * t : 128 * t + 128] = buf[at : at + ROWS, :]
                row[:ROWS, 256:384] = buf[8 * ROWS : 9 * ROWS, :]
                rest = row[:, 256:384]
                if xp:
                    rest = pltpu.roll(rest, 128 - REST * xp, 1)
                w = jnp.concatenate([row[:, 0:256], rest], axis=1)
                if off:
                    w = pltpu.roll(w, off, 1)
                at = XSTEP * xp + 1152 * q + 256 * s
                if off:
                    nat[:, at : at + 128] = jnp.where(
                        lane >= off, w[:, 0:128], nat[:, at : at + 128]
                    )
                else:
                    nat[:, at : at + 128] = w[:, 0:128]
                nat[:, at + 128 : at + 384] = w[:, 128:384]
    out_ref[0] = nat[:ROWS, :].astype(BF16)


def first_body(g_ref, m_ref, clip_ref, out_ref):
    clip = clip_ref[0:1, 0:1]
    out_ref[0] = (
        beta_first * m_ref[0].astype(F32)
        + (1.0 - beta_first) * clip * g_ref[0].astype(F32)
    ).astype(BF16)


def eliminate(d_ref, e_ref):
    sub = lax.broadcasted_iota(jnp.int32, (8, 128), 0)

    def spread(row):
        return jnp.broadcast_to(row, (8, 128))

    for g in range(16):
        at = slice(8 * g, 8 * g + 8)
        v, f = d_ref[at, :], e_ref[at, :]
        cols = [spread(v[:, 8 * g + c : 8 * g + c + 1]) for c in range(8)]
        scale, upper, lower, coef = [], [], [], {}
        for i in range(8):
            rs = lax.rsqrt(spread(cols[i][i : i + 1, :]))
            left = jnp.where(sub > i, cols[i] * rs, 0.0)
            u = spread(v[i : i + 1, :]) * rs
            e = spread(f[i : i + 1, :]) * rs
            v = v - left * u
            f = jnp.where(sub == i, e, f - left * e)
            for c in range(i + 1, 8):
                coef[i, c] = spread(left[c : c + 1, :])
                cols[c] = cols[c] - left * coef[i, c]
            scale.append(rs)
            upper.append(u)
            lower.append(e)
        e_ref[at, :] = f
        for r in range(g + 1, 16):
            to = slice(8 * r, 8 * r + 8)
            w, h = d_ref[to, :], e_ref[to, :]
            cols = [spread(w[:, 8 * g + c : 8 * g + c + 1]) for c in range(8)]
            for i in range(8):
                k = cols[i] * scale[i]
                w = w - k * upper[i]
                h = h - k * lower[i]
                for c in range(i + 1, 8):
                    cols[c] = cols[c] - k * coef[i, c]
            d_ref[to, :] = w
            e_ref[to, :] = h


def factor_body(in_ref, own_ref, out_ref, full, mat, result, diag, inv):
    unpack_square(in_ref, full)
    rows = full[...]
    gram = lax.dot_general(
        rows, rows, (((0,), (0,)), ((), ())), preferred_element_type=F32, precision=HIGH
    )
    r = lax.broadcasted_iota(jnp.int32, (WIDE, WIDE), 0)
    c = lax.broadcasted_iota(jnp.int32, (WIDE, WIDE), 1)
    mat[:WIDE, :] = jnp.where((r == c) & (r >= BK), 1.0, gram)
    mat[WIDE:, :] = own_ref[...]
    eye = (
        lax.broadcasted_iota(jnp.int32, (128, 128), 0)
        == lax.broadcasted_iota(jnp.int32, (128, 128), 1)
    ).astype(F32)
    across = (((1,), (1,)), ((), ()))

    def panel(p, carry):
        here = pl.ds(pl.multiple_of(128 * p, 128), 128)
        diag[...] = mat[here, here]
        inv[...] = eye
        eliminate(diag, inv)
        part = lax.dot_general(
            mat[:, here], inv[...], across, preferred_element_type=F32, precision=HIGH
        )
        result[:, here] = part[WIDE:]
        mat[...] -= lax.dot_general(
            part, part[:WIDE], across, preferred_element_type=F32, precision=HIGH
        )
        return carry

    lax.fori_loop(0, BTILES, panel, 0)
    out_ref[0] = result[:ROWS, :BK]


def local(gradient, first_moment, second_moment, statistic, eigenbasis):
    def a2a(v, axes):
        return lax.all_to_all(v, axes, 0, 0, tiled=True)

    g_packed, sums = call(
        pack_gradient_body,
        [struct((NZ, PACK, 128), BF16), struct((NB, 8, 128), F32)],
        1,
        [pltpu.VMEM((16, FF), F32), pltpu.VMEM((PACK, 128), F32)],
    )(gradient)
    g_mid = a2a(g_packed, "z")
    sums = a2a(sums, ("y", "c"))
    (b_packed,) = call(
        pack_basis_body,
        struct((NZ, BPACK, 128), F32),
        2,
        [pltpu.VMEM((BPACK, 128), F32)],
    )(eigenbasis, sums)
    b_mid = a2a(b_packed, "z")
    b_all = a2a(jnp.broadcast_to(b_mid.reshape(1, NZ * BPACK, 128), (NX, NZ * BPACK, 128)), "x")
    (m_packed,) = call(
        pack_moment_body,
        struct((NZ, PACK, 128), BF16),
        1,
        [pltpu.VMEM((16, FF), F32), pltpu.VMEM((PACK, 128), F32)],
    )(first_moment)
    m_mid = a2a(m_packed, "z")

    (g_own,) = call(
        unpack_gradient_body,
        struct((NX, XROWS, PIECES), BF16),
        1,
        [pltpu.VMEM((PACK, 128), F32), pltpu.VMEM((XROWS, PIECES), F32)],
    )(g_mid)
    g_all = a2a(g_own, "x")
    (share,) = call(
        covariance_body,
        struct((NZ, BPACK, 128), F32),
        2,
        [pltpu.VMEM((XROWS, WIDE), F32)],
        flops=2 * XROWS * BK * PIECES,
    )(g_own, g_all)
    share = a2a(share, "z")

    basis, rounded, clip = call(
        unpack_basis_body,
        [struct((BK, WIDE), F32), struct((BK, BK), BF16), struct((8, 128), F32)],
        1,
    )(b_all.reshape(NX * NZ, BPACK, 128))

    new_stat, own, r_packed = call(
        refresh_body,
        [
            struct((1, ROWS, BK), F32),
            struct((16, WIDE), F32),
            struct((NZ, BPACK, 128), F32),
        ],
        4,
        [pltpu.VMEM((16, WIDE), F32), pltpu.VMEM((BPACK, 128), F32)],
        flops=12 * 16 * BK * WIDE,
    )(share, statistic, basis, clip)
    r_mid = a2a(r_packed, "z")
    r_all = a2a(jnp.broadcast_to(r_mid.reshape(1, NZ * BPACK, 128), (NX, NZ * BPACK, 128)), "x")

    (m_own,) = call(
        unpack_moment_body,
        struct((NX, XROWS, 384), BF16),
        1,
        [pltpu.VMEM((PACK, 128), F32), pltpu.VMEM((XROWS, PIECES), F32)],
    )(m_mid)
    m_all = a2a(m_own, "x")
    x_at = lax.axis_index("x").astype(jnp.int32).reshape(1)
    rotate = pl.pallas_call(
        rotate_body,
        out_shape=(struct((NX, XROWS, 384), BF16), struct((1, COLS, BK), BF16)),
        in_specs=[pl.BlockSpec(memory_space=pltpu.SMEM)] + vmem(5),
        out_specs=tuple(vmem(2)),
        compiler_params=pltpu.CompilerParams(vmem_limit_bytes=48 << 20),
        cost_estimate=pl.CostEstimate(
            flops=6 * BK * BK * 384, bytes_accessed=4 << 20, transcendentals=0
        ),
    )
    up, new_second = rotate(x_at, g_all, m_all, rounded, jnp.swapaxes(second_moment, 1, 2), clip)
    up = a2a(up, "x")
    (up_packed,) = call(
        pack_update_body,
        struct((NZ, PACK, 128), BF16),
        1,
        [pltpu.VMEM((XROWS, PIECES), F32), pltpu.VMEM((PACK, 128), F32)],
    )(up)
    up_packed = a2a(up_packed, "z")
    (update,) = call(
        unpack_update_body,
        struct((1, ROWS, FF), BF16),
        1,
        [pltpu.VMEM((PACK, 128), F32), pltpu.VMEM((16, 384), F32), pltpu.VMEM((16, FF), F32)],
    )(up_packed)
    (new_first,) = call(first_body, struct((1, ROWS, FF), BF16), 3)(gradient, first_moment, clip)

    (new_basis,) = call(
        factor_body,
        struct((1, ROWS, BK), F32),
        2,
        [
            pltpu.VMEM((BK, WIDE), F32),
            pltpu.VMEM((WIDE + 16, WIDE), F32),
            pltpu.VMEM((16, WIDE), F32),
            pltpu.VMEM((128, 128), F32),
            pltpu.VMEM((128, 128), F32),
        ],
        flops=12 * BK * WIDE * WIDE,
    )(r_all.reshape(NX * NZ, BPACK, 128), own)
    return update, new_first, jnp.swapaxes(new_second, 1, 2), new_stat, new_basis


def solution(mesh):
    grid = Mesh(mesh.devices.reshape(NX, NZ, 4, 2), ("x", "z", "y", "c"))
    rows = P(("y", "c"), ("x", "z"), None)
    cols = P(("y", "c"), None, ("x", "z"))
    return jax.shard_map(
        local,
        mesh=grid,
        in_specs=(rows, rows, cols, rows, rows),
        out_specs=(rows, rows, cols, rows, rows),
        check_vma=False,
    )
```

time: 1080 us -> 325 us (0.30)
  the two profiles are of different devices: /device:TPU:8 before, /device:TPU:32 now
where the time goes in v1:
time: 325 us; the launch traced here: 324 us
  waiting for transfers between devices  145 us (45%)
  starting transfers between devices  63.4 us (20%)
  Pallas kernels  54.3 us (17%)
  blocking collectives  49.3 us (15%)
  local copies, waits for them, and re-layouts  11.4 us (4%)
    all_to_all x9, waiting for transfers between devices, a2a(): return lax.all_to_all(v, axes, 0, 0, tiled=True)  145 us
    all_to_all x9, starting transfers between devices, a2a(): return lax.all_to_all(v, axes, 0, 0, tiled=True)  63.4 us
    all_to_all x3, blocking collectives, a2a(): return lax.all_to_all(v, axes, 0, 0, tiled=True)  49.3 us
    pallas_call x1, Pallas kernels, local(): call(factor_body, struct((1, ROWS, BK), F32), 2, [pltpu.VMEM((BK, WIDE),...  36.5 us
    unnamed x26, local copies, waits for them, and re-layouts  8.81 us
  transfers between devices with their start and end apart: 9, of which 9 were waited for; matrix products, arithmetic and copies ran while one was open for 0% of the time, Pallas kernels for 4%

profile of v1, /device:TPU:32, one launch (start us, length us, event | category | flops | bytes accessed | tf_op | source)
XLA Modules:
  0.0 324.0 jit_solution(16344664826037554728)
XLA Ops:
  1.7 2.7 shard_map.92
  4.4 9.7 %all_to_all.60.sums_ref = f32[8,8,128]{2,1,0:T(8,128)S(1)} all-to-all(f32[8,8,128]{2,1,0:T(8,128)S(1)} %get-tuple-element.16), channel_id=1, replica_groups=mesh['x'=4,'z'=16,'y'=4,'c'=2] {'y','c'}, dimensions={0} | all-to-all | bytes 65536 | tf_op jit(solution)/shard_map/all_to_all | solution.py:344
  14.1 15.2 %all-to-all-start = ((bf16[16,96,128]{2,1,0:T(8,128)(2,1)}), bf16[16,96,128]{2,1,0:T(8,128)(2,1)S(1)}, u32[]{:S(2)}, u32[]{:S(2)}) async-start(bf16[16,96,128]{2,1,0:T(8,128)(2,1)} %get-tuple-element.15), calls=%async_computation | async-start | bytes 786432 | tf_op jit(solution)/shard_map/all_to_all | solution.py:344
  29.3 2.6 shard_map.94
  32.0 19.2 %all-to-all-done.in_ref = bf16[16,96,128]{2,1,0:T(8,128)(2,1)S(1)} async-done(((bf16[16,96,128]{2,1,0:T(8,128)(2,1)}), bf16[16,96,128]{2,1,0:T(8,128)(2,1)S(1)}, u32[]{:S(2)}, u32[]{:S(2)}) %all-to-all-start) | async-done | bytes 393248 | tf_op jit(solution)/shard_map/all_to_all | solution.py:344
  51.2 7.9 %all-to-all-start.2 = ((bf16[16,96,128]{2,1,0:T(8,128)(2,1)}), bf16[16,96,128]{2,1,0:T(8,128)(2,1)S(1)}, u32[]{:S(2)}, u32[]{:S(2)}) async-start(bf16[16,96,128]{2,1,0:T(8,128)(2,1)} %shard_map.94), calls=%async_computation.2 | async-start | bytes 786432 | tf_op jit(solution)/shard_map/all_to_all | solution.py:344
  59.9 20.8 %all-to-all-done.2.in_ref = bf16[16,96,128]{2,1,0:T(8,128)(2,1)S(1)} async-done(((bf16[16,96,128]{2,1,0:T(8,128)(2,1)}), bf16[16,96,128]{2,1,0:T(8,128)(2,1)S(1)}, u32[]{:S(2)}, u32[]{:S(2)}) %all-to-all-start.2) | async-done | bytes 393248 | tf_op jit(solution)/shard_map/all_to_all | solution.py:344
  80.6 7.9 %all-to-all-start.5 = ((f32[16,48,128]{2,1,0:T(8,128)}), f32[16,48,128]{2,1,0:T(8,128)S(1)}, u32[]{:S(2)}, u32[]{:S(2)}) async-start(f32[16,48,128]{2,1,0:T(8,128)} %shard_map.96), calls=%async_computation.5 | async-start | bytes 786432 | tf_op jit(solution)/shard_map/all_to_all | solution.py:344
  88.7 21.5 %all-to-all-done.5 = f32[16,48,128]{2,1,0:T(8,128)S(1)} async-done(((f32[16,48,128]{2,1,0:T(8,128)}), f32[16,48,128]{2,1,0:T(8,128)S(1)}, u32[]{:S(2)}, u32[]{:S(2)}) %all-to-all-start.5) | async-done | bytes 393248 | tf_op jit(solution)/shard_map/all_to_all | solution.py:344
  110.3 11.8 %all_to_all.61.m_ref = bf16[4,144,384]{2,1,0:T(8,128)(2,1)} all-to-all(bf16[4,144,384]{2,1,0:T(8,128)(2,1)S(1)} %shard_map.95), channel_id=1, replica_groups=mesh['x'=4,'z'=16,'y'=4,'c'=2] {'x'}, dimensions={0} | all-to-all | bytes 884736 | tf_op jit(solution)/shard_map/all_to_all | solution.py:344
  122.1 1.3 broadcast_in_dim.15
  123.4 3.6 %all-to-all-start.6 = ((f32[4,768,128]{2,1,0:T(8,128)}), f32[4,768,128]{2,1,0:T(8,128)S(1)}, u32[]{:S(2)}, u32[]{:S(2)}) async-start(f32[4,768,128]{2,1,0:T(8,128)} %broadcast_in_dim.15), calls=%async_computation.6 | async-start | bytes 3145728 | tf_op jit(solution)/shard_map/all_to_all | solution.py:344
  126.9 1.3 shard_map.93.own_ref
  128.3 16.7 %all-to-all-done.6 = f32[4,768,128]{2,1,0:T(8,128)S(1)} async-done(((f32[4,768,128]{2,1,0:T(8,128)}), f32[4,768,128]{2,1,0:T(8,128)S(1)}, u32[]{:S(2)}, u32[]{:S(2)}) %all-to-all-start.6) | async-done | bytes 1572896 | tf_op jit(solution)/shard_map/all_to_all | solution.py:344
  145.0 3.5 %all-to-all-start.1 = ((bf16[4,144,1152]{2,1,0:T(8,128)(2,1)}), bf16[4,144,1152]{2,1,0:T(8,128)(2,1)S(1)}, u32[]{:S(2)}, u32[]{:S(2)}) async-start(bf16[4,144,1152]{2,1,0:T(8,128)(2,1)} %shard_map.93.own_ref), calls=%async_computation.1 | async-start | bytes 2654208 | tf_op jit(solution)/shard_map/all_to_all | solution.py:344
  150.9 12.1 %all-to-all-done.1.g_ref.all_ref = bf16[4,144,1152]{2,1,0:T(8,128)(2,1)S(1)} async-done(((bf16[4,144,1152]{2,1,0:T(8,128)(2,1)}), bf16[4,144,1152]{2,1,0:T(8,128)(2,1)S(1)}, u32[]{:S(2)}, u32[]{:S(2)}) %all-to-all-start.1) | async-done | bytes 1327136 | tf_op jit(solution)/shard_map/all_to_all | solution.py:344
  166.1 2.4 shard_map.98
  168.5 3.5 %all-to-all-start.7 = ((bf16[4,144,384]{2,1,0:T(8,128)(2,1)}), bf16[4,144,384]{2,1,0:T(8,128)(2,1)S(1)}, u32[]{:S(2)}, u32[]{:S(2)}) async-start(bf16[4,144,384]{2,1,0:T(8,128)(2,1)} %get-tuple-element.19), calls=%async_computation.7 | async-start | bytes 884736 | tf_op jit(solution)/shard_map/all_to_all | solution.py:344
  172.0 2.7 shard_map.102
  174.7 4.9 %all-to-all-done.7.in_ref = bf16[4,144,384]{2,1,0:T(8,128)(2,1)S(1)} async-done(((bf16[4,144,384]{2,1,0:T(8,128)(2,1)}), bf16[4,144,384]{2,1,0:T(8,128)(2,1)S(1)}, u32[]{:S(2)}, u32[]{:S(2)}) %all-to-all-start.7) | async-done | bytes 442400 | tf_op jit(solution)/shard_map/all_to_all | solution.py:344
  179.6 11.6 %all-to-all-start.9 = ((f32[16,48,128]{2,1,0:T(8,128)}), f32[16,48,128]{2,1,0:T(8,128)S(1)}, u32[]{:S(2)}, u32[]{:S(2)}) async-start(f32[16,48,128]{2,1,0:T(8,128)} %shard_map.102), calls=%async_computation.9 | async-start | bytes 786432 | tf_op jit(solution)/shard_map/all_to_all | solution.py:344
  192.2 18.0 %all-to-all-done.9.rs_ref = f32[16,48,128]{2,1,0:T(8,128)S(1)} async-done(((f32[16,48,128]{2,1,0:T(8,128)}), f32[16,48,128]{2,1,0:T(8,128)S(1)}, u32[]{:S(2)}, u32[]{:S(2)}) %all-to-all-start.9) | async-done | bytes 393248 | tf_op jit(solution)/shard_map/all_to_all | solution.py:344
  210.2 6.3 %all-to-all-start.8 = ((bf16[16,96,128]{2,1,0:T(8,128)(2,1)}), bf16[16,96,128]{2,1,0:T(8,128)(2,1)S(1)}, u32[]{:S(2)}, u32[]{:S(2)}) async-start(bf16[16,96,128]{2,1,0:T(8,128)(2,1)} %shard_map.99), calls=%async_computation.8 | async-start | bytes 786432 | tf_op jit(solution)/shard_map/all_to_all | solution.py:344
  216.6 1.4 copy-done.5
  218.8 18.1 %all-to-all-done.8.in_ref = bf16[16,96,128]{2,1,0:T(8,128)(2,1)S(1)} async-done(((bf16[16,96,128]{2,1,0:T(8,128)(2,1)}), bf16[16,96,128]{2,1,0:T(8,128)(2,1)S(1)}, u32[]{:S(2)}, u32[]{:S(2)}) %all-to-all-start.8) | async-done | bytes 393248 | tf_op jit(solution)/shard_map/all_to_all | solution.py:344
  236.9 27.7 %all_to_all.62 = f32[16,48,128]{2,1,0:T(8,128)S(1)} all-to-all(f32[16,48,128]{2,1,0:T(8,128)S(1)} %get-tuple-element.23), channel_id=1, replica_groups=mesh['x'=4,'z'=16,'y'=4,'c'=2] {'z'}, dimensions={0} | all-to-all | bytes 786432 | tf_op jit(solution)/shard_map/all_to_all | solution.py:344
  264.7 1.3 broadcast_in_dim.17
  265.9 3.9 %all-to-all-start.11 = ((f32[4,768,128]{2,1,0:T(8,128)}), f32[4,768,128]{2,1,0:T(8,128)S(1)}, u32[]{:S(2)}, u32[]{:S(2)}) async-start(f32[4,768,128]{2,1,0:T(8,128)} %broadcast_in_dim.17), calls=%async_computation.11 | async-start | bytes 3145728 | tf_op jit(solution)/shard_map/all_to_all | solution.py:344
  269.8 1.3 shard_map.101
  271.7 1.6 shard_map.100
  273.3 13.6 %all-to-all-done.11 = f32[4,768,128]{2,1,0:T(8,128)S(1)} async-done(((f32[4,768,128]{2,1,0:T(8,128)}), f32[4,768,128]{2,1,0:T(8,128)S(1)}, u32[]{:S(2)}, u32[]{:S(2)}) %all-to-all-start.11) | async-done | bytes 1572896 | tf_op jit(solution)/shard_map/all_to_all | solution.py:344
  286.9 36.5 %shard_map.104 = f32[1,9,576]{2,1,0:T(8,128)S(1)} custom-call(f32[64,48,128]{2,1,0:T(8,128)S(1)} %bitcast.8, f32[16,640]{1,0:T(8,128)S(1)} %get-tuple-element.24.own_ref), custom_call_target="tpu_custom_call" | custom-call | flops 2831155200 | bytes 1048576 | tf_op jit(solution)/shard_map/pallas_call | solution.py:441
  (30 shorter events, 10.6 us)
Async XLA Ops:
  0.6 1.1 copy-start
  1.7 27.6 %copy-start.2 = (bf16[1,9,18432]{2,1,0:T(8,128)(2,1)S(1)}, bf16[1,9,18432]{2,1,0:T(8,128)(2,1)}, u32[]{:S(2)}) copy-start(bf16[1,9,18432]{2,1,0:T(8,128)(2,1)} %m_ref.3) | copy-start | bytes 995332
  1.7 57.4 %copy-start.9 = (f32[1,9,576]{2,0,1:T(1,128)S(1)}, f32[1,9,576]{2,0,1:T(1,128)}, u32[]{:S(2)}) copy-start(f32[1,9,576]{2,0,1:T(1,128)} %param.9) | copy-start | bytes 62212
  14.1 37.0 %all-to-all-start = ((bf16[16,96,128]{2,1,0:T(8,128)(2,1)}), bf16[16,96,128]{2,1,0:T(8,128)(2,1)S(1)}, u32[]{:S(2)}, u32[]{:S(2)}) async-start(bf16[16,96,128]{2,1,0:T(8,128)(2,1)} %get-tuple-element.15), calls=%async_computation | async-start | bytes 786432 | tf_op jit(solution)/shard_map/all_to_all | solution.py:344
  51.2 29.5 %all-to-all-start.2 = ((bf16[16,96,128]{2,1,0:T(8,128)(2,1)}), bf16[16,96,128]{2,1,0:T(8,128)(2,1)S(1)}, u32[]{:S(2)}, u32[]{:S(2)}) async-start(bf16[16,96,128]{2,1,0:T(8,128)(2,1)} %shard_map.94), calls=%async_computation.2 | async-start | bytes 786432 | tf_op jit(solution)/shard_map/all_to_all | solution.py:344
  80.6 29.6 %all-to-all-start.5 = ((f32[16,48,128]{2,1,0:T(8,128)}), f32[16,48,128]{2,1,0:T(8,128)S(1)}, u32[]{:S(2)}, u32[]{:S(2)}) async-start(f32[16,48,128]{2,1,0:T(8,128)} %shard_map.96), calls=%async_computation.5 | async-start | bytes 786432 | tf_op jit(solution)/shard_map/all_to_all | solution.py:344
  123.4 21.6 %all-to-all-start.6 = ((f32[4,768,128]{2,1,0:T(8,128)}), f32[4,768,128]{2,1,0:T(8,128)S(1)}, u32[]{:S(2)}, u32[]{:S(2)}) async-start(f32[4,768,128]{2,1,0:T(8,128)} %broadcast_in_dim.15), calls=%async_computation.6 | async-start | bytes 3145728 | tf_op jit(solution)/shard_map/all_to_all | solution.py:344
  145.0 18.0 %all-to-all-start.1 = ((bf16[4,144,1152]{2,1,0:T(8,128)(2,1)}), bf16[4,144,1152]{2,1,0:T(8,128)(2,1)S(1)}, u32[]{:S(2)}, u32[]{:S(2)}) async-start(bf16[4,144,1152]{2,1,0:T(8,128)(2,1)} %shard_map.93.own_ref), calls=%async_computation.1 | async-start | bytes 2654208 | tf_op jit(solution)/shard_map/all_to_all | solution.py:344
  148.9 1.1 copy-start.4
  150.0 0.9 copy-start.6
  163.0 1.0 copy-start.3
  164.0 1.1 copy-start.7
  165.2 1.0 copy-start.8
  168.5 11.1 %all-to-all-start.7 = ((bf16[4,144,384]{2,1,0:T(8,128)(2,1)}), bf16[4,144,384]{2,1,0:T(8,128)(2,1)S(1)}, u32[]{:S(2)}, u32[]{:S(2)}) async-start(bf16[4,144,384]{2,1,0:T(8,128)(2,1)} %get-tuple-element.19), calls=%async_computation.7 | async-start | bytes 884736 | tf_op jit(solution)/shard_map/all_to_all | solution.py:344
  174.7 41.9 %copy-start.10 = (f32[1,9,576]{2,0,1:T(1,128)S(1)}, f32[1,9,576]{2,0,1:T(1,128)}, u32[]{:S(2)}) copy-start(f32[1,9,576]{2,0,1:T(1,128)} %param.8) | copy-start | bytes 62212
  179.6 30.6 %all-to-all-start.9 = ((f32[16,48,128]{2,1,0:T(8,128)}), f32[16,48,128]{2,1,0:T(8,128)S(1)}, u32[]{:S(2)}, u32[]{:S(2)}) async-start(f32[16,48,128]{2,1,0:T(8,128)} %shard_map.102), calls=%async_computation.9 | async-start | bytes 786432 | tf_op jit(solution)/shard_map/all_to_all | solution.py:344
  210.2 26.7 %all-to-all-start.8 = ((bf16[16,96,128]{2,1,0:T(8,128)(2,1)}), bf16[16,96,128]{2,1,0:T(8,128)(2,1)S(1)}, u32[]{:S(2)}, u32[]{:S(2)}) async-start(bf16[16,96,128]{2,1,0:T(8,128)(2,1)} %shard_map.99), calls=%async_computation.8 | async-start | bytes 786432 | tf_op jit(solution)/shard_map/all_to_all | solution.py:344
  216.6 1.4 copy-start.5
  265.9 3.9 %copy-start.1 = (bf16[1,9,18432]{2,1,0:T(8,128)(2,1)S(1)}, bf16[1,9,18432]{2,1,0:T(8,128)(2,1)}, u32[]{:S(2)}) copy-start(bf16[1,9,18432]{2,1,0:T(8,128)(2,1)} %g_ref.3) | copy-start | bytes 995332
  265.9 21.0 %all-to-all-start.11 = ((f32[4,768,128]{2,1,0:T(8,128)}), f32[4,768,128]{2,1,0:T(8,128)S(1)}, u32[]{:S(2)}, u32[]{:S(2)}) async-start(f32[4,768,128]{2,1,0:T(8,128)} %broadcast_in_dim.17), calls=%async_computation.11 | async-start | bytes 3145728 | tf_op jit(solution)/shard_map/all_to_all | solution.py:344

commit v2 on v1

v2 whole, which is shorter than its diff:
```python
import functools

import jax
import jax.numpy as jnp
from jax import lax
from jax.experimental import pallas as pl
from jax.experimental.pallas import tpu as pltpu
from jax.sharding import Mesh, PartitionSpec as P

FF = 18432
BK = 576
NX, NZ, NB = 4, 16, 8
ROWS = 9
XROWS = ROWS * NZ
COLS = FF // (NX * NZ)
REST = COLS - 256
XSTEP = COLS * NZ
PIECES = NX * COLS
TILES = PIECES // 128
PACK = 88
WIDE = 640
BTILES = WIDE // 128
BPACK = 48
GROWS = XROWS + 16
APACK = 168
SUMS = XROWS
MOMENT = XROWS + 16
XPACK = MOMENT + XROWS // 3
ENTRIES = NB * BK * FF
HIGH = lax.Precision.HIGHEST

beta_first = 0.9
beta_second = 0.95
clip_rms = 0.5
tiny_eps = 1e-08

F32 = jnp.float32
BF16 = jnp.bfloat16


def vmem(n):
    return [pl.BlockSpec(memory_space=pltpu.VMEM)] * n


def call(
    body, out_shape, args, scratch=(), at=None, after=(), far=(), flops=0, nbytes=1 << 20
):
    outs = out_shape if isinstance(out_shape, (tuple, list)) else (out_shape,)
    head = [] if at is None else [at]
    n_head, n_real, n_after = len(head), len(args), len(after) + len(far)

    def run(*refs):
        body(*refs[: n_head + n_real], *refs[n_head + n_real + n_after :])

    return pl.pallas_call(
        run,
        out_shape=tuple(outs),
        in_specs=[pl.BlockSpec(memory_space=pltpu.SMEM)] * n_head
        + vmem(n_real)
        + vmem(len(after))
        + [pl.BlockSpec(memory_space=pl.ANY)] * len(far),
        out_specs=tuple(vmem(len(outs))),
        scratch_shapes=list(scratch),
        compiler_params=pltpu.CompilerParams(vmem_limit_bytes=16 << 20),
        cost_estimate=pl.CostEstimate(
            flops=flops, bytes_accessed=nbytes, transcendentals=0
        ),
    )(*head, *args, *after, *far)


def back(x, d):
    return lax.rem(x + (NX - d), NX)


def struct(shape, dtype):
    return jax.ShapeDtypeStruct(shape, dtype)


def pack_natural(src, put):
    lane = lax.broadcasted_iota(jnp.int32, (16, 128), 1)
    for z in range(NZ):
        rest = jnp.zeros((16, 128), F32)
        for xp in range(NX):
            start = XSTEP * xp + COLS * z
            base = start // 128 * 128
            off = start - base
            w = src[:, base : base + 384]
            if off:
                w = pltpu.roll(w, 384 - off, 1)
            for t in range(2):
                put(z, 2 * xp + t, w[:ROWS, 128 * t : 128 * t + 128])
            r = w[:, 256:384]
            if xp:
                r = pltpu.roll(r, REST * xp, 1)
            rest = jnp.where((lane >= REST * xp) & (lane < REST * (xp + 1)), r, rest)
        put(z, 8, rest[:ROWS])


def split(v):
    high = v.astype(BF16).astype(F32)
    mid = (v - high).astype(BF16).astype(F32)
    return high, mid, v - high - mid


def pack_body(g_ref, m_ref, out_ref, sum_ref, src, buf):
    buf[:, 18 * ROWS :, :] = jnp.zeros((NZ, APACK - 18 * ROWS, 128), F32)

    def put(first):
        def store(z, t, rows):
            at = ROWS * (first + t)
            buf[z, at : at + ROWS, :] = rows

        return store

    g = g_ref[0].astype(F32)
    sum_ref[...] = jnp.full(sum_ref.shape, jnp.sum(g * g), F32)
    src[:ROWS, :] = g
    pack_natural(src, put(0))
    src[:ROWS, :] = m_ref[0].astype(F32)
    pack_natural(src, put(9))
    for z in range(NZ):
        out_ref[z] = buf[z].astype(BF16)


def pack_basis_body(b_ref, out_ref, buf):
    buf[...] = jnp.zeros(buf.shape, F32)
    for t in range(4):
        buf[ROWS * t : ROWS * (t + 1), :] = b_ref[0, :, 128 * t : 128 * t + 128]
    buf[4 * ROWS : 5 * ROWS, 0:64] = b_ref[0, :, 512:576]
    for z in range(NZ):
        out_ref[z] = buf[...]


def unpack_body(x_ref, in_ref, s0, s1, s2, s3, o0, o1, o2, o3, buf, full_g, full_m, parts):
    x = x_ref[0]
    for z in range(NZ):
        buf[...] = in_ref[z].astype(F32)
        for t in range(TILES):
            here = (slice(ROWS * z, ROWS * (z + 1)), slice(128 * t, 128 * t + 128))
            full_g[here] = buf[ROWS * t : ROWS * (t + 1), :]
            full_m[here] = buf[ROWS * (9 + t) : ROWS * (10 + t), :]

    total = (s0[...] + s1[...]) + (s2[...] + s3[...])
    high, mid, low = split(total)
    row = lax.broadcasted_iota(jnp.int32, (8, 128), 0)
    sums = jnp.where(row == 0, high, jnp.where(row == 1, mid, jnp.where(row == 2, low, 0.0)))
    sums = jnp.concatenate([sums, jnp.zeros((8, 128), F32)], axis=0).astype(BF16)
    g = full_g[...].astype(BF16)

    lane = lax.broadcasted_iota(jnp.int32, (XROWS, 128), 1)
    for xp in range(NX):
        to = lax.rem(xp - x + NX, NX)
        parts[to, :, 0:256] = full_m[:, 256 * xp : 256 * xp + 256].astype(BF16)
        r = full_m[:, 1024:1152]
        if xp:
            r = pltpu.roll(r, 128 - REST * xp, 1)
        parts[to, :, 256:384] = jnp.where(lane < REST, r, 0.0).astype(BF16)
    for d, out in enumerate((o0, o1, o2, o3)):
        out[:XROWS] = g
        for t in range(TILES):
            out[SUMS:MOMENT, 128 * t : 128 * t + 128] = sums
        for k in range(3):
            out[MOMENT:, 384 * k : 384 * k + 384] = parts[d, 48 * k : 48 * k + 48, :]


def covariance_body(x_ref, g0, g1, g2, g3, out_ref, piece_ref, moment_ref, every, prod):
    x = x_ref[0]
    for d, g in enumerate((g0, g1, g2, g3)):
        every[back(x, d)] = g[:XROWS]
        for k in range(3):
            moment_ref[back(x, d), 48 * k : 48 * k + 48, :] = g[
                MOMENT:, 384 * k : 384 * k + 384
            ]
    sums = jnp.zeros((1, 128), F32)
    for g in (g0, g1, g2, g3):
        rows = g[SUMS:MOMENT, 0:128].astype(F32)
        sums = sums + ((rows[0:1] + rows[1:2]) + rows[2:3])
    prod[:, :BK] = lax.dot_general(
        g0[:XROWS],
        every[...].reshape(BK, PIECES),
        (((1,), (1,)), ((), ())),
        preferred_element_type=F32,
    )
    prod[:, BK:] = jnp.zeros((XROWS, WIDE - BK), F32)
    for z in range(NZ):
        for t in range(BTILES):
            out_ref[z, ROWS * t : ROWS * (t + 1), :] = prod[
                ROWS * z : ROWS * (z + 1), 128 * t : 128 * t + 128
            ]
        out_ref[z, 45:48, :] = jnp.broadcast_to(sums, (3, 128))
    main = every[:, :, pl.ds(pl.multiple_of(256 * x, 128), 256)].reshape(BK, 256)
    rest = every[:, :, 1024:1152].reshape(BK, 128).astype(F32)
    piece_ref[:, 0:256] = main
    piece_ref[:, 256:384] = pltpu.roll(rest, lax.rem(128 - REST * x, 128), 1).astype(BF16)


def unpack_square(in_ref, full):
    for f in range(in_ref.shape[0]):
        for t in range(BTILES):
            full[ROWS * f : ROWS * (f + 1), 128 * t : 128 * t + 128] = in_ref[
                f, ROWS * t : ROWS * (t + 1), :
            ]


def unpack_basis_body(x_ref, b0, b1, b2, b3, full_ref, round_ref, buf):
    x = x_ref[0]
    for d, b in enumerate((b0, b1, b2, b3)):
        buf[back(x, d)] = b[...]
    for xp in range(NX):
        unpack_square(buf.at[xp], full_ref.at[XROWS * xp : XROWS * (xp + 1)])
    round_ref[...] = full_ref[:, :BK].astype(BF16)


def refresh_body(rs_ref, stat_ref, basis_ref, stat_out, own_out, pack_out, clip_out, cov, buf):
    buf[...] = jnp.sum(rs_ref[...], axis=0)
    clip = jnp.minimum(1.0, clip_rms / jnp.sqrt(buf[45:46, 0:1] / ENTRIES + 1e-06))
    clip_out[...] = jnp.broadcast_to(clip, clip_out.shape)
    cov[...] = jnp.zeros(cov.shape, F32)
    for t in range(BTILES):
        cov[:ROWS, 128 * t : 128 * t + 128] = buf[ROWS * t : ROWS * (t + 1), :]
    share = cov[:, :BK] / FF
    new_stat = (1.0 - beta_second) * clip * clip * share
    new_stat = new_stat[:ROWS] + beta_second * stat_ref[0]
    stat_out[0] = new_stat
    cov[:ROWS, :BK] = new_stat
    refreshed = jnp.dot(
        cov[:, :BK], basis_ref[...], preferred_element_type=F32, precision=HIGH
    )
    own_out[...] = refreshed
    buf[...] = jnp.zeros(buf.shape, F32)
    cov[...] = refreshed
    for t in range(BTILES):
        buf[ROWS * t : ROWS * (t + 1), :] = cov[:ROWS, 128 * t : 128 * t + 128]
    for z in range(NZ):
        pack_out[z] = buf[...]


def rotate_body(
    x_ref, g_ref, m_ref, basis_ref, second_ref, clip_ref, o0, o1, o2, o3, second_out, update
):
    x = x_ref[0]
    clip = clip_ref[0:1, 0:1]
    basis = basis_ref[...]
    lead = (((0,), (0,)), ((), ()))
    grad_rot = lax.dot_general(g_ref[...], basis, lead, preferred_element_type=F32)[:COLS]
    moment_rot = lax.dot_general(
        m_ref[...].reshape(BK, 384), basis, lead, preferred_element_type=F32
    )[:COLS]
    scaled = clip * grad_rot
    first = beta_first * moment_rot + (1.0 - beta_first) * scaled
    second = beta_second * second_ref[0].astype(F32) + (1.0 - beta_second) * scaled * scaled
    second_out[0] = second.astype(BF16)
    direction = (first / (jnp.sqrt(second) + tiny_eps)).astype(BF16)
    product = lax.dot_general(
        basis, direction, (((1,), (1,)), ((), ())), preferred_element_type=F32
    )
    for xp in range(NX):
        to = lax.rem(xp - x + NX, NX)
        update[to, :, 0:COLS] = product[XROWS * xp : XROWS * (xp + 1)].astype(BF16)
        update[to, :, COLS:384] = jnp.zeros((XROWS, 384 - COLS), BF16)
    for d, out in enumerate((o0, o1, o2, o3)):
        out[...] = update[d]


def pack_update_body(x_ref, u0, u1, u2, u3, out_ref, parts, full, buf):
    x = x_ref[0]
    for d, u in enumerate((u0, u1, u2, u3)):
        parts[back(x, d)] = u[...]
    lane = lax.broadcasted_iota(jnp.int32, (XROWS, 128), 1)
    rest = jnp.zeros((XROWS, 128), F32)
    for xp in range(NX):
        full[:, 256 * xp : 256 * xp + 256] = parts[xp, :, 0:256].astype(F32)
        r = parts[xp, :, 256:384].astype(F32)
        if xp:
            r = pltpu.roll(r, REST * xp, 1)
        rest = jnp.where((lane >= REST * xp) & (lane < REST * (xp + 1)), r, rest)
    full[:, 1024:1152] = rest
    buf[9 * ROWS :, :] = jnp.zeros((PACK - 9 * ROWS, 128), F32)
    for z in range(NZ):
        for t in range(TILES):
            buf[ROWS * t : ROWS * (t + 1), :] = full[
                ROWS * z : ROWS * (z + 1), 128 * t : 128 * t + 128
            ]
        out_ref[z] = buf[...].astype(BF16)


def unpack_update_body(in_ref, out_ref, buf, row, nat):
    lane = lax.broadcasted_iota(jnp.int32, (16, 128), 1)
    for q in range(NZ // 4):
        for s in range(4):
            buf[...] = in_ref[4 * q + s].astype(F32)
            off = REST * s
            for xp in range(NX):
                for t in range(2):
                    at = ROWS * (2 * xp + t)
                    row[:ROWS, 128 * t : 128 * t + 128] = buf[at : at + ROWS, :]
                row[:ROWS, 256:384] = buf[8 * ROWS : 9 * ROWS, :]
                rest = row[:, 256:384]
                if xp:
                    rest = pltpu.roll(rest, 128 - REST * xp, 1)
                w = jnp.concatenate([row[:, 0:256], rest], axis=1)
                if off:
                    w = pltpu.roll(w, off, 1)
                at = XSTEP * xp + 1152 * q + 256 * s
                if off:
                    nat[:, at : at + 128] = jnp.where(
                        lane >= off, w[:, 0:128], nat[:, at : at + 128]
                    )
                else:
                    nat[:, at : at + 128] = w[:, 0:128]
                nat[:, at + 128 : at + 384] = w[:, 128:384]
    out_ref[0] = nat[:ROWS, :].astype(BF16)


def first_body(g_ref, m_ref, clip_ref, out_ref):
    clip = clip_ref[0:1, 0:1]
    out_ref[0] = (
        beta_first * m_ref[0].astype(F32)
        + (1.0 - beta_first) * clip * g_ref[0].astype(F32)
    ).astype(BF16)


def eliminate_rows(m_ref, first, last):
    sub = lax.broadcasted_iota(jnp.int32, (8, 128), 0)
    lane = lax.broadcasted_iota(jnp.int32, (8, 128), 1)

    def spread(row):
        return jnp.broadcast_to(row, (8, 128))

    for g in range(first, last):
        at = slice(8 * g, 8 * g + 8)
        here = (lane >= 8 * g) & (lane < 8 * g + 8)
        v = m_ref[at, :]
        cols = [spread(v[:, 8 * g + c : 8 * g + c + 1]) for c in range(8)]
        v = jnp.where(here, jnp.where(lane == 8 * g + sub, 1.0, 0.0), v)
        scale, pivot, coef = [], [], {}
        for i in range(8):
            rs = lax.rsqrt(spread(cols[i][i : i + 1, :]))
            left = jnp.where(sub > i, cols[i] * rs, 0.0)
            row = spread(v[i : i + 1, :]) * rs
            v = jnp.where(sub == i, row, v - left * row)
            for c in range(i + 1, 8):
                coef[i, c] = spread(left[c : c + 1, :])
                cols[c] = cols[c] - left * coef[i, c]
            scale.append(rs)
            pivot.append(row)
        m_ref[at, :] = v
        for r in range(g + 1, 16):
            to = slice(8 * r, 8 * r + 8)
            w = m_ref[to, :]
            cols = [spread(w[:, 8 * g + c : 8 * g + c + 1]) for c in range(8)]
            w = jnp.where(here, 0.0, w)
            for i in range(8):
                k = cols[i] * scale[i]
                w = w - k * pivot[i]
                for c in range(i + 1, 8):
                    cols[c] = cols[c] - k * coef[i, c]
            m_ref[to, :] = w


def copies_body(in_ref, out_ref):
    for xp in range(NX):
        out_ref[xp] = in_ref[...]


def factor_body(r_ref, own_ref, out_ref, full, mat, result, diag):
    for xp in range(NX):
        unpack_square(r_ref.at[xp], full.at[XROWS * xp : XROWS * (xp + 1)])
    rows = full[...]
    across = (((1,), (1,)), ((), ()))

    for c, w in ((0, 256), (256, 256), (512, 128)):
        mat[c:WIDE, c : c + w] = lax.dot_general(
            rows[:, c:],
            rows[:, c : c + w],
            (((0,), (0,)), ((), ())),
            preferred_element_type=F32,
            precision=HIGH,
        )
    r = lax.broadcasted_iota(jnp.int32, (128, 128), 0)
    c = lax.broadcasted_iota(jnp.int32, (128, 128), 1)
    eye, below = r == c, r >= c
    mat[512:WIDE, 512:] = jnp.where(eye & (r >= BK - 512), 1.0, mat[512:WIDE, 512:])
    mat[WIDE:, :] = own_ref[...]

    def panel(p, carry):
        here = pl.ds(pl.multiple_of(128 * p, 128), 128)
        diag[...] = mat[here, here]
        eliminate_rows(diag, 0, 8)

        @pl.when(p < BTILES - 1)
        def _():
            eliminate_rows(diag, 8, 16)

        inv = jnp.where(below, diag[...], 0.0)
        for k in range(BTILES):

            @pl.when(p == k)
            def _(k=k):
                low = 128 * (k + 1)
                part = lax.dot_general(
                    mat[low:, 128 * k : low],
                    inv,
                    across,
                    preferred_element_type=F32,
                    precision=HIGH,
                )
                result[:, 128 * k : low] = part[WIDE - low :]
                for c in range(low, WIDE, 256):
                    w = min(256, WIDE - c)
                    mat[c:, c : c + w] -= lax.dot_general(
                        part[c - low :],
                        part[c - low : c - low + w],
                        across,
                        preferred_element_type=F32,
                        precision=HIGH,
                    )

        return carry

    lax.fori_loop(0, BTILES, panel, 0)
    out_ref[0] = result[:ROWS, :BK]


def local(gradient, first_moment, second_moment, statistic, eigenbasis):
    x = lax.axis_index("x").astype(jnp.int32).reshape(1)

    def swap(v, axis):
        return lax.all_to_all(v, axis, 0, 0, tiled=True)

    def shift(v, axis, d):
        size = lax.axis_size(axis)
        return lax.ppermute(v, axis, [(k, (k + d) % size) for k in range(size)])

    def spread(v, axis="x"):
        return [v] + [shift(v, axis, d) for d in (1, 2, 3)]

    def deal(parts):
        return [parts[0]] + [shift(parts[d], "x", d) for d in (1, 2, 3)]

    natural = pltpu.VMEM((16, FF), F32)
    chunk = pltpu.VMEM((PACK, 128), F32)
    rows = pltpu.VMEM((XROWS, PIECES), F32)
    parts = pltpu.VMEM((NX, XROWS, 384), BF16)

    packed, sums = call(
        pack_body,
        [struct((NZ, APACK, 128), BF16), struct((8, 128), F32)],
        [gradient, first_moment],
        [natural, pltpu.VMEM((NZ, APACK, 128), F32)],
    )
    mid = swap(packed, "z")
    sums = spread(sums + shift(sums, "c", 1), "y")
    (b_packed,) = call(
        pack_basis_body,
        struct((NZ, BPACK, 128), F32),
        [eigenbasis],
        [pltpu.VMEM((BPACK, 128), F32)],
        after=sums[1:],
        far=[mid],
    )
    b_mid = swap(b_packed, "z")
    over_x = call(
        unpack_body,
        [struct((XPACK, PIECES), BF16)] * 4,
        [mid, *sums],
        [pltpu.VMEM((APACK, 128), F32), rows, rows, parts],
        at=x,
    )
    share, piece, moment = call(
        covariance_body,
        [
            struct((NZ, BPACK, 128), F32),
            struct((BK, 384), BF16),
            struct((NX, XROWS, 384), BF16),
        ],
        deal(over_x),
        [pltpu.VMEM((NX, XROWS, PIECES), BF16), pltpu.VMEM((XROWS, WIDE), F32)],
        at=x,
        flops=2 * XROWS * BK * PIECES,
    )
    share = swap(share, "z")
    basis, rounded = call(
        unpack_basis_body,
        [struct((BK, WIDE), F32), struct((BK, BK), BF16)],
        spread(b_mid),
        [pltpu.VMEM((NX, NZ, BPACK, 128), F32)],
        at=x,
    )

    new_stat, own, r_packed, clip = call(
        refresh_body,
        [
            struct((1, ROWS, BK), F32),
            struct((16, WIDE), F32),
            struct((NZ, BPACK, 128), F32),
            struct((8, 128), F32),
        ],
        [share, statistic, basis],
        [pltpu.VMEM((16, WIDE), F32), pltpu.VMEM((BPACK, 128), F32)],
        flops=12 * 16 * BK * WIDE,
    )
    r_mid = swap(r_packed, "z")

    *up_parts, new_second = call(
        rotate_body,
        [struct((XROWS, 384), BF16)] * 4 + [struct((1, COLS, BK), BF16)],
        [piece, moment, rounded, jnp.swapaxes(second_moment, 1, 2), clip],
        [parts],
        at=x,
        flops=6 * BK * BK * 384,
        nbytes=4 << 20,
    )
    up_parts = deal(up_parts)
    (new_first,) = call(
        first_body, struct((1, ROWS, FF), BF16), [gradient, first_moment, clip]
    )
    (r_copies,) = call(
        copies_body, struct((NX, NZ, BPACK, 128), F32), [r_mid], after=up_parts[1:], far=[new_first]
    )
    r_all = swap(r_copies, "x")
    (up_packed,) = call(
        pack_update_body,
        struct((NZ, PACK, 128), BF16),
        up_parts,
        [parts, rows, chunk],
        at=x,
        after=[r_all],
    )
    up_mid = swap(up_packed, "z")

    (new_basis,) = call(
        factor_body,
        struct((1, ROWS, BK), F32),
        [r_all, own],
        [
            pltpu.VMEM((BK, WIDE), F32),
            pltpu.VMEM((WIDE + 16, WIDE), F32),
            pltpu.VMEM((16, WIDE), F32),
            pltpu.VMEM((128, 128), F32),
        ],
        flops=12 * BK * WIDE * WIDE,
    )
    (update,) = call(
        unpack_update_body,
        struct((1, ROWS, FF), BF16),
        [up_mid],
        [chunk, pltpu.VMEM((16, 384), F32), natural],
    )
    return update, new_first, jnp.swapaxes(new_second, 1, 2), new_stat, new_basis


def solution(mesh):
    grid = Mesh(mesh.devices.reshape(NX, NZ, 4, 2), ("x", "z", "y", "c"))
    rows = P(("y", "c"), ("x", "z"), None)
    cols = P(("y", "c"), None, ("x", "z"))
    return jax.shard_map(
        local,
        mesh=grid,
        in_specs=(rows, rows, cols, rows, rows),
        out_specs=(rows, rows, cols, rows, rows),
        check_vma=False,
    )
```

time: 325 us -> 234 us (0.72)
  the two profiles are of different devices: /device:TPU:32 before, /device:TPU:8 now
where the time goes in v2:
time: 234 us; the launch traced here: 233 us
  starting transfers between devices  105 us (45%)
  waiting for transfers between devices  57.9 us (25%)
  Pallas kernels  40.9 us (17%)
  blocking collectives  19.4 us (8%)
  local copies, waits for them, and re-layouts  8.13 us (3%)
    all_to_all x5, starting transfers between devices, swap(): return lax.all_to_all(v, axis, 0, 0, tiled=True)  58.7 us
    ppermute x13, starting transfers between devices, shift(): return lax.ppermute(v, axis, [(k, (k + d) % size) for k in range(size)])  46.7 us
    pallas_call x12, Pallas kernels, call(): pl.pallas_call(run, out_shape=tuple(outs), in_specs=[pl.BlockSpec(memory_...  40.9 us
    ppermute x13, waiting for transfers between devices, shift(): return lax.ppermute(v, axis, [(k, (k + d) % size) for k in range(size)])  34.4 us
    all_to_all x5, waiting for transfers between devices, swap(): return lax.all_to_all(v, axis, 0, 0, tiled=True)  23.5 us
    all_to_all x1, blocking collectives, swap(): return lax.all_to_all(v, axis, 0, 0, tiled=True)  19.4 us
    unnamed x28, local copies, waits for them, and re-layouts  8.13 us
  transfers between devices with their start and end apart: 18, of which 11 were waited for; matrix products, arithmetic and copies ran while one was open for 1% of the time, Pallas kernels for 13%

profile of v2, /device:TPU:8, one launch (start us, length us, event | category | flops | bytes accessed | tf_op | source)
XLA Modules:
  0.0 232.7 jit_solution(8321939366574053974)
XLA Ops:
  2.8 5.7 %shard_map.92 = (bf16[16,168,128]{2,1,0:T(8,128)(2,1)}, f32[8,128]{1,0:T(8,128)S(1)}) custom-call(bf16[1,9,18432]{2,1,0:T(8,128)(2,1)S(1)} %copy-done, bf16[1,9,18432]{2,1,0:T(8,128)(2,1)S(1)} %copy-done.2), custom_call_target="tpu_custom_call" | custom-call | bytes 1048576 | tf_op jit(solution)/shard_map/pallas_call | solution.py:55
  8.5 15.2 %all-to-all-start = ((bf16[16,168,128]{2,1,0:T(8,128)(2,1)}), bf16[16,168,128]{2,1,0:T(8,128)(2,1)S(1)}, u32[]{:S(2)}, u32[]{:S(2)}) async-start(bf16[16,168,128]{2,1,0:T(8,128)(2,1)} %get-tuple-element.25), calls=%async_computation | async-start | bytes 1376256 | tf_op jit(solution)/shard_map/all_to_all | solution.py:429
  23.7 1.9 collective-permute-start
  26.7 3.5 %collective-permute-start.1 = (f32[8,128]{1,0:T(8,128)S(1)}, f32[8,128]{1,0:T(8,128)S(1)}, u32[]{:S(2)}, u32[]{:S(2)}) collective-permute-start(f32[8,128]{1,0:T(8,128)S(1)} %add.3.refs_2_), channel_id=1, source_target_pairs={{0,2},{2,4},{4,6},{6,0},{1,3},{3,5},{5,7},{7,1},{8,10},{10,12},{12... | collective-permute-start | bytes 12296 | tf_op jit(solution)/shard_map/ppermute | solution.py:433
  30.2 2.8 %collective-permute-start.2 = (f32[8,128]{1,0:T(8,128)S(1)}, f32[8,128]{1,0:T(8,128)S(1)}, u32[]{:S(2)}, u32[]{:S(2)}) collective-permute-start(f32[8,128]{1,0:T(8,128)S(1)} %add.3.refs_2_), channel_id=1, source_target_pairs={{0,4},{2,6},{4,0},{6,2},{1,5},{3,7},{5,1},{7,3},{8,12},{10,14},{12... | collective-permute-start | bytes 12296 | tf_op jit(solution)/shard_map/ppermute | solution.py:433
  33.1 4.3 %collective-permute-start.3 = (f32[8,128]{1,0:T(8,128)S(1)}, f32[8,128]{1,0:T(8,128)S(1)}, u32[]{:S(2)}, u32[]{:S(2)}) collective-permute-start(f32[8,128]{1,0:T(8,128)S(1)} %add.3.refs_2_), channel_id=1, source_target_pairs={{0,6},{2,0},{4,2},{6,4},{1,7},{3,1},{5,3},{7,5},{8,14},{10,8},{12,... | collective-permute-start | bytes 12296 | tf_op jit(solution)/shard_map/ppermute | solution.py:433
  38.7 19.9 %all-to-all-done.refs_1_.refs_4_ = bf16[16,168,128]{2,1,0:T(8,128)(2,1)S(1)} async-done(((bf16[16,168,128]{2,1,0:T(8,128)(2,1)}), bf16[16,168,128]{2,1,0:T(8,128)(2,1)S(1)}, u32[]{:S(2)}, u32[]{:S(2)}) %all-to-all-start) | async-done | bytes 688160 | tf_op jit(solution)/shard_map/all_to_all | solution.py:429
  59.4 7.4 %all-to-all-start.1 = ((f32[16,48,128]{2,1,0:T(8,128)}), f32[16,48,128]{2,1,0:T(8,128)S(1)}, u32[]{:S(2)}, u32[]{:S(2)}) async-start(f32[16,48,128]{2,1,0:T(8,128)} %shard_map.95), calls=%async_computation.1 | async-start | bytes 786432 | tf_op jit(solution)/shard_map/all_to_all | solution.py:429
  67.5 3.4 %collective-permute-start.4 = (bf16[208,1152]{1,0:T(8,128)(2,1)S(1)}, bf16[208,1152]{1,0:T(8,128)(2,1)S(1)}, u32[]{:S(2)}, u32[]{:S(2)}) collective-permute-start(bf16[208,1152]{1,0:T(8,128)(2,1)S(1)} %get-tuple-element.28), channel_id=1, source_target_pairs={{0,128},{128,256},{256,384},{384,0},{1,129},{129,257},{257,385},{3... | collective-permute-start | bytes 1437704 | tf_op jit(solution)/shard_map/ppermute | solution.py:433
  70.9 4.6 %collective-permute-start.5 = (bf16[208,1152]{1,0:T(8,128)(2,1)S(1)}, bf16[208,1152]{1,0:T(8,128)(2,1)S(1)}, u32[]{:S(2)}, u32[]{:S(2)}) collective-permute-start(bf16[208,1152]{1,0:T(8,128)(2,1)S(1)} %get-tuple-element.29), channel_id=1, source_target_pairs={{0,256},{128,384},{256,0},{384,128},{1,257},{129,385},{257,1},{385... | collective-permute-start | bytes 1437704 | tf_op jit(solution)/shard_map/ppermute | solution.py:433
  75.6 3.3 %collective-permute-start.6 = (bf16[208,1152]{1,0:T(8,128)(2,1)S(1)}, bf16[208,1152]{1,0:T(8,128)(2,1)S(1)}, u32[]{:S(2)}, u32[]{:S(2)}) collective-permute-start(bf16[208,1152]{1,0:T(8,128)(2,1)S(1)} %get-tuple-element.30), channel_id=1, source_target_pairs={{0,384},{128,0},{256,128},{384,256},{1,385},{129,1},{257,129},{385... | collective-permute-start | bytes 1437704 | tf_op jit(solution)/shard_map/ppermute | solution.py:433
  78.9 4.6 %collective-permute-done.4.refs_2_ = bf16[208,1152]{1,0:T(8,128)(2,1)S(1)} collective-permute-done((bf16[208,1152]{1,0:T(8,128)(2,1)S(1)}, bf16[208,1152]{1,0:T(8,128)(2,1)S(1)}, u32[]{:S(2)}, u32[]{:S(2)}) %collective-permute-start.4) | collective-permute-done | bytes 479264 | tf_op jit(solution)/shard_map/ppermute | solution.py:433
  83.5 10.9 %collective-permute-done.5.refs_3_ = bf16[208,1152]{1,0:T(8,128)(2,1)S(1)} collective-permute-done((bf16[208,1152]{1,0:T(8,128)(2,1)S(1)}, bf16[208,1152]{1,0:T(8,128)(2,1)S(1)}, u32[]{:S(2)}, u32[]{:S(2)}) %collective-permute-start.5) | collective-permute-done | bytes 479264 | tf_op jit(solution)/shard_map/ppermute | solution.py:433
  96.0 1.6 shard_map.94
  99.1 11.7 %all-to-all-start.2 = ((f32[16,48,128]{2,1,0:T(8,128)}), f32[16,48,128]{2,1,0:T(8,128)S(1)}, u32[]{:S(2)}, u32[]{:S(2)}) async-start(f32[16,48,128]{2,1,0:T(8,128)} %get-tuple-element.34), calls=%async_computation.2 | async-start | bytes 786432 | tf_op jit(solution)/shard_map/all_to_all | solution.py:429
  110.8 4.3 %collective-permute-start.7 = (f32[16,48,128]{2,1,0:T(8,128)S(1)}, f32[16,48,128]{2,1,0:T(8,128)S(1)}, u32[]{:S(2)}, u32[]{:S(2)}) collective-permute-start(f32[16,48,128]{2,1,0:T(8,128)S(1)} %all-to-all-done.1.refs_1_), channel_id=1, source_target_pairs={{0,128},{128,256},{256,384},{384,0},{1,129},{129,257},{257,385},{3... | collective-permute-start | bytes 1179656 | tf_op jit(solution)/shard_map/ppermute | solution.py:433
  115.1 3.6 %collective-permute-start.8 = (f32[16,48,128]{2,1,0:T(8,128)S(1)}, f32[16,48,128]{2,1,0:T(8,128)S(1)}, u32[]{:S(2)}, u32[]{:S(2)}) collective-permute-start(f32[16,48,128]{2,1,0:T(8,128)S(1)} %all-to-all-done.1.refs_1_), channel_id=1, source_target_pairs={{0,256},{128,384},{256,0},{384,128},{1,257},{129,385},{257,1},{385... | collective-permute-start | bytes 1179656 | tf_op jit(solution)/shard_map/ppermute | solution.py:433
  118.7 3.5 %collective-permute-start.9 = (f32[16,48,128]{2,1,0:T(8,128)S(1)}, f32[16,48,128]{2,1,0:T(8,128)S(1)}, u32[]{:S(2)}, u32[]{:S(2)}) collective-permute-start(f32[16,48,128]{2,1,0:T(8,128)S(1)} %all-to-all-done.1.refs_1_), channel_id=1, source_target_pairs={{0,384},{128,0},{256,128},{384,256},{1,385},{129,1},{257,129},{385... | collective-permute-start | bytes 1179656 | tf_op jit(solution)/shard_map/ppermute | solution.py:433
  122.2 2.4 %collective-permute-done.7.refs_2_ = f32[16,48,128]{2,1,0:T(8,128)S(1)} collective-permute-done((f32[16,48,128]{2,1,0:T(8,128)S(1)}, f32[16,48,128]{2,1,0:T(8,128)S(1)}, u32[]{:S(2)}, u32[]{:S(2)}) %collective-permute-start.7) | collective-permute-done | bytes 393248 | tf_op jit(solution)/shard_map/ppermute | solution.py:433
  124.6 9.3 %collective-permute-done.8.refs_3_ = f32[16,48,128]{2,1,0:T(8,128)S(1)} collective-permute-done((f32[16,48,128]{2,1,0:T(8,128)S(1)}, f32[16,48,128]{2,1,0:T(8,128)S(1)}, u32[]{:S(2)}, u32[]{:S(2)}) %collective-permute-start.8) | collective-permute-done | bytes 393248 | tf_op jit(solution)/shard_map/ppermute | solution.py:433
  135.8 1.6 shard_map.97
  137.3 11.7 %all-to-all-start.3 = ((f32[16,48,128]{2,1,0:T(8,128)}), f32[16,48,128]{2,1,0:T(8,128)S(1)}, u32[]{:S(2)}, u32[]{:S(2)}) async-start(f32[16,48,128]{2,1,0:T(8,128)} %get-tuple-element.41), calls=%async_computation.3 | async-start | bytes 786432 | tf_op jit(solution)/shard_map/all_to_all | solution.py:429
  151.2 2.3 shard_map.98
  153.5 4.3 %collective-permute-start.10 = (bf16[144,384]{1,0:T(8,128)(2,1)S(1)}, bf16[144,384]{1,0:T(8,128)(2,1)S(1)}, u32[]{:S(2)}, u32[]{:S(2)}) collective-permute-start(bf16[144,384]{1,0:T(8,128)(2,1)S(1)} %get-tuple-element.38), channel_id=1, source_target_pairs={{0,128},{128,256},{256,384},{384,0},{1,129},{129,257},{257,385},{3... | collective-permute-start | bytes 331784 | tf_op jit(solution)/shard_map/ppermute | solution.py:433
  157.7 3.6 %collective-permute-start.11 = (bf16[144,384]{1,0:T(8,128)(2,1)S(1)}, bf16[144,384]{1,0:T(8,128)(2,1)S(1)}, u32[]{:S(2)}, u32[]{:S(2)}) collective-permute-start(bf16[144,384]{1,0:T(8,128)(2,1)S(1)} %get-tuple-element.39), channel_id=1, source_target_pairs={{0,256},{128,384},{256,0},{384,128},{1,257},{129,385},{257,1},{385... | collective-permute-start | bytes 331784 | tf_op jit(solution)/shard_map/ppermute | solution.py:433
  161.4 3.5 %collective-permute-start.12 = (bf16[144,384]{1,0:T(8,128)(2,1)S(1)}, bf16[144,384]{1,0:T(8,128)(2,1)S(1)}, u32[]{:S(2)}, u32[]{:S(2)}) collective-permute-start(bf16[144,384]{1,0:T(8,128)(2,1)S(1)} %get-tuple-element.40), channel_id=1, source_target_pairs={{0,384},{128,0},{256,128},{384,256},{1,385},{129,1},{257,129},{385... | collective-permute-start | bytes 331784 | tf_op jit(solution)/shard_map/ppermute | solution.py:433
  166.1 1.9 collective-permute-done.12.refs_3_.refs_4_
  168.0 3.5 %all-to-all-done.3.refs_0_ = f32[16,48,128]{2,1,0:T(8,128)S(1)} async-done(((f32[16,48,128]{2,1,0:T(8,128)}), f32[16,48,128]{2,1,0:T(8,128)S(1)}, u32[]{:S(2)}, u32[]{:S(2)}) %all-to-all-start.3) | async-done | bytes 393248 | tf_op jit(solution)/shard_map/all_to_all | solution.py:429
  172.7 19.4 %all_to_all.30.refs_5_.refs_0_ = f32[4,16,48,128]{3,2,1,0:T(8,128)S(1)} all-to-all(f32[4,16,48,128]{3,2,1,0:T(8,128)S(1)} %shard_map.100), channel_id=1, replica_groups=mesh['x'=4,'z'=16,'y'=4,'c'=2] {'x'}, dimensions={0} | all-to-all | bytes 3145728 | tf_op jit(solution)/shard_map/all_to_all | solution.py:429
  193.2 12.6 %all-to-all-start.5 = ((bf16[16,88,128]{2,1,0:T(8,128)(2,1)}), bf16[16,88,128]{2,1,0:T(8,128)(2,1)S(1)}, u32[]{:S(2)}, u32[]{:S(2)}) async-start(bf16[16,88,128]{2,1,0:T(8,128)(2,1)} %shard_map.101), calls=%async_computation.5 | async-start | bytes 720896 | tf_op jit(solution)/shard_map/all_to_all | solution.py:429
  206.5 23.9 %shard_map.103 = f32[1,9,576]{2,1,0:T(8,128)S(1)} custom-call(f32[4,16,48,128]{3,2,1,0:T(8,128)S(1)} %all_to_all.30.refs_5_.refs_0_, f32[16,640]{1,0:T(8,128)S(1)} %get-tuple-element.44.refs_1_), custom_call_target="tpu_custom_call" | custom-call | flops 2831155200 | bytes 1048576 | tf_op jit(solution)/shard_map/pallas_call | solution.py:55
  231.1 1.6 shard_map.102
  (46 shorter events, 17.7 us)
Async XLA Ops:
  0.6 1.1 copy-start
  1.7 1.1 copy-start.2
  2.8 34.6 %copy-start.10 = (f32[1,9,576]{2,0,1:T(1,128)S(1)}, f32[1,9,576]{2,0,1:T(1,128)}, u32[]{:S(2)}) copy-start(f32[1,9,576]{2,0,1:T(1,128)} %param.9) | copy-start | bytes 62212
  8.5 50.2 %all-to-all-start = ((bf16[16,168,128]{2,1,0:T(8,128)(2,1)}), bf16[16,168,128]{2,1,0:T(8,128)(2,1)S(1)}, u32[]{:S(2)}, u32[]{:S(2)}) async-start(bf16[16,168,128]{2,1,0:T(8,128)(2,1)} %get-tuple-element.25), calls=%async_computation | async-start | bytes 1376256 | tf_op jit(solution)/shard_map/all_to_all | solution.py:429
  23.7 3.1 %collective-permute-start = (f32[8,128]{1,0:T(8,128)S(1)}, f32[8,128]{1,0:T(8,128)S(1)}, u32[]{:S(2)}, u32[]{:S(2)}) collective-permute-start(f32[8,128]{1,0:T(8,128)S(1)} %get-tuple-element.26), channel_id=1, source_target_pairs={{0,1},{1,0},{2,3},{3,2},{4,5},{5,4},{6,7},{7,6},{8,9},{9,8},{10,11... | collective-permute-start | bytes 12296 | tf_op jit(solution)/shard_map/ppermute | solution.py:433
  26.7 10.7 %collective-permute-start.1 = (f32[8,128]{1,0:T(8,128)S(1)}, f32[8,128]{1,0:T(8,128)S(1)}, u32[]{:S(2)}, u32[]{:S(2)}) collective-permute-start(f32[8,128]{1,0:T(8,128)S(1)} %add.3.refs_2_), channel_id=1, source_target_pairs={{0,2},{2,4},{4,6},{6,0},{1,3},{3,5},{5,7},{7,1},{8,10},{10,12},{12... | collective-permute-start | bytes 12296 | tf_op jit(solution)/shard_map/ppermute | solution.py:433
  30.2 7.2 %collective-permute-start.2 = (f32[8,128]{1,0:T(8,128)S(1)}, f32[8,128]{1,0:T(8,128)S(1)}, u32[]{:S(2)}, u32[]{:S(2)}) collective-permute-start(f32[8,128]{1,0:T(8,128)S(1)} %add.3.refs_2_), channel_id=1, source_target_pairs={{0,4},{2,6},{4,0},{6,2},{1,5},{3,7},{5,1},{7,3},{8,12},{10,14},{12... | collective-permute-start | bytes 12296 | tf_op jit(solution)/shard_map/ppermute | solution.py:433
  33.1 5.6 %collective-permute-start.3 = (f32[8,128]{1,0:T(8,128)S(1)}, f32[8,128]{1,0:T(8,128)S(1)}, u32[]{:S(2)}, u32[]{:S(2)}) collective-permute-start(f32[8,128]{1,0:T(8,128)S(1)} %add.3.refs_2_), channel_id=1, source_target_pairs={{0,6},{2,0},{4,2},{6,4},{1,7},{3,1},{5,3},{7,5},{8,14},{10,8},{12,... | collective-permute-start | bytes 12296 | tf_op jit(solution)/shard_map/ppermute | solution.py:433
  59.4 39.6 %all-to-all-start.1 = ((f32[16,48,128]{2,1,0:T(8,128)}), f32[16,48,128]{2,1,0:T(8,128)S(1)}, u32[]{:S(2)}, u32[]{:S(2)}) async-start(f32[16,48,128]{2,1,0:T(8,128)} %shard_map.95), calls=%async_computation.1 | async-start | bytes 786432 | tf_op jit(solution)/shard_map/all_to_all | solution.py:429
  66.9 55.3 %copy-start.11 = (f32[1,9,576]{2,0,1:T(1,128)S(1)}, f32[1,9,576]{2,0,1:T(1,128)}, u32[]{:S(2)}) copy-start(f32[1,9,576]{2,0,1:T(1,128)} %param.8) | copy-start | bytes 62212
  67.5 16.0 %collective-permute-start.4 = (bf16[208,1152]{1,0:T(8,128)(2,1)S(1)}, bf16[208,1152]{1,0:T(8,128)(2,1)S(1)}, u32[]{:S(2)}, u32[]{:S(2)}) collective-permute-start(bf16[208,1152]{1,0:T(8,128)(2,1)S(1)} %get-tuple-element.28), channel_id=1, source_target_pairs={{0,128},{128,256},{256,384},{384,0},{1,129},{129,257},{257,385},{3... | collective-permute-start | bytes 1437704 | tf_op jit(solution)/shard_map/ppermute | solution.py:433
  70.9 23.5 %collective-permute-start.5 = (bf16[208,1152]{1,0:T(8,128)(2,1)S(1)}, bf16[208,1152]{1,0:T(8,128)(2,1)S(1)}, u32[]{:S(2)}, u32[]{:S(2)}) collective-permute-start(bf16[208,1152]{1,0:T(8,128)(2,1)S(1)} %get-tuple-element.29), channel_id=1, source_target_pairs={{0,256},{128,384},{256,0},{384,128},{1,257},{129,385},{257,1},{385... | collective-permute-start | bytes 1437704 | tf_op jit(solution)/shard_map/ppermute | solution.py:433
  75.6 20.4 %collective-permute-start.6 = (bf16[208,1152]{1,0:T(8,128)(2,1)S(1)}, bf16[208,1152]{1,0:T(8,128)(2,1)S(1)}, u32[]{:S(2)}, u32[]{:S(2)}) collective-permute-start(bf16[208,1152]{1,0:T(8,128)(2,1)S(1)} %get-tuple-element.30), channel_id=1, source_target_pairs={{0,384},{128,0},{256,128},{384,256},{1,385},{129,1},{257,129},{385... | collective-permute-start | bytes 1437704 | tf_op jit(solution)/shard_map/ppermute | solution.py:433
  97.5 0.8 copy-start.5
  98.3 0.8 copy-start.7
  99.1 36.7 %all-to-all-start.2 = ((f32[16,48,128]{2,1,0:T(8,128)}), f32[16,48,128]{2,1,0:T(8,128)S(1)}, u32[]{:S(2)}, u32[]{:S(2)}) async-start(f32[16,48,128]{2,1,0:T(8,128)} %get-tuple-element.34), calls=%async_computation.2 | async-start | bytes 786432 | tf_op jit(solution)/shard_map/all_to_all | solution.py:429
  110.8 13.8 %collective-permute-start.7 = (f32[16,48,128]{2,1,0:T(8,128)S(1)}, f32[16,48,128]{2,1,0:T(8,128)S(1)}, u32[]{:S(2)}, u32[]{:S(2)}) collective-permute-start(f32[16,48,128]{2,1,0:T(8,128)S(1)} %all-to-all-done.1.refs_1_), channel_id=1, source_target_pairs={{0,128},{128,256},{256,384},{384,0},{1,129},{129,257},{257,385},{3... | collective-permute-start | bytes 1179656 | tf_op jit(solution)/shard_map/ppermute | solution.py:433
  115.1 18.9 %collective-permute-start.8 = (f32[16,48,128]{2,1,0:T(8,128)S(1)}, f32[16,48,128]{2,1,0:T(8,128)S(1)}, u32[]{:S(2)}, u32[]{:S(2)}) collective-permute-start(f32[16,48,128]{2,1,0:T(8,128)S(1)} %all-to-all-done.1.refs_1_), channel_id=1, source_target_pairs={{0,256},{128,384},{256,0},{384,128},{1,257},{129,385},{257,1},{385... | collective-permute-start | bytes 1179656 | tf_op jit(solution)/shard_map/ppermute | solution.py:433
  118.7 16.6 %collective-permute-start.9 = (f32[16,48,128]{2,1,0:T(8,128)S(1)}, f32[16,48,128]{2,1,0:T(8,128)S(1)}, u32[]{:S(2)}, u32[]{:S(2)}) collective-permute-start(f32[16,48,128]{2,1,0:T(8,128)S(1)} %all-to-all-done.1.refs_1_), channel_id=1, source_target_pairs={{0,384},{128,0},{256,128},{384,256},{1,385},{129,1},{257,129},{385... | collective-permute-start | bytes 1179656 | tf_op jit(solution)/shard_map/ppermute | solution.py:433
  135.7 13.4 %copy-start.6 = (bf16[576,384]{1,0:T(8,128)(2,1)S(1)}, bf16[576,384]{1,0:T(8,128)(2,1)}, u32[]{:S(2)}) copy-start(bf16[576,384]{1,0:T(8,128)(2,1)} %copy-done.5) | copy-start | bytes 1327108
  137.3 34.2 %all-to-all-start.3 = ((f32[16,48,128]{2,1,0:T(8,128)}), f32[16,48,128]{2,1,0:T(8,128)S(1)}, u32[]{:S(2)}, u32[]{:S(2)}) async-start(f32[16,48,128]{2,1,0:T(8,128)} %get-tuple-element.41), calls=%async_computation.3 | async-start | bytes 786432 | tf_op jit(solution)/shard_map/all_to_all | solution.py:429
  149.1 15.8 %copy-start.1 = (bf16[1,9,18432]{2,1,0:T(8,128)(2,1)S(1)}, bf16[1,9,18432]{2,1,0:T(8,128)(2,1)}, u32[]{:S(2)}) copy-start(bf16[1,9,18432]{2,1,0:T(8,128)(2,1)} %refs_0_.4) | copy-start | bytes 995332
  149.1 15.8 %copy-start.3 = (bf16[1,9,18432]{2,1,0:T(8,128)(2,1)S(1)}, bf16[1,9,18432]{2,1,0:T(8,128)(2,1)}, u32[]{:S(2)}) copy-start(bf16[1,9,18432]{2,1,0:T(8,128)(2,1)} %refs_1_.4) | copy-start | bytes 995332
  149.1 1.1 copy-start.8
  150.2 1.0 copy-start.9
  153.5 12.7 %collective-permute-start.10 = (bf16[144,384]{1,0:T(8,128)(2,1)S(1)}, bf16[144,384]{1,0:T(8,128)(2,1)S(1)}, u32[]{:S(2)}, u32[]{:S(2)}) collective-permute-start(bf16[144,384]{1,0:T(8,128)(2,1)S(1)} %get-tuple-element.38), channel_id=1, source_target_pairs={{0,128},{128,256},{256,384},{384,0},{1,129},{129,257},{257,385},{3... | collective-permute-start | bytes 331784 | tf_op jit(solution)/shard_map/ppermute | solution.py:433
  157.7 8.4 %collective-permute-start.11 = (bf16[144,384]{1,0:T(8,128)(2,1)S(1)}, bf16[144,384]{1,0:T(8,128)(2,1)S(1)}, u32[]{:S(2)}, u32[]{:S(2)}) collective-permute-start(bf16[144,384]{1,0:T(8,128)(2,1)S(1)} %get-tuple-element.39), channel_id=1, source_target_pairs={{0,256},{128,384},{256,0},{384,128},{1,257},{129,385},{257,1},{385... | collective-permute-start | bytes 331784 | tf_op jit(solution)/shard_map/ppermute | solution.py:433
  161.4 6.6 %collective-permute-start.12 = (bf16[144,384]{1,0:T(8,128)(2,1)S(1)}, bf16[144,384]{1,0:T(8,128)(2,1)S(1)}, u32[]{:S(2)}, u32[]{:S(2)}) collective-permute-start(bf16[144,384]{1,0:T(8,128)(2,1)S(1)} %get-tuple-element.40), channel_id=1, source_target_pairs={{0,384},{128,0},{256,128},{384,256},{1,385},{129,1},{257,129},{385... | collective-permute-start | bytes 331784 | tf_op jit(solution)/shard_map/ppermute | solution.py:433
  171.6 1.1 copy-start.4
  193.2 37.9 %all-to-all-start.5 = ((bf16[16,88,128]{2,1,0:T(8,128)(2,1)}), bf16[16,88,128]{2,1,0:T(8,128)(2,1)S(1)}, u32[]{:S(2)}, u32[]{:S(2)}) async-start(bf16[16,88,128]{2,1,0:T(8,128)(2,1)} %shard_map.101), calls=%async_computation.5 | async-start | bytes 720896 | tf_op jit(solution)/shard_map/all_to_all | solution.py:429

commit v3 on v2

--- a/solution.py
+++ b/solution.py
@@ -58,7 +58,7 @@
         in_specs=[pl.BlockSpec(memory_space=pltpu.SMEM)] * n_head
         + vmem(n_real)
         + vmem(len(after))
-        + [pl.BlockSpec(memory_space=pl.ANY)] * len(far),
+        + [pl.BlockSpec(memory_space=pltpu.HBM)] * len(far),
         out_specs=tuple(vmem(len(outs))),
         scratch_shapes=list(scratch),
         compiler_params=pltpu.CompilerParams(vmem_limit_bytes=16 << 20),
@@ -68,6 +68,9 @@
     )(*head, *args, *after, *far)
 
 
+ORDER = (0, 2, 1, 3)
+
+
 def back(x, d):
     return lax.rem(x + (NX - d), NX)
 
@@ -76,24 +79,53 @@
     return jax.ShapeDtypeStruct(shape, dtype)
 
 
-def pack_natural(src, put):
+def pack_natural(src, last, buf, first):
     lane = lax.broadcasted_iota(jnp.int32, (16, 128), 1)
-    for z in range(NZ):
-        rest = jnp.zeros((16, 128), F32)
+    row = lax.broadcasted_iota(jnp.int32, (16, 128), 0)
+    lane8 = lane[:8]
+    for s in range(4):
+        off = REST * s
+        rest = [jnp.zeros((8, 128), F32)] * 4
         for xp in range(NX):
-            start = XSTEP * xp + COLS * z
-            base = start // 128 * 128
-            off = start - base
-            w = src[:, base : base + 384]
-            if off:
-                w = pltpu.roll(w, 384 - off, 1)
-            for t in range(2):
-                put(z, 2 * xp + t, w[:ROWS, 128 * t : 128 * t + 128])
-            r = w[:, 256:384]
-            if xp:
-                r = pltpu.roll(r, REST * xp, 1)
-            rest = jnp.where((lane >= REST * xp) & (lane < REST * (xp + 1)), r, rest)
-        put(z, 8, rest[:ROWS])
+            for j in range(4):
+                z = 4 * j + s
+                base = XSTEP * xp + COLS * z - off
+                k = 4 * xp + j
+                last[k : k + 1, :] = src[8:9, base : base + 384]
+                w = src[:8, base : base + 384]
+                if off:
+                    w = pltpu.roll(w, 384 - off, 1)
+                for t in range(2):
+                    at = first + ROWS * (2 * xp + t)
+                    buf[z, at : at + 8, :] = w[:, 128 * t : 128 * t + 128]
+                r = w[:, 256:384]
+                if xp:
+                    r = pltpu.roll(r, REST * xp, 1)
+                mine = (lane8 >= REST * xp) & (lane8 < REST * (xp + 1))
+                rest[j] = jnp.where(mine, r, rest[j])
+        w = last[...]
+        if off:
+            w = pltpu.roll(w, 384 - off, 1)
+        r = w[:, 256:384]
+        turned = r
+        for xp in range(1, NX):
+            mine = (row >= 4 * xp) & (row < 4 * xp + 4)
+            turned = jnp.where(mine, pltpu.roll(r, REST * xp, 1), turned)
+        last[:, 0:256] = w[:, 0:256]
+        last[:, 256:384] = turned
+        for j in range(4):
+            z = 4 * j + s
+            end = first + 8 * ROWS
+            buf[z, end : end + 8, :] = rest[j]
+            for xp in range(NX):
+                k = 4 * xp + j
+                for t in range(2):
+                    at = first + ROWS * (2 * xp + t) + 8
+                    buf[z, at : at + 1, :] = last[k : k + 1, 128 * t : 128 * t + 128]
+                here = slice(REST * xp, REST * (xp + 1))
+                buf[z, end + 8 : end + 9, here] = last[
+                    k : k + 1, 256 + REST * xp : 256 + REST * (xp + 1)
+                ]
 
 
 def split(v):
@@ -102,22 +134,14 @@
     return high, mid, v - high - mid
 
 
-def pack_body(g_ref, m_ref, out_ref, sum_ref, src, buf):
+def pack_body(g_ref, m_ref, out_ref, sum_ref, src, last, buf):
     buf[:, 18 * ROWS :, :] = jnp.zeros((NZ, APACK - 18 * ROWS, 128), F32)
-
-    def put(first):
-        def store(z, t, rows):
-            at = ROWS * (first + t)
-            buf[z, at : at + ROWS, :] = rows
-
-        return store
-
     g = g_ref[0].astype(F32)
     sum_ref[...] = jnp.full(sum_ref.shape, jnp.sum(g * g), F32)
     src[:ROWS, :] = g
-    pack_natural(src, put(0))
+    pack_natural(src, last, buf, 0)
     src[:ROWS, :] = m_ref[0].astype(F32)
-    pack_natural(src, put(9))
+    pack_natural(src, last, buf, 9 * ROWS)
     for z in range(NZ):
         out_ref[z] = buf[z].astype(BF16)
 
@@ -165,7 +189,7 @@
 
 def covariance_body(x_ref, g0, g1, g2, g3, out_ref, piece_ref, moment_ref, every, prod):
     x = x_ref[0]
-    for d, g in enumerate((g0, g1, g2, g3)):
+    for d, g in zip(ORDER, (g0, g1, g2, g3)):
         every[back(x, d)] = g[:XROWS]
         for k in range(3):
             moment_ref[back(x, d), 48 * k : 48 * k + 48, :] = g[
@@ -204,7 +228,7 @@
 
 def unpack_basis_body(x_ref, b0, b1, b2, b3, full_ref, round_ref, buf):
     x = x_ref[0]
-    for d, b in enumerate((b0, b1, b2, b3)):
+    for d, b in zip(ORDER, (b0, b1, b2, b3)):
         buf[back(x, d)] = b[...]
     for xp in range(NX):
         unpack_square(buf.at[xp], full_ref.at[XROWS * xp : XROWS * (xp + 1)])
@@ -264,7 +288,7 @@
 
 def pack_update_body(x_ref, u0, u1, u2, u3, out_ref, parts, full, buf):
     x = x_ref[0]
-    for d, u in enumerate((u0, u1, u2, u3)):
+    for d, u in zip(ORDER, (u0, u1, u2, u3)):
         parts[back(x, d)] = u[...]
     lane = lax.broadcasted_iota(jnp.int32, (XROWS, 128), 1)
     rest = jnp.zeros((XROWS, 128), F32)
@@ -312,7 +336,8 @@
     out_ref[0] = nat[:ROWS, :].astype(BF16)
 
 
-def first_body(g_ref, m_ref, clip_ref, out_ref):
+def first_body(g_ref, m_ref, clip_ref, out_ref, done_ref):
+    done_ref[...] = clip_ref[...]
     clip = clip_ref[0:1, 0:1]
     out_ref[0] = (
         beta_first * m_ref[0].astype(F32)
@@ -327,35 +352,53 @@
     def spread(row):
         return jnp.broadcast_to(row, (8, 128))
 
+    def columns(rows, g):
+        return [spread(rows[:, 8 * g + c : 8 * g + c + 1]) for c in range(8)]
+
+    cols = columns(m_ref[8 * first : 8 * first + 8, :], first)
     for g in range(first, last):
         at = slice(8 * g, 8 * g + 8)
         here = (lane >= 8 * g) & (lane < 8 * g + 8)
-        v = m_ref[at, :]
-        cols = [spread(v[:, 8 * g + c : 8 * g + c + 1]) for c in range(8)]
-        v = jnp.where(here, jnp.where(lane == 8 * g + sub, 1.0, 0.0), v)
+        v = jnp.where(here, jnp.where(lane == 8 * g + sub, 1.0, 0.0), m_ref[at, :])
+        if g + 1 < 16:
+            w = m_ref[8 * g + 8 : 8 * g + 16, :]
+            down, ahead = columns(w, g), columns(w, g + 1)
         scale, pivot, coef = [], [], {}
         for i in range(8):
             rs = lax.rsqrt(spread(cols[i][i : i + 1, :]))
             left = jnp.where(sub > i, cols[i] * rs, 0.0)
-            row = spread(v[i : i + 1, :]) * rs
-            v = jnp.where(sub == i, row, v - left * row)
             for c in range(i + 1, 8):
                 coef[i, c] = spread(left[c : c + 1, :])
                 cols[c] = cols[c] - left * coef[i, c]
+            if g + 1 < 16:
+                k = down[i] * rs
+                for c in range(i + 1, 8):
+                    down[c] = down[c] - k * coef[i, c]
+                for c in range(8):
+                    ahead[c] = ahead[c] - k * spread(k[c : c + 1, :])
+                down[i] = k
+            row = spread(v[i : i + 1, :]) * rs
+            v = jnp.where(sub == i, row, v - left * row)
             scale.append(rs)
             pivot.append(row)
         m_ref[at, :] = v
         for r in range(g + 1, 16):
             to = slice(8 * r, 8 * r + 8)
             w = m_ref[to, :]
-            cols = [spread(w[:, 8 * g + c : 8 * g + c + 1]) for c in range(8)]
+            if r > g + 1:
+                part = columns(w, g)
             w = jnp.where(here, 0.0, w)
             for i in range(8):
-                k = cols[i] * scale[i]
+                if r > g + 1:
+                    k = part[i] * scale[i]
+                    for c in range(i + 1, 8):
+                        part[c] = part[c] - k * coef[i, c]
+                else:
+                    k = down[i]
                 w = w - k * pivot[i]
-                for c in range(i + 1, 8):
-                    cols[c] = cols[c] - k * coef[i, c]
             m_ref[to, :] = w
+        if g + 1 < 16:
+            cols = ahead
 
 
 def copies_body(in_ref, out_ref):
@@ -433,10 +476,10 @@
         return lax.ppermute(v, axis, [(k, (k + d) % size) for k in range(size)])
 
     def spread(v, axis="x"):
-        return [v] + [shift(v, axis, d) for d in (1, 2, 3)]
+        return [shift(v, axis, d) if d else v for d in ORDER]
 
     def deal(parts):
-        return [parts[0]] + [shift(parts[d], "x", d) for d in (1, 2, 3)]
+        return [shift(parts[d], "x", d) if d else parts[d] for d in ORDER]
 
     natural = pltpu.VMEM((16, FF), F32)
     chunk = pltpu.VMEM((PACK, 128), F32)
@@ -447,7 +490,7 @@
         pack_body,
         [struct((NZ, APACK, 128), BF16), struct((8, 128), F32)],
         [gradient, first_moment],
-        [natural, pltpu.VMEM((NZ, APACK, 128), F32)],
+        [natural, pltpu.VMEM((16, 384), F32), pltpu.VMEM((NZ, APACK, 128), F32)],
     )
     mid = swap(packed, "z")
     sums = spread(sums + shift(sums, "c", 1), "y")
@@ -512,11 +555,13 @@
         nbytes=4 << 20,
     )
     up_parts = deal(up_parts)
-    (new_first,) = call(
-        first_body, struct((1, ROWS, FF), BF16), [gradient, first_moment, clip]
+    new_first, first_done = call(
+        first_body,
+        [struct((1, ROWS, FF), BF16), struct((8, 128), F32)],
+        [gradient, first_moment, clip],
     )
     (r_copies,) = call(
-        copies_body, struct((NX, NZ, BPACK, 128), F32), [r_mid], after=up_parts[1:], far=[new_first]
+        copies_body, struct((NX, NZ, BPACK, 128), F32), [r_mid], after=[*up_parts[1:], first_done]
     )
     r_all = swap(r_copies, "x")
     (up_packed,) = call(

time: 234 us -> 224 us (0.957)
  Pallas kernels: 40.9 us -> 36.3 us
  waiting for transfers between devices: 57.9 us -> 55.2 us
    ppermute x13, waiting for transfers between devices: 34.4 us -> 28.6 us  [shift(): return lax.ppermute(v, axis, [(k, (k + d) % size) for k in range(size)])]
    pallas_call x12, Pallas kernels: 40.9 us -> 36.3 us  [call(): pl.pallas_call(run, out_shape=tuple(outs), in_specs=[pl.BlockSpec(memory_...]
    all_to_all x5, waiting for transfers between devices: 23.5 us -> 26.6 us  [swap(): return lax.all_to_all(v, axis, 0, 0, tiled=True)]
    unnamed x28 -> x26, local copies, waits for them, and re-layouts: 8.13 us -> 7.07 us
  transfers between devices with their start and end apart: 18 -> 18, of which waited for: 11 -> 12; matrix products, arithmetic and copies ran while one was open for 1% -> 1% of each run, Pallas kernels for 13% -> 12%
where the time goes in v3:
time: 224 us; the launch traced here: 223 us
  starting transfers between devices  105 us (47%)
  waiting for transfers between devices  55.2 us (25%)
  Pallas kernels  36.3 us (16%)
  blocking collectives  18.5 us (8%)
  local copies, waits for them, and re-layouts  7.07 us (3%)
    all_to_all x5, starting transfers between devices, swap(): return lax.all_to_all(v, axis, 0, 0, tiled=True)  57.5 us
    ppermute x13, starting transfers between devices, shift(): return lax.ppermute(v, axis, [(k, (k + d) % size) for k in range(size)])  47.7 us
    pallas_call x12, Pallas kernels, call(): pl.pallas_call(run, out_shape=tuple(outs), in_specs=[pl.BlockSpec(memory_...  36.3 us
    ppermute x13, waiting for transfers between devices, shift(): return lax.ppermute(v, axis, [(k, (k + d) % size) for k in range(size)])  28.6 us
    all_to_all x5, waiting for transfers between devices, swap(): return lax.all_to_all(v, axis, 0, 0, tiled=True)  26.6 us
    all_to_all x1, blocking collectives, swap(): return lax.all_to_all(v, axis, 0, 0, tiled=True)  18.5 us
    unnamed x26, local copies, waits for them, and re-layouts  7.07 us
  transfers between devices with their start and end apart: 18, of which 12 were waited for; matrix products, arithmetic and copies ran while one was open for 1% of the time, Pallas kernels for 12%

profile of v3, /device:TPU:8, one launch (start us, length us, event | category | flops | bytes accessed | tf_op | source)
XLA Modules:
  0.0 223.2 jit_solution(12169695288501223868)
XLA Ops:
  2.8 4.5 %shard_map.92 = (bf16[16,168,128]{2,1,0:T(8,128)(2,1)}, f32[8,128]{1,0:T(8,128)S(1)}) custom-call(bf16[1,9,18432]{2,1,0:T(8,128)(2,1)S(1)} %copy-done, bf16[1,9,18432]{2,1,0:T(8,128)(2,1)S(1)} %copy-done.2), custom_call_target="tpu_custom_call" | custom-call | bytes 1048576 | tf_op jit(solution)/shard_map/pallas_call | solution.py:55
  7.2 15.2 %all-to-all-start = ((bf16[16,168,128]{2,1,0:T(8,128)(2,1)}), bf16[16,168,128]{2,1,0:T(8,128)(2,1)S(1)}, u32[]{:S(2)}, u32[]{:S(2)}) async-start(bf16[16,168,128]{2,1,0:T(8,128)(2,1)} %get-tuple-element.27), calls=%async_computation | async-start | bytes 1376256 | tf_op jit(solution)/shard_map/all_to_all | solution.py:472
  22.4 1.9 collective-permute-start
  25.5 4.2 %collective-permute-start.1 = (f32[8,128]{1,0:T(8,128)S(1)}, f32[8,128]{1,0:T(8,128)S(1)}, u32[]{:S(2)}, u32[]{:S(2)}) collective-permute-start(f32[8,128]{1,0:T(8,128)S(1)} %add.3.refs_2_), channel_id=1, source_target_pairs={{0,4},{2,6},{4,0},{6,2},{1,5},{3,7},{5,1},{7,3},{8,12},{10,14},{12... | collective-permute-start | bytes 12296 | tf_op jit(solution)/shard_map/ppermute | solution.py:476
  29.7 1.9 collective-permute-start.2
  31.6 3.9 %collective-permute-start.3 = (f32[8,128]{1,0:T(8,128)S(1)}, f32[8,128]{1,0:T(8,128)S(1)}, u32[]{:S(2)}, u32[]{:S(2)}) collective-permute-start(f32[8,128]{1,0:T(8,128)S(1)} %add.3.refs_2_), channel_id=1, source_target_pairs={{0,6},{2,0},{4,2},{6,4},{1,7},{3,1},{5,3},{7,5},{8,14},{10,8},{12,... | collective-permute-start | bytes 12296 | tf_op jit(solution)/shard_map/ppermute | solution.py:476
  35.6 1.5 collective-permute-done.3.refs_5_.refs_3_
  37.1 20.3 %all-to-all-done.refs_1_.refs_4_ = bf16[16,168,128]{2,1,0:T(8,128)(2,1)S(1)} async-done(((bf16[16,168,128]{2,1,0:T(8,128)(2,1)}), bf16[16,168,128]{2,1,0:T(8,128)(2,1)S(1)}, u32[]{:S(2)}, u32[]{:S(2)}) %all-to-all-start) | async-done | bytes 688160 | tf_op jit(solution)/shard_map/all_to_all | solution.py:472
  58.2 7.4 %all-to-all-start.1 = ((f32[16,48,128]{2,1,0:T(8,128)}), f32[16,48,128]{2,1,0:T(8,128)S(1)}, u32[]{:S(2)}, u32[]{:S(2)}) async-start(f32[16,48,128]{2,1,0:T(8,128)} %shard_map.95), calls=%async_computation.1 | async-start | bytes 786432 | tf_op jit(solution)/shard_map/all_to_all | solution.py:472
  66.3 4.9 %collective-permute-start.4 = (bf16[208,1152]{1,0:T(8,128)(2,1)S(1)}, bf16[208,1152]{1,0:T(8,128)(2,1)S(1)}, u32[]{:S(2)}, u32[]{:S(2)}) collective-permute-start(bf16[208,1152]{1,0:T(8,128)(2,1)S(1)} %get-tuple-element.30), channel_id=1, source_target_pairs={{0,256},{128,384},{256,0},{384,128},{1,257},{129,385},{257,1},{385... | collective-permute-start | bytes 1437704 | tf_op jit(solution)/shard_map/ppermute | solution.py:476
  71.2 2.5 %collective-permute-start.5 = (bf16[208,1152]{1,0:T(8,128)(2,1)S(1)}, bf16[208,1152]{1,0:T(8,128)(2,1)S(1)}, u32[]{:S(2)}, u32[]{:S(2)}) collective-permute-start(bf16[208,1152]{1,0:T(8,128)(2,1)S(1)} %get-tuple-element.31), channel_id=1, source_target_pairs={{0,128},{128,256},{256,384},{384,0},{1,129},{129,257},{257,385},{3... | collective-permute-start | bytes 1437704 | tf_op jit(solution)/shard_map/ppermute | solution.py:476
  73.7 4.6 %collective-permute-start.6 = (bf16[208,1152]{1,0:T(8,128)(2,1)S(1)}, bf16[208,1152]{1,0:T(8,128)(2,1)S(1)}, u32[]{:S(2)}, u32[]{:S(2)}) collective-permute-start(bf16[208,1152]{1,0:T(8,128)(2,1)S(1)} %get-tuple-element.32), channel_id=1, source_target_pairs={{0,384},{128,0},{256,128},{384,256},{1,385},{129,1},{257,129},{385... | collective-permute-start | bytes 1437704 | tf_op jit(solution)/shard_map/ppermute | solution.py:476
  78.3 5.3 %collective-permute-done.4.refs_2_ = bf16[208,1152]{1,0:T(8,128)(2,1)S(1)} collective-permute-done((bf16[208,1152]{1,0:T(8,128)(2,1)S(1)}, bf16[208,1152]{1,0:T(8,128)(2,1)S(1)}, u32[]{:S(2)}, u32[]{:S(2)}) %collective-permute-start.4) | collective-permute-done | bytes 479264 | tf_op jit(solution)/shard_map/ppermute | solution.py:476
  83.6 8.9 %collective-permute-done.5.refs_3_ = bf16[208,1152]{1,0:T(8,128)(2,1)S(1)} collective-permute-done((bf16[208,1152]{1,0:T(8,128)(2,1)S(1)}, bf16[208,1152]{1,0:T(8,128)(2,1)S(1)}, u32[]{:S(2)}, u32[]{:S(2)}) %collective-permute-start.5) | collective-permute-done | bytes 479264 | tf_op jit(solution)/shard_map/ppermute | solution.py:476
  92.6 1.6 shard_map.94
  95.7 11.7 %all-to-all-start.2 = ((f32[16,48,128]{2,1,0:T(8,128)}), f32[16,48,128]{2,1,0:T(8,128)S(1)}, u32[]{:S(2)}, u32[]{:S(2)}) async-start(f32[16,48,128]{2,1,0:T(8,128)} %get-tuple-element.36), calls=%async_computation.2 | async-start | bytes 786432 | tf_op jit(solution)/shard_map/all_to_all | solution.py:472
  107.5 4.8 %collective-permute-start.7 = (f32[16,48,128]{2,1,0:T(8,128)S(1)}, f32[16,48,128]{2,1,0:T(8,128)S(1)}, u32[]{:S(2)}, u32[]{:S(2)}) collective-permute-start(f32[16,48,128]{2,1,0:T(8,128)S(1)} %all-to-all-done.1.refs_1_), channel_id=1, source_target_pairs={{0,256},{128,384},{256,0},{384,128},{1,257},{129,385},{257,1},{385... | collective-permute-start | bytes 1179656 | tf_op jit(solution)/shard_map/ppermute | solution.py:476
  112.3 2.5 %collective-permute-start.8 = (f32[16,48,128]{2,1,0:T(8,128)S(1)}, f32[16,48,128]{2,1,0:T(8,128)S(1)}, u32[]{:S(2)}, u32[]{:S(2)}) collective-permute-start(f32[16,48,128]{2,1,0:T(8,128)S(1)} %all-to-all-done.1.refs_1_), channel_id=1, source_target_pairs={{0,128},{128,256},{256,384},{384,0},{1,129},{129,257},{257,385},{3... | collective-permute-start | bytes 1179656 | tf_op jit(solution)/shard_map/ppermute | solution.py:476
  114.8 4.6 %collective-permute-start.9 = (f32[16,48,128]{2,1,0:T(8,128)S(1)}, f32[16,48,128]{2,1,0:T(8,128)S(1)}, u32[]{:S(2)}, u32[]{:S(2)}) collective-permute-start(f32[16,48,128]{2,1,0:T(8,128)S(1)} %all-to-all-done.1.refs_1_), channel_id=1, source_target_pairs={{0,384},{128,0},{256,128},{384,256},{1,385},{129,1},{257,129},{385... | collective-permute-start | bytes 1179656 | tf_op jit(solution)/shard_map/ppermute | solution.py:476
  119.4 3.6 %collective-permute-done.7.refs_2_ = f32[16,48,128]{2,1,0:T(8,128)S(1)} collective-permute-done((f32[16,48,128]{2,1,0:T(8,128)S(1)}, f32[16,48,128]{2,1,0:T(8,128)S(1)}, u32[]{:S(2)}, u32[]{:S(2)}) %collective-permute-start.7) | collective-permute-done | bytes 393248 | tf_op jit(solution)/shard_map/ppermute | solution.py:476
  122.9 7.0 %collective-permute-done.8.refs_3_ = f32[16,48,128]{2,1,0:T(8,128)S(1)} collective-permute-done((f32[16,48,128]{2,1,0:T(8,128)S(1)}, f32[16,48,128]{2,1,0:T(8,128)S(1)}, u32[]{:S(2)}, u32[]{:S(2)}) %collective-permute-start.8) | collective-permute-done | bytes 393248 | tf_op jit(solution)/shard_map/ppermute | solution.py:476
  131.4 1.6 shard_map.97
  132.9 10.8 %all-to-all-start.3 = ((f32[16,48,128]{2,1,0:T(8,128)}), f32[16,48,128]{2,1,0:T(8,128)S(1)}, u32[]{:S(2)}, u32[]{:S(2)}) async-start(f32[16,48,128]{2,1,0:T(8,128)} %get-tuple-element.43), calls=%async_computation.3 | async-start | bytes 786432 | tf_op jit(solution)/shard_map/all_to_all | solution.py:472
  145.9 2.3 %shard_map.98 = (bf16[144,384]{1,0:T(8,128)(2,1)S(1)}, bf16[144,384]{1,0:T(8,128)(2,1)S(1)}, bf16[144,384]{1,0:T(8,128)(2,1)S(1)}, bf16[144,384]{1,0:T(8,128)(2,1)S(1)}, bf16[1,288,576]{2,1,0:T(8,128)(2,1)}) custom-call(s32[1]{0:T(128)} %bitcast.refs_0_, bf16[576,384]{1,0:T(8,128)(2,1)S(1)} %copy-done.5, bf16[4,144,384]{2,1,0:T(8,128)(2,1)S(1)} %copy-done.7, ...), custom_call_target="tpu_custom_call" | custom-call | flops 764411904 | bytes 4194304 | tf_op jit(solution)/shard_map/pallas_call | solution.py:55
  148.2 4.8 %collective-permute-start.10 = (bf16[144,384]{1,0:T(8,128)(2,1)S(1)}, bf16[144,384]{1,0:T(8,128)(2,1)S(1)}, u32[]{:S(2)}, u32[]{:S(2)}) collective-permute-start(bf16[144,384]{1,0:T(8,128)(2,1)S(1)} %get-tuple-element.40), channel_id=1, source_target_pairs={{0,256},{128,384},{256,0},{384,128},{1,257},{129,385},{257,1},{385... | collective-permute-start | bytes 331784 | tf_op jit(solution)/shard_map/ppermute | solution.py:476
  153.0 2.5 %collective-permute-start.11 = (bf16[144,384]{1,0:T(8,128)(2,1)S(1)}, bf16[144,384]{1,0:T(8,128)(2,1)S(1)}, u32[]{:S(2)}, u32[]{:S(2)}) collective-permute-start(bf16[144,384]{1,0:T(8,128)(2,1)S(1)} %get-tuple-element.41), channel_id=1, source_target_pairs={{0,128},{128,256},{256,384},{384,0},{1,129},{129,257},{257,385},{3... | collective-permute-start | bytes 331784 | tf_op jit(solution)/shard_map/ppermute | solution.py:476
  155.5 4.6 %collective-permute-start.12 = (bf16[144,384]{1,0:T(8,128)(2,1)S(1)}, bf16[144,384]{1,0:T(8,128)(2,1)S(1)}, u32[]{:S(2)}, u32[]{:S(2)}) collective-permute-start(bf16[144,384]{1,0:T(8,128)(2,1)S(1)} %get-tuple-element.42), channel_id=1, source_target_pairs={{0,384},{128,0},{256,128},{384,256},{1,385},{129,1},{257,129},{385... | collective-permute-start | bytes 331784 | tf_op jit(solution)/shard_map/ppermute | solution.py:476
  162.4 5.4 %all-to-all-done.3.refs_0_ = f32[16,48,128]{2,1,0:T(8,128)S(1)} async-done(((f32[16,48,128]{2,1,0:T(8,128)}), f32[16,48,128]{2,1,0:T(8,128)S(1)}, u32[]{:S(2)}, u32[]{:S(2)}) %all-to-all-start.3) | async-done | bytes 393248 | tf_op jit(solution)/shard_map/all_to_all | solution.py:472
  167.9 18.5 %all_to_all.30.refs_5_.refs_0_ = f32[4,16,48,128]{3,2,1,0:T(8,128)S(1)} all-to-all(f32[4,16,48,128]{3,2,1,0:T(8,128)S(1)} %shard_map.100), channel_id=1, replica_groups=mesh['x'=4,'z'=16,'y'=4,'c'=2] {'x'}, dimensions={0} | all-to-all | bytes 3145728 | tf_op jit(solution)/shard_map/all_to_all | solution.py:472
  187.5 12.3 %all-to-all-start.5 = ((bf16[16,88,128]{2,1,0:T(8,128)(2,1)}), bf16[16,88,128]{2,1,0:T(8,128)(2,1)S(1)}, u32[]{:S(2)}, u32[]{:S(2)}) async-start(bf16[16,88,128]{2,1,0:T(8,128)(2,1)} %shard_map.101), calls=%async_computation.5 | async-start | bytes 720896 | tf_op jit(solution)/shard_map/all_to_all | solution.py:472
  200.4 20.5 %shard_map.103 = f32[1,9,576]{2,1,0:T(8,128)S(1)} custom-call(f32[4,16,48,128]{3,2,1,0:T(8,128)S(1)} %all_to_all.30.refs_5_.refs_0_, f32[16,640]{1,0:T(8,128)S(1)} %get-tuple-element.48.refs_1_), custom_call_target="tpu_custom_call" | custom-call | flops 2831155200 | bytes 1048576 | tf_op jit(solution)/shard_map/pallas_call | solution.py:55
  221.6 1.6 shard_map.102
  (44 shorter events, 14.6 us)
Async XLA Ops:
  0.6 1.1 copy-start
  1.7 1.1 copy-start.2
  2.8 32.8 %copy-start.9 = (f32[1,9,576]{2,0,1:T(1,128)S(1)}, f32[1,9,576]{2,0,1:T(1,128)}, u32[]{:S(2)}) copy-start(f32[1,9,576]{2,0,1:T(1,128)} %param.9) | copy-start | bytes 62212
  7.2 50.2 %all-to-all-start = ((bf16[16,168,128]{2,1,0:T(8,128)(2,1)}), bf16[16,168,128]{2,1,0:T(8,128)(2,1)S(1)}, u32[]{:S(2)}, u32[]{:S(2)}) async-start(bf16[16,168,128]{2,1,0:T(8,128)(2,1)} %get-tuple-element.27), calls=%async_computation | async-start | bytes 1376256 | tf_op jit(solution)/shard_map/all_to_all | solution.py:472
  22.4 3.1 %collective-permute-start = (f32[8,128]{1,0:T(8,128)S(1)}, f32[8,128]{1,0:T(8,128)S(1)}, u32[]{:S(2)}, u32[]{:S(2)}) collective-permute-start(f32[8,128]{1,0:T(8,128)S(1)} %get-tuple-element.28), channel_id=1, source_target_pairs={{0,1},{1,0},{2,3},{3,2},{4,5},{5,4},{6,7},{7,6},{8,9},{9,8},{10,11... | collective-permute-start | bytes 12296 | tf_op jit(solution)/shard_map/ppermute | solution.py:476
  25.5 10.1 %collective-permute-start.1 = (f32[8,128]{1,0:T(8,128)S(1)}, f32[8,128]{1,0:T(8,128)S(1)}, u32[]{:S(2)}, u32[]{:S(2)}) collective-permute-start(f32[8,128]{1,0:T(8,128)S(1)} %add.3.refs_2_), channel_id=1, source_target_pairs={{0,4},{2,6},{4,0},{6,2},{1,5},{3,7},{5,1},{7,3},{8,12},{10,14},{12... | collective-permute-start | bytes 12296 | tf_op jit(solution)/shard_map/ppermute | solution.py:476
  29.7 5.9 %collective-permute-start.2 = (f32[8,128]{1,0:T(8,128)S(1)}, f32[8,128]{1,0:T(8,128)S(1)}, u32[]{:S(2)}, u32[]{:S(2)}) collective-permute-start(f32[8,128]{1,0:T(8,128)S(1)} %add.3.refs_2_), channel_id=1, source_target_pairs={{0,2},{2,4},{4,6},{6,0},{1,3},{3,5},{5,7},{7,1},{8,10},{10,12},{12... | collective-permute-start | bytes 12296 | tf_op jit(solution)/shard_map/ppermute | solution.py:476
  31.6 5.5 %collective-permute-start.3 = (f32[8,128]{1,0:T(8,128)S(1)}, f32[8,128]{1,0:T(8,128)S(1)}, u32[]{:S(2)}, u32[]{:S(2)}) collective-permute-start(f32[8,128]{1,0:T(8,128)S(1)} %add.3.refs_2_), channel_id=1, source_target_pairs={{0,6},{2,0},{4,2},{6,4},{1,7},{3,1},{5,3},{7,5},{8,14},{10,8},{12,... | collective-permute-start | bytes 12296 | tf_op jit(solution)/shard_map/ppermute | solution.py:476
  58.2 37.5 %all-to-all-start.1 = ((f32[16,48,128]{2,1,0:T(8,128)}), f32[16,48,128]{2,1,0:T(8,128)S(1)}, u32[]{:S(2)}, u32[]{:S(2)}) async-start(f32[16,48,128]{2,1,0:T(8,128)} %shard_map.95), calls=%async_computation.1 | async-start | bytes 786432 | tf_op jit(solution)/shard_map/all_to_all | solution.py:472
  65.6 53.7 %copy-start.10 = (f32[1,9,576]{2,0,1:T(1,128)S(1)}, f32[1,9,576]{2,0,1:T(1,128)}, u32[]{:S(2)}) copy-start(f32[1,9,576]{2,0,1:T(1,128)} %param.8) | copy-start | bytes 62212
  66.3 17.3 %collective-permute-start.4 = (bf16[208,1152]{1,0:T(8,128)(2,1)S(1)}, bf16[208,1152]{1,0:T(8,128)(2,1)S(1)}, u32[]{:S(2)}, u32[]{:S(2)}) collective-permute-start(bf16[208,1152]{1,0:T(8,128)(2,1)S(1)} %get-tuple-element.30), channel_id=1, source_target_pairs={{0,256},{128,384},{256,0},{384,128},{1,257},{129,385},{257,1},{385... | collective-permute-start | bytes 1437704 | tf_op jit(solution)/shard_map/ppermute | solution.py:476
  71.2 21.3 %collective-permute-start.5 = (bf16[208,1152]{1,0:T(8,128)(2,1)S(1)}, bf16[208,1152]{1,0:T(8,128)(2,1)S(1)}, u32[]{:S(2)}, u32[]{:S(2)}) collective-permute-start(bf16[208,1152]{1,0:T(8,128)(2,1)S(1)} %get-tuple-element.31), channel_id=1, source_target_pairs={{0,128},{128,256},{256,384},{384,0},{1,129},{129,257},{257,385},{3... | collective-permute-start | bytes 1437704 | tf_op jit(solution)/shard_map/ppermute | solution.py:476
  73.7 18.9 %collective-permute-start.6 = (bf16[208,1152]{1,0:T(8,128)(2,1)S(1)}, bf16[208,1152]{1,0:T(8,128)(2,1)S(1)}, u32[]{:S(2)}, u32[]{:S(2)}) collective-permute-start(bf16[208,1152]{1,0:T(8,128)(2,1)S(1)} %get-tuple-element.32), channel_id=1, source_target_pairs={{0,384},{128,0},{256,128},{384,256},{1,385},{129,1},{257,129},{385... | collective-permute-start | bytes 1437704 | tf_op jit(solution)/shard_map/ppermute | solution.py:476
  94.2 0.8 copy-start.4
  95.0 0.8 copy-start.6
  95.7 35.6 %all-to-all-start.2 = ((f32[16,48,128]{2,1,0:T(8,128)}), f32[16,48,128]{2,1,0:T(8,128)S(1)}, u32[]{:S(2)}, u32[]{:S(2)}) async-start(f32[16,48,128]{2,1,0:T(8,128)} %get-tuple-element.36), calls=%async_computation.2 | async-start | bytes 786432 | tf_op jit(solution)/shard_map/all_to_all | solution.py:472
  107.5 15.5 %collective-permute-start.7 = (f32[16,48,128]{2,1,0:T(8,128)S(1)}, f32[16,48,128]{2,1,0:T(8,128)S(1)}, u32[]{:S(2)}, u32[]{:S(2)}) collective-permute-start(f32[16,48,128]{2,1,0:T(8,128)S(1)} %all-to-all-done.1.refs_1_), channel_id=1, source_target_pairs={{0,256},{128,384},{256,0},{384,128},{1,257},{129,385},{257,1},{385... | collective-permute-start | bytes 1179656 | tf_op jit(solution)/shard_map/ppermute | solution.py:476
  112.3 17.6 %collective-permute-start.8 = (f32[16,48,128]{2,1,0:T(8,128)S(1)}, f32[16,48,128]{2,1,0:T(8,128)S(1)}, u32[]{:S(2)}, u32[]{:S(2)}) collective-permute-start(f32[16,48,128]{2,1,0:T(8,128)S(1)} %all-to-all-done.1.refs_1_), channel_id=1, source_target_pairs={{0,128},{128,256},{256,384},{384,0},{1,129},{129,257},{257,385},{3... | collective-permute-start | bytes 1179656 | tf_op jit(solution)/shard_map/ppermute | solution.py:476
  114.8 15.2 %collective-permute-start.9 = (f32[16,48,128]{2,1,0:T(8,128)S(1)}, f32[16,48,128]{2,1,0:T(8,128)S(1)}, u32[]{:S(2)}, u32[]{:S(2)}) collective-permute-start(f32[16,48,128]{2,1,0:T(8,128)S(1)} %all-to-all-done.1.refs_1_), channel_id=1, source_target_pairs={{0,384},{128,0},{256,128},{384,256},{1,385},{129,1},{257,129},{385... | collective-permute-start | bytes 1179656 | tf_op jit(solution)/shard_map/ppermute | solution.py:476
  130.4 13.4 %copy-start.5 = (bf16[576,384]{1,0:T(8,128)(2,1)S(1)}, bf16[576,384]{1,0:T(8,128)(2,1)}, u32[]{:S(2)}) copy-start(bf16[576,384]{1,0:T(8,128)(2,1)} %copy-done.4) | copy-start | bytes 1327108
  132.9 34.8 %all-to-all-start.3 = ((f32[16,48,128]{2,1,0:T(8,128)}), f32[16,48,128]{2,1,0:T(8,128)S(1)}, u32[]{:S(2)}, u32[]{:S(2)}) async-start(f32[16,48,128]{2,1,0:T(8,128)} %get-tuple-element.43), calls=%async_computation.3 | async-start | bytes 786432 | tf_op jit(solution)/shard_map/all_to_all | solution.py:472
  143.8 16.3 %copy-start.1 = (bf16[1,9,18432]{2,1,0:T(8,128)(2,1)S(1)}, bf16[1,9,18432]{2,1,0:T(8,128)(2,1)}, u32[]{:S(2)}) copy-start(bf16[1,9,18432]{2,1,0:T(8,128)(2,1)} %refs_0_.4) | copy-start | bytes 995332
  143.8 16.3 %copy-start.3 = (bf16[1,9,18432]{2,1,0:T(8,128)(2,1)S(1)}, bf16[1,9,18432]{2,1,0:T(8,128)(2,1)}, u32[]{:S(2)}) copy-start(bf16[1,9,18432]{2,1,0:T(8,128)(2,1)} %refs_1_.4) | copy-start | bytes 995332
  143.8 1.1 copy-start.7
  144.9 1.0 copy-start.8
  148.2 13.2 %collective-permute-start.10 = (bf16[144,384]{1,0:T(8,128)(2,1)S(1)}, bf16[144,384]{1,0:T(8,128)(2,1)S(1)}, u32[]{:S(2)}, u32[]{:S(2)}) collective-permute-start(bf16[144,384]{1,0:T(8,128)(2,1)S(1)} %get-tuple-element.40), channel_id=1, source_target_pairs={{0,256},{128,384},{256,0},{384,128},{1,257},{129,385},{257,1},{385... | collective-permute-start | bytes 331784 | tf_op jit(solution)/shard_map/ppermute | solution.py:476
  153.0 8.4 %collective-permute-start.11 = (bf16[144,384]{1,0:T(8,128)(2,1)S(1)}, bf16[144,384]{1,0:T(8,128)(2,1)S(1)}, u32[]{:S(2)}, u32[]{:S(2)}) collective-permute-start(bf16[144,384]{1,0:T(8,128)(2,1)S(1)} %get-tuple-element.41), channel_id=1, source_target_pairs={{0,128},{128,256},{256,384},{384,0},{1,129},{129,257},{257,385},{3... | collective-permute-start | bytes 331784 | tf_op jit(solution)/shard_map/ppermute | solution.py:476
  155.5 6.9 %collective-permute-start.12 = (bf16[144,384]{1,0:T(8,128)(2,1)S(1)}, bf16[144,384]{1,0:T(8,128)(2,1)S(1)}, u32[]{:S(2)}, u32[]{:S(2)}) collective-permute-start(bf16[144,384]{1,0:T(8,128)(2,1)S(1)} %get-tuple-element.42), channel_id=1, source_target_pairs={{0,384},{128,0},{256,128},{384,256},{1,385},{129,1},{257,129},{385... | collective-permute-start | bytes 331784 | tf_op jit(solution)/shard_map/ppermute | solution.py:476
  187.5 34.2 %all-to-all-start.5 = ((bf16[16,88,128]{2,1,0:T(8,128)(2,1)}), bf16[16,88,128]{2,1,0:T(8,128)(2,1)S(1)}, u32[]{:S(2)}, u32[]{:S(2)}) async-start(bf16[16,88,128]{2,1,0:T(8,128)(2,1)} %shard_map.101), calls=%async_computation.5 | async-start | bytes 720896 | tf_op jit(solution)/shard_map/all_to_all | solution.py:472

commit v4 on v3

--- a/solution.py
+++ b/solution.py
@@ -401,14 +401,13 @@
             cols = ahead
 
 
-def copies_body(in_ref, out_ref):
-    for xp in range(NX):
-        out_ref[xp] = in_ref[...]
-
-
-def factor_body(r_ref, own_ref, out_ref, full, mat, result, diag):
-    for xp in range(NX):
-        unpack_square(r_ref.at[xp], full.at[XROWS * xp : XROWS * (xp + 1)])
+def copy_body(in_ref, out_ref):
+    out_ref[...] = in_ref[...]
+
+
+def factor_body(r0, r1, r2, r3, own_ref, out_ref, full, mat, result, diag):
+    for d, r in enumerate((r0, r1, r2, r3)):
+        unpack_square(r, full.at[XROWS * d : XROWS * (d + 1)])
     rows = full[...]
     across = (((1,), (1,)), ((), ()))
 
@@ -560,24 +559,27 @@
         [struct((1, ROWS, FF), BF16), struct((8, 128), F32)],
         [gradient, first_moment, clip],
     )
-    (r_copies,) = call(
-        copies_body, struct((NX, NZ, BPACK, 128), F32), [r_mid], after=[*up_parts[1:], first_done]
-    )
-    r_all = swap(r_copies, "x")
+    (r_mid,) = call(
+        copy_body,
+        struct((NZ, BPACK, 128), F32),
+        [r_mid],
+        after=[*up_parts[1:], first_done],
+    )
+    r_parts = spread(r_mid)
     (up_packed,) = call(
         pack_update_body,
         struct((NZ, PACK, 128), BF16),
         up_parts,
         [parts, rows, chunk],
         at=x,
-        after=[r_all],
+        after=r_parts[1:],
     )
     up_mid = swap(up_packed, "z")
 
     (new_basis,) = call(
         factor_body,
         struct((1, ROWS, BK), F32),
-        [r_all, own],
+        [*r_parts, own],
         [
             pltpu.VMEM((BK, WIDE), F32),
             pltpu.VMEM((WIDE + 16, WIDE), F32),

time: 224 us -> 223 us (level)
  the two profiles are of different devices: /device:TPU:8 before, /device:TPU:20 now
where the time goes in v4:
time: 223 us; the launch traced here: 222 us
  starting transfers between devices  101 us (45%)
  waiting for transfers between devices  76 us (34%)
  Pallas kernels  36.2 us (16%)
  local copies, waits for them, and re-layouts  8.07 us (4%)
    all_to_all x5, starting transfers between devices, swap(): return lax.all_to_all(v, axis, 0, 0, tiled=True)  56.9 us
    ppermute x16, waiting for transfers between devices, shift(): return lax.ppermute(v, axis, [(k, (k + d) % size) for k in range(size)])  48.4 us
    ppermute x16, starting transfers between devices, shift(): return lax.ppermute(v, axis, [(k, (k + d) % size) for k in range(size)])  43.8 us
    pallas_call x12, Pallas kernels, call(): pl.pallas_call(run, out_shape=tuple(outs), in_specs=[pl.BlockSpec(memory_...  36.2 us
    all_to_all x5, waiting for transfers between devices, swap(): return lax.all_to_all(v, axis, 0, 0, tiled=True)  27.6 us
    unnamed x26, local copies, waits for them, and re-layouts  8.07 us
  transfers between devices with their start and end apart: 21, of which 15 were waited for; matrix products, arithmetic and copies ran while one was open for 1% of the time, Pallas kernels for 12%

profile of v4, /device:TPU:20, one launch (start us, length us, event | category | flops | bytes accessed | tf_op | source)
XLA Modules:
  0.0 221.8 jit_solution(9312887587055154059)
XLA Ops:
  2.8 4.4 %shard_map.92 = (bf16[16,168,128]{2,1,0:T(8,128)(2,1)}, f32[8,128]{1,0:T(8,128)S(1)}) custom-call(bf16[1,9,18432]{2,1,0:T(8,128)(2,1)S(1)} %copy-done, bf16[1,9,18432]{2,1,0:T(8,128)(2,1)S(1)} %copy-done.2), custom_call_target="tpu_custom_call" | custom-call | bytes 1048576 | tf_op jit(solution)/shard_map/pallas_call | solution.py:55
  7.2 15.2 %all-to-all-start = ((bf16[16,168,128]{2,1,0:T(8,128)(2,1)}), bf16[16,168,128]{2,1,0:T(8,128)(2,1)S(1)}, u32[]{:S(2)}, u32[]{:S(2)}) async-start(bf16[16,168,128]{2,1,0:T(8,128)(2,1)} %get-tuple-element.27), calls=%async_computation | async-start | bytes 1376256 | tf_op jit(solution)/shard_map/all_to_all | solution.py:471
  25.5 2.2 %collective-permute-start.1 = (f32[8,128]{1,0:T(8,128)S(1)}, f32[8,128]{1,0:T(8,128)S(1)}, u32[]{:S(2)}, u32[]{:S(2)}) collective-permute-start(f32[8,128]{1,0:T(8,128)S(1)} %add.3.refs_2_), channel_id=1, source_target_pairs={{0,4},{2,6},{4,0},{6,2},{1,5},{3,7},{5,1},{7,3},{8,12},{10,14},{12... | collective-permute-start | bytes 12296 | tf_op jit(solution)/shard_map/ppermute | solution.py:475
  27.7 4.1 %collective-permute-start.2 = (f32[8,128]{1,0:T(8,128)S(1)}, f32[8,128]{1,0:T(8,128)S(1)}, u32[]{:S(2)}, u32[]{:S(2)}) collective-permute-start(f32[8,128]{1,0:T(8,128)S(1)} %add.3.refs_2_), channel_id=1, source_target_pairs={{0,2},{2,4},{4,6},{6,0},{1,3},{3,5},{5,7},{7,1},{8,10},{10,12},{12... | collective-permute-start | bytes 12296 | tf_op jit(solution)/shard_map/ppermute | solution.py:475
  31.8 2.1 collective-permute-start.3
  34.0 3.5 %collective-permute-done.3.refs_5_.refs_3_ = f32[8,128]{1,0:T(8,128)S(1)} collective-permute-done((f32[8,128]{1,0:T(8,128)S(1)}, f32[8,128]{1,0:T(8,128)S(1)}, u32[]{:S(2)}, u32[]{:S(2)}) %collective-permute-start.3) | collective-permute-done | bytes 4128 | tf_op jit(solution)/shard_map/ppermute | solution.py:475
  37.5 19.9 %all-to-all-done.refs_1_.refs_4_ = bf16[16,168,128]{2,1,0:T(8,128)(2,1)S(1)} async-done(((bf16[16,168,128]{2,1,0:T(8,128)(2,1)}), bf16[16,168,128]{2,1,0:T(8,128)(2,1)S(1)}, u32[]{:S(2)}, u32[]{:S(2)}) %all-to-all-start) | async-done | bytes 688160 | tf_op jit(solution)/shard_map/all_to_all | solution.py:471
  58.2 7.4 %all-to-all-start.1 = ((f32[16,48,128]{2,1,0:T(8,128)}), f32[16,48,128]{2,1,0:T(8,128)S(1)}, u32[]{:S(2)}, u32[]{:S(2)}) async-start(f32[16,48,128]{2,1,0:T(8,128)} %shard_map.95), calls=%async_computation.1 | async-start | bytes 786432 | tf_op jit(solution)/shard_map/all_to_all | solution.py:471
  66.3 2.4 %collective-permute-start.4 = (bf16[208,1152]{1,0:T(8,128)(2,1)S(1)}, bf16[208,1152]{1,0:T(8,128)(2,1)S(1)}, u32[]{:S(2)}, u32[]{:S(2)}) collective-permute-start(bf16[208,1152]{1,0:T(8,128)(2,1)S(1)} %get-tuple-element.30), channel_id=1, source_target_pairs={{0,256},{128,384},{256,0},{384,128},{1,257},{129,385},{257,1},{385... | collective-permute-start | bytes 1437704 | tf_op jit(solution)/shard_map/ppermute | solution.py:475
  68.7 4.0 %collective-permute-start.5 = (bf16[208,1152]{1,0:T(8,128)(2,1)S(1)}, bf16[208,1152]{1,0:T(8,128)(2,1)S(1)}, u32[]{:S(2)}, u32[]{:S(2)}) collective-permute-start(bf16[208,1152]{1,0:T(8,128)(2,1)S(1)} %get-tuple-element.31), channel_id=1, source_target_pairs={{0,128},{128,256},{256,384},{384,0},{1,129},{129,257},{257,385},{3... | collective-permute-start | bytes 1437704 | tf_op jit(solution)/shard_map/ppermute | solution.py:475
  72.7 2.0 collective-permute-start.6
  74.7 8.9 %collective-permute-done.4.refs_2_ = bf16[208,1152]{1,0:T(8,128)(2,1)S(1)} collective-permute-done((bf16[208,1152]{1,0:T(8,128)(2,1)S(1)}, bf16[208,1152]{1,0:T(8,128)(2,1)S(1)}, u32[]{:S(2)}, u32[]{:S(2)}) %collective-permute-start.4) | collective-permute-done | bytes 479264 | tf_op jit(solution)/shard_map/ppermute | solution.py:475
  83.6 8.9 %collective-permute-done.5.refs_3_ = bf16[208,1152]{1,0:T(8,128)(2,1)S(1)} collective-permute-done((bf16[208,1152]{1,0:T(8,128)(2,1)S(1)}, bf16[208,1152]{1,0:T(8,128)(2,1)S(1)}, u32[]{:S(2)}, u32[]{:S(2)}) %collective-permute-start.5) | collective-permute-done | bytes 479264 | tf_op jit(solution)/shard_map/ppermute | solution.py:475
  95.6 11.7 %all-to-all-start.2 = ((f32[16,48,128]{2,1,0:T(8,128)}), f32[16,48,128]{2,1,0:T(8,128)S(1)}, u32[]{:S(2)}, u32[]{:S(2)}) async-start(f32[16,48,128]{2,1,0:T(8,128)} %get-tuple-element.36), calls=%async_computation.2 | async-start | bytes 786432 | tf_op jit(solution)/shard_map/all_to_all | solution.py:471
  107.3 2.5 %collective-permute-start.7 = (f32[16,48,128]{2,1,0:T(8,128)S(1)}, f32[16,48,128]{2,1,0:T(8,128)S(1)}, u32[]{:S(2)}, u32[]{:S(2)}) collective-permute-start(f32[16,48,128]{2,1,0:T(8,128)S(1)} %all-to-all-done.1.refs_1_), channel_id=1, source_target_pairs={{0,256},{128,384},{256,0},{384,128},{1,257},{129,385},{257,1},{385... | collective-permute-start | bytes 1179656 | tf_op jit(solution)/shard_map/ppermute | solution.py:475
  109.8 4.0 %collective-permute-start.8 = (f32[16,48,128]{2,1,0:T(8,128)S(1)}, f32[16,48,128]{2,1,0:T(8,128)S(1)}, u32[]{:S(2)}, u32[]{:S(2)}) collective-permute-start(f32[16,48,128]{2,1,0:T(8,128)S(1)} %all-to-all-done.1.refs_1_), channel_id=1, source_target_pairs={{0,128},{128,256},{256,384},{384,0},{1,129},{129,257},{257,385},{3... | collective-permute-start | bytes 1179656 | tf_op jit(solution)/shard_map/ppermute | solution.py:475
  113.8 1.9 collective-permute-start.9
  115.8 7.0 %collective-permute-done.7.refs_2_ = f32[16,48,128]{2,1,0:T(8,128)S(1)} collective-permute-done((f32[16,48,128]{2,1,0:T(8,128)S(1)}, f32[16,48,128]{2,1,0:T(8,128)S(1)}, u32[]{:S(2)}, u32[]{:S(2)}) %collective-permute-start.7) | collective-permute-done | bytes 393248 | tf_op jit(solution)/shard_map/ppermute | solution.py:475
  122.8 7.1 %collective-permute-done.8.refs_3_ = f32[16,48,128]{2,1,0:T(8,128)S(1)} collective-permute-done((f32[16,48,128]{2,1,0:T(8,128)S(1)}, f32[16,48,128]{2,1,0:T(8,128)S(1)}, u32[]{:S(2)}, u32[]{:S(2)}) %collective-permute-start.8) | collective-permute-done | bytes 393248 | tf_op jit(solution)/shard_map/ppermute | solution.py:475
  133.1 10.6 %all-to-all-start.3 = ((f32[16,48,128]{2,1,0:T(8,128)}), f32[16,48,128]{2,1,0:T(8,128)S(1)}, u32[]{:S(2)}, u32[]{:S(2)}) async-start(f32[16,48,128]{2,1,0:T(8,128)} %get-tuple-element.43), calls=%async_computation.3 | async-start | bytes 786432 | tf_op jit(solution)/shard_map/all_to_all | solution.py:471
  146.8 2.3 %shard_map.98 = (bf16[144,384]{1,0:T(8,128)(2,1)S(1)}, bf16[144,384]{1,0:T(8,128)(2,1)S(1)}, bf16[144,384]{1,0:T(8,128)(2,1)S(1)}, bf16[144,384]{1,0:T(8,128)(2,1)S(1)}, bf16[1,288,576]{2,1,0:T(8,128)(2,1)}) custom-call(s32[1]{0:T(128)} %bitcast.refs_0_, bf16[576,384]{1,0:T(8,128)(2,1)S(1)} %copy-done.5, bf16[4,144,384]{2,1,0:T(8,128)(2,1)S(1)} %copy-done.7, ...), custom_call_target="tpu_custom_call" | custom-call | flops 764411904 | bytes 4194304 | tf_op jit(solution)/shard_map/pallas_call | solution.py:55
  149.0 2.5 %collective-permute-start.10 = (bf16[144,384]{1,0:T(8,128)(2,1)S(1)}, bf16[144,384]{1,0:T(8,128)(2,1)S(1)}, u32[]{:S(2)}, u32[]{:S(2)}) collective-permute-start(bf16[144,384]{1,0:T(8,128)(2,1)S(1)} %get-tuple-element.40), channel_id=1, source_target_pairs={{0,256},{128,384},{256,0},{384,128},{1,257},{129,385},{257,1},{385... | collective-permute-start | bytes 331784 | tf_op jit(solution)/shard_map/ppermute | solution.py:475
  151.5 4.0 %collective-permute-start.11 = (bf16[144,384]{1,0:T(8,128)(2,1)S(1)}, bf16[144,384]{1,0:T(8,128)(2,1)S(1)}, u32[]{:S(2)}, u32[]{:S(2)}) collective-permute-start(bf16[144,384]{1,0:T(8,128)(2,1)S(1)} %get-tuple-element.41), channel_id=1, source_target_pairs={{0,128},{128,256},{256,384},{384,0},{1,129},{129,257},{257,385},{3... | collective-permute-start | bytes 331784 | tf_op jit(solution)/shard_map/ppermute | solution.py:475
  155.5 1.9 collective-permute-start.12
  159.5 2.7 %collective-permute-done.12.refs_3_.refs_4_ = bf16[144,384]{1,0:T(8,128)(2,1)S(1)} collective-permute-done((bf16[144,384]{1,0:T(8,128)(2,1)S(1)}, bf16[144,384]{1,0:T(8,128)(2,1)S(1)}, u32[]{:S(2)}, u32[]{:S(2)}) %collective-permute-start.12) | collective-permute-done | bytes 110624 | tf_op jit(solution)/shard_map/ppermute | solution.py:475
  162.2 5.6 %all-to-all-done.3.refs_0_ = f32[16,48,128]{2,1,0:T(8,128)S(1)} async-done(((f32[16,48,128]{2,1,0:T(8,128)}), f32[16,48,128]{2,1,0:T(8,128)S(1)}, u32[]{:S(2)}, u32[]{:S(2)}) %all-to-all-start.3) | async-done | bytes 393248 | tf_op jit(solution)/shard_map/all_to_all | solution.py:471
  167.8 2.3 %collective-permute-start.13 = (f32[16,48,128]{2,1,0:T(8,128)S(1)}, f32[16,48,128]{2,1,0:T(8,128)S(1)}, u32[]{:S(2)}, u32[]{:S(2)}) collective-permute-start(f32[16,48,128]{2,1,0:T(8,128)S(1)} %shard_map.100.refs_0_), channel_id=1, source_target_pairs={{0,256},{128,384},{256,0},{384,128},{1,257},{129,385},{257,1},{385... | collective-permute-start | bytes 1179656 | tf_op jit(solution)/shard_map/ppermute | solution.py:475
  170.1 4.0 %collective-permute-start.14 = (f32[16,48,128]{2,1,0:T(8,128)S(1)}, f32[16,48,128]{2,1,0:T(8,128)S(1)}, u32[]{:S(2)}, u32[]{:S(2)}) collective-permute-start(f32[16,48,128]{2,1,0:T(8,128)S(1)} %shard_map.100.refs_0_), channel_id=1, source_target_pairs={{0,128},{128,256},{256,384},{384,0},{1,129},{129,257},{257,385},{3... | collective-permute-start | bytes 1179656 | tf_op jit(solution)/shard_map/ppermute | solution.py:475
  176.1 3.7 %collective-permute-done.13.refs_5_.refs_1_ = f32[16,48,128]{2,1,0:T(8,128)S(1)} collective-permute-done((f32[16,48,128]{2,1,0:T(8,128)S(1)}, f32[16,48,128]{2,1,0:T(8,128)S(1)}, u32[]{:S(2)}, u32[]{:S(2)}) %collective-permute-start.13) | collective-permute-done | bytes 393248 | tf_op jit(solution)/shard_map/ppermute | solution.py:475
  179.7 4.1 %collective-permute-done.14.refs_6_.refs_2_ = f32[16,48,128]{2,1,0:T(8,128)S(1)} collective-permute-done((f32[16,48,128]{2,1,0:T(8,128)S(1)}, f32[16,48,128]{2,1,0:T(8,128)S(1)}, u32[]{:S(2)}, u32[]{:S(2)}) %collective-permute-start.14) | collective-permute-done | bytes 393248 | tf_op jit(solution)/shard_map/ppermute | solution.py:475
  185.6 11.9 %all-to-all-start.4 = ((bf16[16,88,128]{2,1,0:T(8,128)(2,1)}), bf16[16,88,128]{2,1,0:T(8,128)(2,1)S(1)}, u32[]{:S(2)}, u32[]{:S(2)}) async-start(bf16[16,88,128]{2,1,0:T(8,128)(2,1)} %shard_map.101), calls=%async_computation.4 | async-start | bytes 720896 | tf_op jit(solution)/shard_map/all_to_all | solution.py:471
  198.1 20.6 %shard_map.103 = f32[1,9,576]{2,1,0:T(8,128)S(1)} custom-call(f32[16,48,128]{2,1,0:T(8,128)S(1)} %shard_map.100.refs_0_, f32[16,48,128]{2,1,0:T(8,128)S(1)} %collective-permute-done.13.refs_5_.refs_1_, f32[16,48,128]{2,1,0:T(8,128)S(1)} %collective-permute-done.14.refs_6_.refs_2_, f32[16,48,128]{2,1,0:T(8,128)S(1)} %collective-permute-done.15.refs_7_.refs_3_, ...), custom_call_target="tpu_custom_call" | custom-call | flops 2831155200 | bytes 1048576 | tf_op jit(solution)/shard_map/pallas_call | solution.py:55
  (49 shorter events, 25.4 us)
Async XLA Ops:
  0.6 1.1 copy-start
  1.7 1.1 copy-start.2
  2.8 31.2 %copy-start.9 = (f32[1,9,576]{2,0,1:T(1,128)S(1)}, f32[1,9,576]{2,0,1:T(1,128)}, u32[]{:S(2)}) copy-start(f32[1,9,576]{2,0,1:T(1,128)} %param.9) | copy-start | bytes 62212
  7.2 50.2 %all-to-all-start = ((bf16[16,168,128]{2,1,0:T(8,128)(2,1)}), bf16[16,168,128]{2,1,0:T(8,128)(2,1)S(1)}, u32[]{:S(2)}, u32[]{:S(2)}) async-start(bf16[16,168,128]{2,1,0:T(8,128)(2,1)} %get-tuple-element.27), calls=%async_computation | async-start | bytes 1376256 | tf_op jit(solution)/shard_map/all_to_all | solution.py:471
  22.4 3.1 %collective-permute-start = (f32[8,128]{1,0:T(8,128)S(1)}, f32[8,128]{1,0:T(8,128)S(1)}, u32[]{:S(2)}, u32[]{:S(2)}) collective-permute-start(f32[8,128]{1,0:T(8,128)S(1)} %get-tuple-element.28), channel_id=1, source_target_pairs={{0,1},{1,0},{2,3},{3,2},{4,5},{5,4},{6,7},{7,6},{8,9},{9,8},{10,11... | collective-permute-start | bytes 12296 | tf_op jit(solution)/shard_map/ppermute | solution.py:475
  25.5 8.5 %collective-permute-start.1 = (f32[8,128]{1,0:T(8,128)S(1)}, f32[8,128]{1,0:T(8,128)S(1)}, u32[]{:S(2)}, u32[]{:S(2)}) collective-permute-start(f32[8,128]{1,0:T(8,128)S(1)} %add.3.refs_2_), channel_id=1, source_target_pairs={{0,4},{2,6},{4,0},{6,2},{1,5},{3,7},{5,1},{7,3},{8,12},{10,14},{12... | collective-permute-start | bytes 12296 | tf_op jit(solution)/shard_map/ppermute | solution.py:475
  27.7 6.3 %collective-permute-start.2 = (f32[8,128]{1,0:T(8,128)S(1)}, f32[8,128]{1,0:T(8,128)S(1)}, u32[]{:S(2)}, u32[]{:S(2)}) collective-permute-start(f32[8,128]{1,0:T(8,128)S(1)} %add.3.refs_2_), channel_id=1, source_target_pairs={{0,2},{2,4},{4,6},{6,0},{1,3},{3,5},{5,7},{7,1},{8,10},{10,12},{12... | collective-permute-start | bytes 12296 | tf_op jit(solution)/shard_map/ppermute | solution.py:475
  31.8 5.7 %collective-permute-start.3 = (f32[8,128]{1,0:T(8,128)S(1)}, f32[8,128]{1,0:T(8,128)S(1)}, u32[]{:S(2)}, u32[]{:S(2)}) collective-permute-start(f32[8,128]{1,0:T(8,128)S(1)} %add.3.refs_2_), channel_id=1, source_target_pairs={{0,6},{2,0},{4,2},{6,4},{1,7},{3,1},{5,3},{7,5},{8,14},{10,8},{12,... | collective-permute-start | bytes 12296 | tf_op jit(solution)/shard_map/ppermute | solution.py:475
  58.2 37.4 %all-to-all-start.1 = ((f32[16,48,128]{2,1,0:T(8,128)}), f32[16,48,128]{2,1,0:T(8,128)S(1)}, u32[]{:S(2)}, u32[]{:S(2)}) async-start(f32[16,48,128]{2,1,0:T(8,128)} %shard_map.95), calls=%async_computation.1 | async-start | bytes 786432 | tf_op jit(solution)/shard_map/all_to_all | solution.py:471
  66.3 49.5 %copy-start.10 = (f32[1,9,576]{2,0,1:T(1,128)S(1)}, f32[1,9,576]{2,0,1:T(1,128)}, u32[]{:S(2)}) copy-start(f32[1,9,576]{2,0,1:T(1,128)} %param.8) | copy-start | bytes 62212
  66.3 17.3 %collective-permute-start.4 = (bf16[208,1152]{1,0:T(8,128)(2,1)S(1)}, bf16[208,1152]{1,0:T(8,128)(2,1)S(1)}, u32[]{:S(2)}, u32[]{:S(2)}) collective-permute-start(bf16[208,1152]{1,0:T(8,128)(2,1)S(1)} %get-tuple-element.30), channel_id=1, source_target_pairs={{0,256},{128,384},{256,0},{384,128},{1,257},{129,385},{257,1},{385... | collective-permute-start | bytes 1437704 | tf_op jit(solution)/shard_map/ppermute | solution.py:475
  68.7 23.8 %collective-permute-start.5 = (bf16[208,1152]{1,0:T(8,128)(2,1)S(1)}, bf16[208,1152]{1,0:T(8,128)(2,1)S(1)}, u32[]{:S(2)}, u32[]{:S(2)}) collective-permute-start(bf16[208,1152]{1,0:T(8,128)(2,1)S(1)} %get-tuple-element.31), channel_id=1, source_target_pairs={{0,128},{128,256},{256,384},{384,0},{1,129},{129,257},{257,385},{3... | collective-permute-start | bytes 1437704 | tf_op jit(solution)/shard_map/ppermute | solution.py:475
  72.7 19.8 %collective-permute-start.6 = (bf16[208,1152]{1,0:T(8,128)(2,1)S(1)}, bf16[208,1152]{1,0:T(8,128)(2,1)S(1)}, u32[]{:S(2)}, u32[]{:S(2)}) collective-permute-start(bf16[208,1152]{1,0:T(8,128)(2,1)S(1)} %get-tuple-element.32), channel_id=1, source_target_pairs={{0,384},{128,0},{256,128},{384,256},{1,385},{129,1},{257,129},{385... | collective-permute-start | bytes 1437704 | tf_op jit(solution)/shard_map/ppermute | solution.py:475
  94.0 0.8 copy-start.4
  94.8 0.8 copy-start.6
  95.6 35.9 %all-to-all-start.2 = ((f32[16,48,128]{2,1,0:T(8,128)}), f32[16,48,128]{2,1,0:T(8,128)S(1)}, u32[]{:S(2)}, u32[]{:S(2)}) async-start(f32[16,48,128]{2,1,0:T(8,128)} %get-tuple-element.36), calls=%async_computation.2 | async-start | bytes 786432 | tf_op jit(solution)/shard_map/all_to_all | solution.py:471
  107.3 15.5 %collective-permute-start.7 = (f32[16,48,128]{2,1,0:T(8,128)S(1)}, f32[16,48,128]{2,1,0:T(8,128)S(1)}, u32[]{:S(2)}, u32[]{:S(2)}) collective-permute-start(f32[16,48,128]{2,1,0:T(8,128)S(1)} %all-to-all-done.1.refs_1_), channel_id=1, source_target_pairs={{0,256},{128,384},{256,0},{384,128},{1,257},{129,385},{257,1},{385... | collective-permute-start | bytes 1179656 | tf_op jit(solution)/shard_map/ppermute | solution.py:475
  109.8 20.0 %collective-permute-start.8 = (f32[16,48,128]{2,1,0:T(8,128)S(1)}, f32[16,48,128]{2,1,0:T(8,128)S(1)}, u32[]{:S(2)}, u32[]{:S(2)}) collective-permute-start(f32[16,48,128]{2,1,0:T(8,128)S(1)} %all-to-all-done.1.refs_1_), channel_id=1, source_target_pairs={{0,128},{128,256},{256,384},{384,0},{1,129},{129,257},{257,385},{3... | collective-permute-start | bytes 1179656 | tf_op jit(solution)/shard_map/ppermute | solution.py:475
  113.8 16.1 %collective-permute-start.9 = (f32[16,48,128]{2,1,0:T(8,128)S(1)}, f32[16,48,128]{2,1,0:T(8,128)S(1)}, u32[]{:S(2)}, u32[]{:S(2)}) collective-permute-start(f32[16,48,128]{2,1,0:T(8,128)S(1)} %all-to-all-done.1.refs_1_), channel_id=1, source_target_pairs={{0,384},{128,0},{256,128},{384,256},{1,385},{129,1},{257,129},{385... | collective-permute-start | bytes 1179656 | tf_op jit(solution)/shard_map/ppermute | solution.py:475
  133.1 34.7 %all-to-all-start.3 = ((f32[16,48,128]{2,1,0:T(8,128)}), f32[16,48,128]{2,1,0:T(8,128)S(1)}, u32[]{:S(2)}, u32[]{:S(2)}) async-start(f32[16,48,128]{2,1,0:T(8,128)} %get-tuple-element.43), calls=%async_computation.3 | async-start | bytes 786432 | tf_op jit(solution)/shard_map/all_to_all | solution.py:471
  143.6 13.8 %copy-start.1 = (bf16[1,9,18432]{2,1,0:T(8,128)(2,1)S(1)}, bf16[1,9,18432]{2,1,0:T(8,128)(2,1)}, u32[]{:S(2)}) copy-start(bf16[1,9,18432]{2,1,0:T(8,128)(2,1)} %refs_0_.4) | copy-start | bytes 995332
  143.6 13.8 %copy-start.3 = (bf16[1,9,18432]{2,1,0:T(8,128)(2,1)S(1)}, bf16[1,9,18432]{2,1,0:T(8,128)(2,1)}, u32[]{:S(2)}) copy-start(bf16[1,9,18432]{2,1,0:T(8,128)(2,1)} %refs_1_.4) | copy-start | bytes 995332
  143.7 1.1 copy-start.5
  144.8 1.0 copy-start.7
  145.8 1.0 copy-start.8
  149.0 9.7 %collective-permute-start.10 = (bf16[144,384]{1,0:T(8,128)(2,1)S(1)}, bf16[144,384]{1,0:T(8,128)(2,1)S(1)}, u32[]{:S(2)}, u32[]{:S(2)}) collective-permute-start(bf16[144,384]{1,0:T(8,128)(2,1)S(1)} %get-tuple-element.40), channel_id=1, source_target_pairs={{0,256},{128,384},{256,0},{384,128},{1,257},{129,385},{257,1},{385... | collective-permute-start | bytes 331784 | tf_op jit(solution)/shard_map/ppermute | solution.py:475
  151.5 8.0 %collective-permute-start.11 = (bf16[144,384]{1,0:T(8,128)(2,1)S(1)}, bf16[144,384]{1,0:T(8,128)(2,1)S(1)}, u32[]{:S(2)}, u32[]{:S(2)}) collective-permute-start(bf16[144,384]{1,0:T(8,128)(2,1)S(1)} %get-tuple-element.41), channel_id=1, source_target_pairs={{0,128},{128,256},{256,384},{384,0},{1,129},{129,257},{257,385},{3... | collective-permute-start | bytes 331784 | tf_op jit(solution)/shard_map/ppermute | solution.py:475
  155.5 6.7 %collective-permute-start.12 = (bf16[144,384]{1,0:T(8,128)(2,1)S(1)}, bf16[144,384]{1,0:T(8,128)(2,1)S(1)}, u32[]{:S(2)}, u32[]{:S(2)}) collective-permute-start(bf16[144,384]{1,0:T(8,128)(2,1)S(1)} %get-tuple-element.42), channel_id=1, source_target_pairs={{0,384},{128,0},{256,128},{384,256},{1,385},{129,1},{257,129},{385... | collective-permute-start | bytes 331784 | tf_op jit(solution)/shard_map/ppermute | solution.py:475
  167.8 11.9 %collective-permute-start.13 = (f32[16,48,128]{2,1,0:T(8,128)S(1)}, f32[16,48,128]{2,1,0:T(8,128)S(1)}, u32[]{:S(2)}, u32[]{:S(2)}) collective-permute-start(f32[16,48,128]{2,1,0:T(8,128)S(1)} %shard_map.100.refs_0_), channel_id=1, source_target_pairs={{0,256},{128,384},{256,0},{384,128},{1,257},{129,385},{257,1},{385... | collective-permute-start | bytes 1179656 | tf_op jit(solution)/shard_map/ppermute | solution.py:475
  170.1 13.7 %collective-permute-start.14 = (f32[16,48,128]{2,1,0:T(8,128)S(1)}, f32[16,48,128]{2,1,0:T(8,128)S(1)}, u32[]{:S(2)}, u32[]{:S(2)}) collective-permute-start(f32[16,48,128]{2,1,0:T(8,128)S(1)} %shard_map.100.refs_0_), channel_id=1, source_target_pairs={{0,128},{128,256},{256,384},{384,0},{1,129},{129,257},{257,385},{3... | collective-permute-start | bytes 1179656 | tf_op jit(solution)/shard_map/ppermute | solution.py:475
  174.1 10.4 %collective-permute-start.15 = (f32[16,48,128]{2,1,0:T(8,128)S(1)}, f32[16,48,128]{2,1,0:T(8,128)S(1)}, u32[]{:S(2)}, u32[]{:S(2)}) collective-permute-start(f32[16,48,128]{2,1,0:T(8,128)S(1)} %shard_map.100.refs_0_), channel_id=1, source_target_pairs={{0,384},{128,0},{256,128},{384,256},{1,385},{129,1},{257,129},{385... | collective-permute-start | bytes 1179656 | tf_op jit(solution)/shard_map/ppermute | solution.py:475
  185.6 34.7 %all-to-all-start.4 = ((bf16[16,88,128]{2,1,0:T(8,128)(2,1)}), bf16[16,88,128]{2,1,0:T(8,128)(2,1)S(1)}, u32[]{:S(2)}, u32[]{:S(2)}) async-start(bf16[16,88,128]{2,1,0:T(8,128)(2,1)} %shard_map.101), calls=%async_computation.4 | async-start | bytes 720896 | tf_op jit(solution)/shard_map/all_to_all | solution.py:471

commit v5 on v4

--- a/solution.py
+++ b/solution.py
@@ -68,7 +68,7 @@
     )(*head, *args, *after, *far)
 
 
-ORDER = (0, 2, 1, 3)
+ORDER = (0, 2, 3, 1)
 
 
 def back(x, d):
@@ -187,12 +187,12 @@
             out[MOMENT:, 384 * k : 384 * k + 384] = parts[d, 48 * k : 48 * k + 48, :]
 
 
-def covariance_body(x_ref, g0, g1, g2, g3, out_ref, piece_ref, moment_ref, every, prod):
+def covariance_body(x_ref, g0, g1, g2, g3, out_ref, both_ref, every, prod):
     x = x_ref[0]
     for d, g in zip(ORDER, (g0, g1, g2, g3)):
         every[back(x, d)] = g[:XROWS]
         for k in range(3):
-            moment_ref[back(x, d), 48 * k : 48 * k + 48, :] = g[
+            both_ref[back(x, d), 48 * k : 48 * k + 48, 384:768] = g[
                 MOMENT:, 384 * k : 384 * k + 384
             ]
     sums = jnp.zeros((1, 128), F32)
@@ -212,10 +212,10 @@
                 ROWS * z : ROWS * (z + 1), 128 * t : 128 * t + 128
             ]
         out_ref[z, 45:48, :] = jnp.broadcast_to(sums, (3, 128))
-    main = every[:, :, pl.ds(pl.multiple_of(256 * x, 128), 256)].reshape(BK, 256)
+    both_ref[:, :, 0:256] = every[:, :, pl.ds(pl.multiple_of(256 * x, 128), 256)]
     rest = every[:, :, 1024:1152].reshape(BK, 128).astype(F32)
-    piece_ref[:, 0:256] = main
-    piece_ref[:, 256:384] = pltpu.roll(rest, lax.rem(128 - REST * x, 128), 1).astype(BF16)
+    rest = pltpu.roll(rest, lax.rem(128 - REST * x, 128), 1).astype(BF16)
+    both_ref[:, :, 256:384] = rest.reshape(NX, XROWS, 128)
 
 
 def unpack_square(in_ref, full):
@@ -260,16 +260,15 @@
 
 
 def rotate_body(
-    x_ref, g_ref, m_ref, basis_ref, second_ref, clip_ref, o0, o1, o2, o3, second_out, update
+    x_ref, both_ref, basis_ref, second_ref, clip_ref, o0, o1, o2, o3, second_out, update
 ):
     x = x_ref[0]
     clip = clip_ref[0:1, 0:1]
     basis = basis_ref[...]
     lead = (((0,), (0,)), ((), ()))
-    grad_rot = lax.dot_general(g_ref[...], basis, lead, preferred_element_type=F32)[:COLS]
-    moment_rot = lax.dot_general(
-        m_ref[...].reshape(BK, 384), basis, lead, preferred_element_type=F32
-    )[:COLS]
+    both = both_ref[...].reshape(BK, 768)
+    rotated = lax.dot_general(both, basis, lead, preferred_element_type=F32)
+    grad_rot, moment_rot = rotated[:COLS], rotated[384 : 384 + COLS]
     scaled = clip * grad_rot
     first = beta_first * moment_rot + (1.0 - beta_first) * scaled
     second = beta_second * second_ref[0].astype(F32) + (1.0 - beta_second) * scaled * scaled
@@ -509,12 +508,11 @@
         [pltpu.VMEM((APACK, 128), F32), rows, rows, parts],
         at=x,
     )
-    share, piece, moment = call(
+    share, both = call(
         covariance_body,
         [
             struct((NZ, BPACK, 128), F32),
-            struct((BK, 384), BF16),
-            struct((NX, XROWS, 384), BF16),
+            struct((NX, XROWS, 768), BF16),
         ],
         deal(over_x),
         [pltpu.VMEM((NX, XROWS, PIECES), BF16), pltpu.VMEM((XROWS, WIDE), F32)],
@@ -547,7 +545,7 @@
     *up_parts, new_second = call(
         rotate_body,
         [struct((XROWS, 384), BF16)] * 4 + [struct((1, COLS, BK), BF16)],
-        [piece, moment, rounded, jnp.swapaxes(second_moment, 1, 2), clip],
+        [both, rounded, jnp.swapaxes(second_moment, 1, 2), clip],
         [parts],
         at=x,
         flops=6 * BK * BK * 384,

time: 223 us -> 222 us (level)
  the two profiles are of different devices: /device:TPU:20 before, /device:TPU:14 now
where the time goes in v5:
time: 222 us; the launch traced here: 221 us
  starting transfers between devices  112 us (50%)
  waiting for transfers between devices  66.1 us (30%)
  Pallas kernels  35.7 us (16%)
  local copies, waits for them, and re-layouts  6.51 us (3%)
    all_to_all x5, starting transfers between devices, swap(): return lax.all_to_all(v, axis, 0, 0, tiled=True)  58.4 us
    ppermute x16, starting transfers between devices, shift(): return lax.ppermute(v, axis, [(k, (k + d) % size) for k in range(size)])  53.5 us
    ppermute x16, waiting for transfers between devices, shift(): return lax.ppermute(v, axis, [(k, (k + d) % size) for k in range(size)])  38.6 us
    pallas_call x12, Pallas kernels, call(): pl.pallas_call(run, out_shape=tuple(outs), in_specs=[pl.BlockSpec(memory_...  35.7 us
    all_to_all x5, waiting for transfers between devices, swap(): return lax.all_to_all(v, axis, 0, 0, tiled=True)  27.5 us
    unnamed x22, local copies, waits for them, and re-layouts  6.51 us
  transfers between devices with their start and end apart: 21, of which 13 were waited for; matrix products, arithmetic and copies ran while one was open for 1% of the time, Pallas kernels for 12%

profile of v5, /device:TPU:14, one launch (start us, length us, event | category | flops | bytes accessed | tf_op | source)
XLA Modules:
  0.0 221.2 jit_solution(15651483365804523159)
XLA Ops:
  2.8 4.4 %shard_map.92 = (bf16[16,168,128]{2,1,0:T(8,128)(2,1)}, f32[8,128]{1,0:T(8,128)S(1)}) custom-call(bf16[1,9,18432]{2,1,0:T(8,128)(2,1)S(1)} %copy-done, bf16[1,9,18432]{2,1,0:T(8,128)(2,1)S(1)} %copy-done.2), custom_call_target="tpu_custom_call" | custom-call | bytes 1048576 | tf_op jit(solution)/shard_map/pallas_call | solution.py:55
  7.2 15.2 %all-to-all-start = ((bf16[16,168,128]{2,1,0:T(8,128)(2,1)}), bf16[16,168,128]{2,1,0:T(8,128)(2,1)S(1)}, u32[]{:S(2)}, u32[]{:S(2)}) async-start(bf16[16,168,128]{2,1,0:T(8,128)(2,1)} %get-tuple-element.26), calls=%async_computation | async-start | bytes 1376256 | tf_op jit(solution)/shard_map/all_to_all | solution.py:470
  22.4 1.9 collective-permute-start
  25.5 4.2 %collective-permute-start.1 = (f32[8,128]{1,0:T(8,128)S(1)}, f32[8,128]{1,0:T(8,128)S(1)}, u32[]{:S(2)}, u32[]{:S(2)}) collective-permute-start(f32[8,128]{1,0:T(8,128)S(1)} %add.3.refs_2_), channel_id=1, source_target_pairs={{0,4},{2,6},{4,0},{6,2},{1,5},{3,7},{5,1},{7,3},{8,12},{10,14},{12... | collective-permute-start | bytes 12296 | tf_op jit(solution)/shard_map/ppermute | solution.py:474
  29.7 3.3 %collective-permute-start.2 = (f32[8,128]{1,0:T(8,128)S(1)}, f32[8,128]{1,0:T(8,128)S(1)}, u32[]{:S(2)}, u32[]{:S(2)}) collective-permute-start(f32[8,128]{1,0:T(8,128)S(1)} %add.3.refs_2_), channel_id=1, source_target_pairs={{0,6},{2,0},{4,2},{6,4},{1,7},{3,1},{5,3},{7,5},{8,14},{10,8},{12,... | collective-permute-start | bytes 12296 | tf_op jit(solution)/shard_map/ppermute | solution.py:474
  32.9 2.6 %collective-permute-start.3 = (f32[8,128]{1,0:T(8,128)S(1)}, f32[8,128]{1,0:T(8,128)S(1)}, u32[]{:S(2)}, u32[]{:S(2)}) collective-permute-start(f32[8,128]{1,0:T(8,128)S(1)} %add.3.refs_2_), channel_id=1, source_target_pairs={{0,2},{2,4},{4,6},{6,0},{1,3},{3,5},{5,7},{7,1},{8,10},{10,12},{12... | collective-permute-start | bytes 12296 | tf_op jit(solution)/shard_map/ppermute | solution.py:474
  35.6 2.9 %collective-permute-done.3.refs_5_.refs_3_ = f32[8,128]{1,0:T(8,128)S(1)} collective-permute-done((f32[8,128]{1,0:T(8,128)S(1)}, f32[8,128]{1,0:T(8,128)S(1)}, u32[]{:S(2)}, u32[]{:S(2)}) %collective-permute-start.3) | collective-permute-done | bytes 4128 | tf_op jit(solution)/shard_map/ppermute | solution.py:474
  38.4 18.9 %all-to-all-done.refs_1_.refs_4_ = bf16[16,168,128]{2,1,0:T(8,128)(2,1)S(1)} async-done(((bf16[16,168,128]{2,1,0:T(8,128)(2,1)}), bf16[16,168,128]{2,1,0:T(8,128)(2,1)S(1)}, u32[]{:S(2)}, u32[]{:S(2)}) %all-to-all-start) | async-done | bytes 688160 | tf_op jit(solution)/shard_map/all_to_all | solution.py:470
  58.2 7.4 %all-to-all-start.1 = ((f32[16,48,128]{2,1,0:T(8,128)}), f32[16,48,128]{2,1,0:T(8,128)S(1)}, u32[]{:S(2)}, u32[]{:S(2)}) async-start(f32[16,48,128]{2,1,0:T(8,128)} %shard_map.95), calls=%async_computation.1 | async-start | bytes 786432 | tf_op jit(solution)/shard_map/all_to_all | solution.py:470
  66.3 3.3 %collective-permute-start.4 = (bf16[208,1152]{1,0:T(8,128)(2,1)S(1)}, bf16[208,1152]{1,0:T(8,128)(2,1)S(1)}, u32[]{:S(2)}, u32[]{:S(2)}) collective-permute-start(bf16[208,1152]{1,0:T(8,128)(2,1)S(1)} %get-tuple-element.29), channel_id=1, source_target_pairs={{0,256},{128,384},{256,0},{384,128},{1,257},{129,385},{257,1},{385... | collective-permute-start | bytes 1437704 | tf_op jit(solution)/shard_map/ppermute | solution.py:474
  69.6 1.9 collective-permute-start.5
  71.5 5.1 %collective-permute-start.6 = (bf16[208,1152]{1,0:T(8,128)(2,1)S(1)}, bf16[208,1152]{1,0:T(8,128)(2,1)S(1)}, u32[]{:S(2)}, u32[]{:S(2)}) collective-permute-start(bf16[208,1152]{1,0:T(8,128)(2,1)S(1)} %get-tuple-element.31), channel_id=1, source_target_pairs={{0,128},{128,256},{256,384},{384,0},{1,129},{129,257},{257,385},{3... | collective-permute-start | bytes 1437704 | tf_op jit(solution)/shard_map/ppermute | solution.py:474
  76.7 6.9 %collective-permute-done.4.refs_2_ = bf16[208,1152]{1,0:T(8,128)(2,1)S(1)} collective-permute-done((bf16[208,1152]{1,0:T(8,128)(2,1)S(1)}, bf16[208,1152]{1,0:T(8,128)(2,1)S(1)}, u32[]{:S(2)}, u32[]{:S(2)}) %collective-permute-start.4) | collective-permute-done | bytes 479264 | tf_op jit(solution)/shard_map/ppermute | solution.py:474
  83.6 8.9 %collective-permute-done.5.refs_3_ = bf16[208,1152]{1,0:T(8,128)(2,1)S(1)} collective-permute-done((bf16[208,1152]{1,0:T(8,128)(2,1)S(1)}, bf16[208,1152]{1,0:T(8,128)(2,1)S(1)}, u32[]{:S(2)}, u32[]{:S(2)}) %collective-permute-start.5) | collective-permute-done | bytes 479264 | tf_op jit(solution)/shard_map/ppermute | solution.py:474
  94.0 11.7 %all-to-all-start.2 = ((f32[16,48,128]{2,1,0:T(8,128)}), f32[16,48,128]{2,1,0:T(8,128)S(1)}, u32[]{:S(2)}, u32[]{:S(2)}) async-start(f32[16,48,128]{2,1,0:T(8,128)} %get-tuple-element.34), calls=%async_computation.2 | async-start | bytes 786432 | tf_op jit(solution)/shard_map/all_to_all | solution.py:470
  105.8 3.4 %collective-permute-start.7 = (f32[16,48,128]{2,1,0:T(8,128)S(1)}, f32[16,48,128]{2,1,0:T(8,128)S(1)}, u32[]{:S(2)}, u32[]{:S(2)}) collective-permute-start(f32[16,48,128]{2,1,0:T(8,128)S(1)} %all-to-all-done.1.refs_1_), channel_id=1, source_target_pairs={{0,256},{128,384},{256,0},{384,128},{1,257},{129,385},{257,1},{385... | collective-permute-start | bytes 1179656 | tf_op jit(solution)/shard_map/ppermute | solution.py:474
  109.2 1.9 collective-permute-start.8
  111.1 5.1 %collective-permute-start.9 = (f32[16,48,128]{2,1,0:T(8,128)S(1)}, f32[16,48,128]{2,1,0:T(8,128)S(1)}, u32[]{:S(2)}, u32[]{:S(2)}) collective-permute-start(f32[16,48,128]{2,1,0:T(8,128)S(1)} %all-to-all-done.1.refs_1_), channel_id=1, source_target_pairs={{0,128},{128,256},{256,384},{384,0},{1,129},{129,257},{257,385},{3... | collective-permute-start | bytes 1179656 | tf_op jit(solution)/shard_map/ppermute | solution.py:474
  116.3 5.0 %collective-permute-done.7.refs_2_ = f32[16,48,128]{2,1,0:T(8,128)S(1)} collective-permute-done((f32[16,48,128]{2,1,0:T(8,128)S(1)}, f32[16,48,128]{2,1,0:T(8,128)S(1)}, u32[]{:S(2)}, u32[]{:S(2)}) %collective-permute-start.7) | collective-permute-done | bytes 393248 | tf_op jit(solution)/shard_map/ppermute | solution.py:474
  121.2 7.1 %collective-permute-done.8.refs_3_ = f32[16,48,128]{2,1,0:T(8,128)S(1)} collective-permute-done((f32[16,48,128]{2,1,0:T(8,128)S(1)}, f32[16,48,128]{2,1,0:T(8,128)S(1)}, u32[]{:S(2)}, u32[]{:S(2)}) %collective-permute-start.8) | collective-permute-done | bytes 393248 | tf_op jit(solution)/shard_map/ppermute | solution.py:474
  131.5 11.4 %all-to-all-start.3 = ((f32[16,48,128]{2,1,0:T(8,128)}), f32[16,48,128]{2,1,0:T(8,128)S(1)}, u32[]{:S(2)}, u32[]{:S(2)}) async-start(f32[16,48,128]{2,1,0:T(8,128)} %get-tuple-element.41), calls=%async_computation.3 | async-start | bytes 786432 | tf_op jit(solution)/shard_map/all_to_all | solution.py:470
  145.2 1.8 shard_map.98
  147.0 3.4 %collective-permute-start.10 = (bf16[144,384]{1,0:T(8,128)(2,1)S(1)}, bf16[144,384]{1,0:T(8,128)(2,1)S(1)}, u32[]{:S(2)}, u32[]{:S(2)}) collective-permute-start(bf16[144,384]{1,0:T(8,128)(2,1)S(1)} %get-tuple-element.38), channel_id=1, source_target_pairs={{0,256},{128,384},{256,0},{384,128},{1,257},{129,385},{257,1},{385... | collective-permute-start | bytes 331784 | tf_op jit(solution)/shard_map/ppermute | solution.py:474
  150.4 2.0 collective-permute-start.11
  152.4 5.1 %collective-permute-start.12 = (bf16[144,384]{1,0:T(8,128)(2,1)S(1)}, bf16[144,384]{1,0:T(8,128)(2,1)S(1)}, u32[]{:S(2)}, u32[]{:S(2)}) collective-permute-start(bf16[144,384]{1,0:T(8,128)(2,1)S(1)} %get-tuple-element.40), channel_id=1, source_target_pairs={{0,128},{128,256},{256,384},{384,0},{1,129},{129,257},{257,385},{3... | collective-permute-start | bytes 331784 | tf_op jit(solution)/shard_map/ppermute | solution.py:474
  159.8 7.4 %all-to-all-done.3.refs_0_ = f32[16,48,128]{2,1,0:T(8,128)S(1)} async-done(((f32[16,48,128]{2,1,0:T(8,128)}), f32[16,48,128]{2,1,0:T(8,128)S(1)}, u32[]{:S(2)}, u32[]{:S(2)}) %all-to-all-start.3) | async-done | bytes 393248 | tf_op jit(solution)/shard_map/all_to_all | solution.py:470
  167.2 3.2 %collective-permute-start.13 = (f32[16,48,128]{2,1,0:T(8,128)S(1)}, f32[16,48,128]{2,1,0:T(8,128)S(1)}, u32[]{:S(2)}, u32[]{:S(2)}) collective-permute-start(f32[16,48,128]{2,1,0:T(8,128)S(1)} %shard_map.100.refs_0_), channel_id=1, source_target_pairs={{0,256},{128,384},{256,0},{384,128},{1,257},{129,385},{257,1},{385... | collective-permute-start | bytes 1179656 | tf_op jit(solution)/shard_map/ppermute | solution.py:474
  170.4 1.9 collective-permute-start.14
  172.4 5.1 %collective-permute-start.15 = (f32[16,48,128]{2,1,0:T(8,128)S(1)}, f32[16,48,128]{2,1,0:T(8,128)S(1)}, u32[]{:S(2)}, u32[]{:S(2)}) collective-permute-start(f32[16,48,128]{2,1,0:T(8,128)S(1)} %shard_map.100.refs_0_), channel_id=1, source_target_pairs={{0,128},{128,256},{256,384},{384,0},{1,129},{129,257},{257,385},{3... | collective-permute-start | bytes 1179656 | tf_op jit(solution)/shard_map/ppermute | solution.py:474
  179.1 4.1 %collective-permute-done.14.refs_6_.refs_2_ = f32[16,48,128]{2,1,0:T(8,128)S(1)} collective-permute-done((f32[16,48,128]{2,1,0:T(8,128)S(1)}, f32[16,48,128]{2,1,0:T(8,128)S(1)}, u32[]{:S(2)}, u32[]{:S(2)}) %collective-permute-start.14) | collective-permute-done | bytes 393248 | tf_op jit(solution)/shard_map/ppermute | solution.py:474
  184.2 12.6 %all-to-all-start.4 = ((bf16[16,88,128]{2,1,0:T(8,128)(2,1)}), bf16[16,88,128]{2,1,0:T(8,128)(2,1)S(1)}, u32[]{:S(2)}, u32[]{:S(2)}) async-start(bf16[16,88,128]{2,1,0:T(8,128)(2,1)} %shard_map.101), calls=%async_computation.4 | async-start | bytes 720896 | tf_op jit(solution)/shard_map/all_to_all | solution.py:470
  197.5 20.6 %shard_map.103 = f32[1,9,576]{2,1,0:T(8,128)S(1)} custom-call(f32[16,48,128]{2,1,0:T(8,128)S(1)} %shard_map.100.refs_0_, f32[16,48,128]{2,1,0:T(8,128)S(1)} %collective-permute-done.13.refs_5_.refs_1_, f32[16,48,128]{2,1,0:T(8,128)S(1)} %collective-permute-done.14.refs_6_.refs_2_, f32[16,48,128]{2,1,0:T(8,128)S(1)} %collective-permute-done.15.refs_7_.refs_3_, ...), custom_call_target="tpu_custom_call" | custom-call | flops 2831155200 | bytes 1048576 | tf_op jit(solution)/shard_map/pallas_call | solution.py:55
  (45 shorter events, 20.3 us)
Async XLA Ops:
  0.6 1.1 copy-start
  1.7 1.1 copy-start.2
  2.8 32.8 %copy-start.7 = (f32[1,9,576]{2,0,1:T(1,128)S(1)}, f32[1,9,576]{2,0,1:T(1,128)}, u32[]{:S(2)}) copy-start(f32[1,9,576]{2,0,1:T(1,128)} %param.9) | copy-start | bytes 62212
  7.2 50.2 %all-to-all-start = ((bf16[16,168,128]{2,1,0:T(8,128)(2,1)}), bf16[16,168,128]{2,1,0:T(8,128)(2,1)S(1)}, u32[]{:S(2)}, u32[]{:S(2)}) async-start(bf16[16,168,128]{2,1,0:T(8,128)(2,1)} %get-tuple-element.26), calls=%async_computation | async-start | bytes 1376256 | tf_op jit(solution)/shard_map/all_to_all | solution.py:470
  22.4 3.1 %collective-permute-start = (f32[8,128]{1,0:T(8,128)S(1)}, f32[8,128]{1,0:T(8,128)S(1)}, u32[]{:S(2)}, u32[]{:S(2)}) collective-permute-start(f32[8,128]{1,0:T(8,128)S(1)} %get-tuple-element.27), channel_id=1, source_target_pairs={{0,1},{1,0},{2,3},{3,2},{4,5},{5,4},{6,7},{7,6},{8,9},{9,8},{10,11... | collective-permute-start | bytes 12296 | tf_op jit(solution)/shard_map/ppermute | solution.py:474
  25.5 10.1 %collective-permute-start.1 = (f32[8,128]{1,0:T(8,128)S(1)}, f32[8,128]{1,0:T(8,128)S(1)}, u32[]{:S(2)}, u32[]{:S(2)}) collective-permute-start(f32[8,128]{1,0:T(8,128)S(1)} %add.3.refs_2_), channel_id=1, source_target_pairs={{0,4},{2,6},{4,0},{6,2},{1,5},{3,7},{5,1},{7,3},{8,12},{10,14},{12... | collective-permute-start | bytes 12296 | tf_op jit(solution)/shard_map/ppermute | solution.py:474
  29.7 5.9 %collective-permute-start.2 = (f32[8,128]{1,0:T(8,128)S(1)}, f32[8,128]{1,0:T(8,128)S(1)}, u32[]{:S(2)}, u32[]{:S(2)}) collective-permute-start(f32[8,128]{1,0:T(8,128)S(1)} %add.3.refs_2_), channel_id=1, source_target_pairs={{0,6},{2,0},{4,2},{6,4},{1,7},{3,1},{5,3},{7,5},{8,14},{10,8},{12,... | collective-permute-start | bytes 12296 | tf_op jit(solution)/shard_map/ppermute | solution.py:474
  32.9 5.5 %collective-permute-start.3 = (f32[8,128]{1,0:T(8,128)S(1)}, f32[8,128]{1,0:T(8,128)S(1)}, u32[]{:S(2)}, u32[]{:S(2)}) collective-permute-start(f32[8,128]{1,0:T(8,128)S(1)} %add.3.refs_2_), channel_id=1, source_target_pairs={{0,2},{2,4},{4,6},{6,0},{1,3},{3,5},{5,7},{7,1},{8,10},{10,12},{12... | collective-permute-start | bytes 12296 | tf_op jit(solution)/shard_map/ppermute | solution.py:474
  58.2 35.9 %all-to-all-start.1 = ((f32[16,48,128]{2,1,0:T(8,128)}), f32[16,48,128]{2,1,0:T(8,128)S(1)}, u32[]{:S(2)}, u32[]{:S(2)}) async-start(f32[16,48,128]{2,1,0:T(8,128)} %shard_map.95), calls=%async_computation.1 | async-start | bytes 786432 | tf_op jit(solution)/shard_map/all_to_all | solution.py:470
  66.2 50.0 %copy-start.8 = (f32[1,9,576]{2,0,1:T(1,128)S(1)}, f32[1,9,576]{2,0,1:T(1,128)}, u32[]{:S(2)}) copy-start(f32[1,9,576]{2,0,1:T(1,128)} %param.8) | copy-start | bytes 62212
  66.3 17.3 %collective-permute-start.4 = (bf16[208,1152]{1,0:T(8,128)(2,1)S(1)}, bf16[208,1152]{1,0:T(8,128)(2,1)S(1)}, u32[]{:S(2)}, u32[]{:S(2)}) collective-permute-start(bf16[208,1152]{1,0:T(8,128)(2,1)S(1)} %get-tuple-element.29), channel_id=1, source_target_pairs={{0,256},{128,384},{256,0},{384,128},{1,257},{129,385},{257,1},{385... | collective-permute-start | bytes 1437704 | tf_op jit(solution)/shard_map/ppermute | solution.py:474
  69.6 22.9 %collective-permute-start.5 = (bf16[208,1152]{1,0:T(8,128)(2,1)S(1)}, bf16[208,1152]{1,0:T(8,128)(2,1)S(1)}, u32[]{:S(2)}, u32[]{:S(2)}) collective-permute-start(bf16[208,1152]{1,0:T(8,128)(2,1)S(1)} %get-tuple-element.30), channel_id=1, source_target_pairs={{0,384},{128,0},{256,128},{384,256},{1,385},{129,1},{257,129},{385... | collective-permute-start | bytes 1437704 | tf_op jit(solution)/shard_map/ppermute | solution.py:474
  71.5 20.9 %collective-permute-start.6 = (bf16[208,1152]{1,0:T(8,128)(2,1)S(1)}, bf16[208,1152]{1,0:T(8,128)(2,1)S(1)}, u32[]{:S(2)}, u32[]{:S(2)}) collective-permute-start(bf16[208,1152]{1,0:T(8,128)(2,1)S(1)} %get-tuple-element.31), channel_id=1, source_target_pairs={{0,128},{128,256},{256,384},{384,0},{1,129},{129,257},{257,385},{3... | collective-permute-start | bytes 1437704 | tf_op jit(solution)/shard_map/ppermute | solution.py:474
  94.0 35.9 %all-to-all-start.2 = ((f32[16,48,128]{2,1,0:T(8,128)}), f32[16,48,128]{2,1,0:T(8,128)S(1)}, u32[]{:S(2)}, u32[]{:S(2)}) async-start(f32[16,48,128]{2,1,0:T(8,128)} %get-tuple-element.34), calls=%async_computation.2 | async-start | bytes 786432 | tf_op jit(solution)/shard_map/all_to_all | solution.py:470
  105.8 15.5 %collective-permute-start.7 = (f32[16,48,128]{2,1,0:T(8,128)S(1)}, f32[16,48,128]{2,1,0:T(8,128)S(1)}, u32[]{:S(2)}, u32[]{:S(2)}) collective-permute-start(f32[16,48,128]{2,1,0:T(8,128)S(1)} %all-to-all-done.1.refs_1_), channel_id=1, source_target_pairs={{0,256},{128,384},{256,0},{384,128},{1,257},{129,385},{257,1},{385... | collective-permute-start | bytes 1179656 | tf_op jit(solution)/shard_map/ppermute | solution.py:474
  109.2 19.2 %collective-permute-start.8 = (f32[16,48,128]{2,1,0:T(8,128)S(1)}, f32[16,48,128]{2,1,0:T(8,128)S(1)}, u32[]{:S(2)}, u32[]{:S(2)}) collective-permute-start(f32[16,48,128]{2,1,0:T(8,128)S(1)} %all-to-all-done.1.refs_1_), channel_id=1, source_target_pairs={{0,384},{128,0},{256,128},{384,256},{1,385},{129,1},{257,129},{385... | collective-permute-start | bytes 1179656 | tf_op jit(solution)/shard_map/ppermute | solution.py:474
  111.1 17.3 %collective-permute-start.9 = (f32[16,48,128]{2,1,0:T(8,128)S(1)}, f32[16,48,128]{2,1,0:T(8,128)S(1)}, u32[]{:S(2)}, u32[]{:S(2)}) collective-permute-start(f32[16,48,128]{2,1,0:T(8,128)S(1)} %all-to-all-done.1.refs_1_), channel_id=1, source_target_pairs={{0,128},{128,256},{256,384},{384,0},{1,129},{129,257},{257,385},{3... | collective-permute-start | bytes 1179656 | tf_op jit(solution)/shard_map/ppermute | solution.py:474
  128.8 0.9 copy-start.4
  131.5 35.6 %all-to-all-start.3 = ((f32[16,48,128]{2,1,0:T(8,128)}), f32[16,48,128]{2,1,0:T(8,128)S(1)}, u32[]{:S(2)}, u32[]{:S(2)}) async-start(f32[16,48,128]{2,1,0:T(8,128)} %get-tuple-element.41), calls=%async_computation.3 | async-start | bytes 786432 | tf_op jit(solution)/shard_map/all_to_all | solution.py:470
  143.0 14.5 %copy-start.1 = (bf16[1,9,18432]{2,1,0:T(8,128)(2,1)S(1)}, bf16[1,9,18432]{2,1,0:T(8,128)(2,1)}, u32[]{:S(2)}) copy-start(bf16[1,9,18432]{2,1,0:T(8,128)(2,1)} %refs_0_.4) | copy-start | bytes 995332
  143.0 14.5 %copy-start.3 = (bf16[1,9,18432]{2,1,0:T(8,128)(2,1)S(1)}, bf16[1,9,18432]{2,1,0:T(8,128)(2,1)}, u32[]{:S(2)}) copy-start(bf16[1,9,18432]{2,1,0:T(8,128)(2,1)} %refs_1_.4) | copy-start | bytes 995332
  143.0 1.2 copy-start.5
  144.2 1.0 copy-start.6
  147.0 11.7 %collective-permute-start.10 = (bf16[144,384]{1,0:T(8,128)(2,1)S(1)}, bf16[144,384]{1,0:T(8,128)(2,1)S(1)}, u32[]{:S(2)}, u32[]{:S(2)}) collective-permute-start(bf16[144,384]{1,0:T(8,128)(2,1)S(1)} %get-tuple-element.38), channel_id=1, source_target_pairs={{0,256},{128,384},{256,0},{384,128},{1,257},{129,385},{257,1},{385... | collective-permute-start | bytes 331784 | tf_op jit(solution)/shard_map/ppermute | solution.py:474
  150.4 8.4 %collective-permute-start.11 = (bf16[144,384]{1,0:T(8,128)(2,1)S(1)}, bf16[144,384]{1,0:T(8,128)(2,1)S(1)}, u32[]{:S(2)}, u32[]{:S(2)}) collective-permute-start(bf16[144,384]{1,0:T(8,128)(2,1)S(1)} %get-tuple-element.39), channel_id=1, source_target_pairs={{0,384},{128,0},{256,128},{384,256},{1,385},{129,1},{257,129},{385... | collective-permute-start | bytes 331784 | tf_op jit(solution)/shard_map/ppermute | solution.py:474
  152.4 7.4 %collective-permute-start.12 = (bf16[144,384]{1,0:T(8,128)(2,1)S(1)}, bf16[144,384]{1,0:T(8,128)(2,1)S(1)}, u32[]{:S(2)}, u32[]{:S(2)}) collective-permute-start(bf16[144,384]{1,0:T(8,128)(2,1)S(1)} %get-tuple-element.40), channel_id=1, source_target_pairs={{0,128},{128,256},{256,384},{384,0},{1,129},{129,257},{257,385},{3... | collective-permute-start | bytes 331784 | tf_op jit(solution)/shard_map/ppermute | solution.py:474
  167.2 11.9 %collective-permute-start.13 = (f32[16,48,128]{2,1,0:T(8,128)S(1)}, f32[16,48,128]{2,1,0:T(8,128)S(1)}, u32[]{:S(2)}, u32[]{:S(2)}) collective-permute-start(f32[16,48,128]{2,1,0:T(8,128)S(1)} %shard_map.100.refs_0_), channel_id=1, source_target_pairs={{0,256},{128,384},{256,0},{384,128},{1,257},{129,385},{257,1},{385... | collective-permute-start | bytes 1179656 | tf_op jit(solution)/shard_map/ppermute | solution.py:474
  170.4 12.7 %collective-permute-start.14 = (f32[16,48,128]{2,1,0:T(8,128)S(1)}, f32[16,48,128]{2,1,0:T(8,128)S(1)}, u32[]{:S(2)}, u32[]{:S(2)}) collective-permute-start(f32[16,48,128]{2,1,0:T(8,128)S(1)} %shard_map.100.refs_0_), channel_id=1, source_target_pairs={{0,384},{128,0},{256,128},{384,256},{1,385},{129,1},{257,129},{385... | collective-permute-start | bytes 1179656 | tf_op jit(solution)/shard_map/ppermute | solution.py:474
  172.4 10.8 %collective-permute-start.15 = (f32[16,48,128]{2,1,0:T(8,128)S(1)}, f32[16,48,128]{2,1,0:T(8,128)S(1)}, u32[]{:S(2)}, u32[]{:S(2)}) collective-permute-start(f32[16,48,128]{2,1,0:T(8,128)S(1)} %shard_map.100.refs_0_), channel_id=1, source_target_pairs={{0,128},{128,256},{256,384},{384,0},{1,129},{129,257},{257,385},{3... | collective-permute-start | bytes 1179656 | tf_op jit(solution)/shard_map/ppermute | solution.py:474
  184.2 35.4 %all-to-all-start.4 = ((bf16[16,88,128]{2,1,0:T(8,128)(2,1)}), bf16[16,88,128]{2,1,0:T(8,128)(2,1)S(1)}, u32[]{:S(2)}, u32[]{:S(2)}) async-start(bf16[16,88,128]{2,1,0:T(8,128)(2,1)} %shard_map.101), calls=%async_computation.4 | async-start | bytes 720896 | tf_op jit(solution)/shard_map/all_to_all | solution.py:470
